TPU v7x, 32 devices: a whole 2x2x4 slice. The times are simulated.
32 devices in a mesh: leaf: 2 (over x), row: 4 (over z), col: 4 (over y, core).
Axes of the slice: x: 2, y: 2, z: 4, core: 2. Of those that a mesh axis runs over, the one named last changes fastest.
Arguments:
- leaf_rhs: float32 [4, 16, 4096], P('leaf', None, 'col'), may hold values from -6 to 6
- leaf_inverse: float32 [4, 4096, 4096], P('leaf', 'row', 'col'), as said below
- update_rows: float32 [4, 2048, 4096], P('leaf', 'col', 'row'), may hold values from -0.09375 to 0.09375
- update_map: int32 [4, 16], P('leaf'), may hold values from 0 to 31, as said below
- sep_rhs: float32 [16, 4096], replicated, may hold values from -6 to 6
- sep_inverse: float32 [4096, 4096], P(('leaf', 'row', 'col')), as said below
Outputs:
- leaf_solution: float32 [4, 16, 4096], P('leaf', None, ('col', 'row'))
- sep_solution: float32 [16, 4096], P(None, ('leaf', 'row', 'col'))
Inputs may be any that keep to these rules, and one draw needn't show every extreme that they name: `update_map`: each row names 16 different separator blocks. `leaf_inverse`: entries off the diagonal are independent and of order 1 / sqrt(4096); each diagonal entry is one plus such a term. `sep_inverse`: entries off the diagonal are independent and of order 1 / sqrt(4096); each diagonal entry is one plus such a term.
All inputs are finite; a program needn't handle non-finite values.
Results may differ from a plain program's by a relative error of at most 0.000068.
Values sent between devices are 32-bit elements; how exact they have to be, the bound alone decides.
No kernel may reach another device: no remote copies, remote signals or barrier semaphores. Data moves between devices by JAX's collectives and lax.ppermute only.
A program may use at most 64 MiB of HBM per device.

v0:
```python
import jax
import jax.numpy as jnp
from jax import lax
from jax.sharding import PartitionSpec as P

BLOCK = 128


HIGH = lax.Precision.HIGHEST


def body(leaf_rhs, leaf_inverse, update_rows, update_map, sep_rhs, sep_inverse):
    subs = leaf_rhs.shape[0]
    nrhs = leaf_rhs.shape[1]
    width = sep_rhs.shape[1]
    blocks_total = width // BLOCK
    blocks_here = update_rows.shape[1] // BLOCK
    first_block = lax.axis_index("col") * blocks_here
    local_map = lax.dynamic_slice_in_dim(update_map, first_block, blocks_here, 1)
    onehot = (
        local_map[:, :, None] == jnp.arange(blocks_total, dtype=jnp.int32)[None, None, :]
    ).astype(jnp.float32)
    partial_fwd = jnp.einsum("sij,srj->sri", leaf_inverse, leaf_rhs, precision=HIGH)
    forward = lax.psum(partial_fwd, "col")
    coupled = jnp.einsum("sun,srn->sru", update_rows, forward, precision=HIGH)
    coupled = coupled.reshape(subs, nrhs, blocks_here, BLOCK)
    contrib = jnp.einsum("srkc,skb->rbc", coupled, onehot, precision=HIGH).reshape(nrhs, width)
    sep_rows = sep_inverse.shape[0]
    row_start = lax.axis_index(("leaf", "row", "col")) * sep_rows
    total = lax.psum(contrib, ("leaf", "row", "col"))
    updated = sep_rhs - total
    sep_forward = jnp.einsum("ij,rj->ri", sep_inverse, updated, precision=HIGH)
    back_terms = jnp.einsum("ij,ri->rj", sep_inverse, sep_forward, precision=HIGH)
    sep_whole = lax.psum(back_terms, ("leaf", "row", "col"))
    sep_solution = lax.dynamic_slice_in_dim(sep_whole, row_start, sep_rows, 1)
    pulled = jnp.einsum(
        "rbc,skb->srkc", sep_whole.reshape(nrhs, blocks_total, BLOCK), onehot, precision=HIGH
    )
    pulled = pulled.reshape(subs, nrhs, blocks_here * BLOCK)
    pull_terms = jnp.einsum("sun,sru->srn", update_rows, pulled, precision=HIGH)
    pull_total = lax.psum(pull_terms, "col")
    reduced = forward - pull_total
    column_terms = jnp.einsum("sij,sri->srj", leaf_inverse, reduced, precision=HIGH)
    leaf_solution = lax.psum_scatter(column_terms, "row", scatter_dimension=2, tiled=True)
    return (leaf_solution, sep_solution)


def solution(mesh):
    in_specs = (
        P("leaf", None, "col"),
        P("leaf", "row", "col"),
        P("leaf", "col", "row"),
        P("leaf", None),
        P(),
        P(("leaf", "row", "col"), None),
    )
    out_specs = (P("leaf", None, ("col", "row")), P(None, ("leaf", "row", "col")))
    return jax.shard_map(body, mesh=mesh, in_specs=in_specs, out_specs=out_specs, check_vma=False)
```

profile of v0, /device:TPU:0, one launch (start us, length us, event | category | flops | bytes accessed | tf_op | source)
XLA Modules:
  0.0 386.2 jit_solution(15580366361775697781)
XLA Ops:
  7.2 0.0 copy-start
  7.2 0.0 copy-start.3
  7.2 0.0 all-reduce.5.cloned.1.call-start
  7.2 11.1 %fusion.10 = f32[2,16,1024]{2,1,0:T(8,128)} fusion(f32[2,16,1024]{2,1,0:T(8,128)} %param.6, f32[2,1024,1024]{2,1,0:T(8,128)} %param.7), kind=kOutput, calls=%fused_computation.13 | convolution fusion | flops 402653184 | bytes 8650752 | tf_op jit(solution)/shard_map/sij,srj->sri/dot_general | solution.py:23
  18.3 0.0 copy-start.2
  18.3 0.0 all-reduce.5.cloned.1.call-update
  18.3 0.0 all-reduce.7.cloned.1.call-start
  18.4 0.0 copy-done.3
  18.4 0.1 constant_dynamic-slice_fusion.1
  18.5 34.1 %all-reduce.5.cloned.1.call-done = f32[2,16,1024]{2,1,0:T(8,128)} async-done(((f32[2,16,1024]{2,1,0:T(8,128)}), f32[2,16,1024]{2,1,0:T(8,128)}) %all-reduce.5.cloned.1.call-update) | async-done | bytes 131088 | tf_op jit(solution)/shard_map/psum | solution.py:24
  52.6 5.7 %fusion.11 = f32[2,16,512]{2,1,0:T(8,128)S(1)} fusion(f32[2,16,1024]{2,1,0:T(8,128)} %all-reduce.5.cloned.1.call-done, f32[2,512,1024]{2,1,0:T(8,128)} %param.8), kind=kOutput, calls=%fused_computation.14 | convolution fusion | flops 201326592 | bytes 4390912 | tf_op jit(solution)/shard_map/sun,srn->sru/dot_general | solution.py:25
  58.4 0.4 fusion.5
  58.8 0.9 copy.14
  59.6 0.0 all-reduce.7.cloned.1.call-update
  59.7 0.2 all-reduce.9.cloned.1.call-start
  59.9 124.9 %all-reduce.7.cloned.1.call-done = f32[16,4096]{1,0:T(8,128)} async-done(((f32[16,4096]{1,0:T(8,128)}), f32[16,4096]{1,0:T(8,128)}) %all-reduce.7.cloned.1.call-update) | async-done | bytes 262160 | tf_op jit(solution)/shard_map/psum | solution.py:30
  184.8 0.0 copy-done
  184.8 0.0 copy-done.2
  184.8 2.7 fusion
  187.5 0.0 copy-start.1
  187.5 1.8 fusion.12
  189.3 0.0 all-reduce.9.cloned.1.call-update
  189.3 0.0 all-reduce.11.cloned.1.call-start
  189.4 125.9 %all-reduce.9.cloned.1.call-done = f32[16,4096]{1,0:T(8,128)} async-done(((f32[16,4096]{1,0:T(8,128)}), f32[16,4096]{1,0:T(8,128)}) %all-reduce.9.cloned.1.call-update) | async-done | bytes 262160 | tf_op jit(solution)/shard_map/psum | solution.py:34
  315.3 1.0 copy.12
  316.3 0.3 convolution_bitcast_fusion
  316.6 4.9 %fusion.13 = f32[2,16,1024]{2,1,0:T(8,128)} fusion(f32[2,16,512]{2,1,0:T(8,128)S(1)} %reshape.20, f32[2,512,1024]{2,1,0:T(8,128)} %param.8), kind=kOutput, calls=%fused_computation.16 | convolution fusion | flops 201326592 | bytes 4390912 | tf_op jit(solution)/shard_map/sun,sru->srn/dot_general | solution.py:40
  321.5 0.0 all-reduce.11.cloned.1.call-update
  321.6 0.0 reduce-scatter.2.cloned.1.call-start
  321.6 30.5 %all-reduce.11.cloned.1.call-done = f32[2,16,1024]{2,1,0:T(8,128)} async-done(((f32[2,16,1024]{2,1,0:T(8,128)}), f32[2,16,1024]{2,1,0:T(8,128)}) %all-reduce.11.cloned.1.call-update) | async-done | bytes 131088 | tf_op jit(solution)/shard_map/psum | solution.py:41
  352.1 0.0 copy-done.1
  352.1 8.2 %fusion.2 = f32[2,16,1024]{2,1,0:T(8,128)} fusion(f32[2,1024,1024]{2,1,0:T(8,128)} %param.7, f32[2,16,1024]{2,1,0:T(8,128)S(1)} %copy-done.1, f32[2,16,1024]{2,1,0:T(8,128)} %all-reduce.11.cloned.1.call-done), kind=kOutput, calls=%fused_computation.4 | convolution fusion | flops 402685952 | bytes 8781824 | tf_op jit(solution)/shard_map/sij,sri->srj/dot_general | solution.py:43
  360.3 0.0 reduce-scatter.2.cloned.1.call-update
  360.3 1.3 constant_dynamic-slice_fusion
  361.6 18.0 %reduce-scatter.2.cloned.1.call-done = f32[2,16,256]{2,1,0:T(8,128)} async-done(((f32[2,16,1024]{2,1,0:T(8,128)}), f32[2,16,256]{2,1,0:T(8,128)}) %reduce-scatter.2.cloned.1.call-update) | async-done | bytes 32784 | tf_op jit(solution)/shard_map/reduce_scatter | solution.py:44
  (2 shorter events, 0.1 us)
Async XLA Ops:
  7.2 177.6 %copy-start = (f32[128,4096]{1,0:T(8,128)S(1)}, f32[128,4096]{1,0:T(8,128)}, u32[]{:S(2)}) copy-start(f32[128,4096]{1,0:T(8,128)} %param.11) | copy-start | bytes 6291460
  7.2 11.2 %copy-start.3 = (s32[2,16]{1,0:T(2,128)S(1)}, s32[2,16]{1,0:T(2,128)}, u32[]{:S(2)}) copy-start(s32[2,16]{1,0:T(2,128)} %param.9) | copy-start | bytes 388
  7.2 45.4 %all-reduce.5.cloned.1.call-start = ((), (), s32[]{:S(2)}) async-start(), calls=%async_computation.1 | async-start | bytes 262144 | tf_op jit(solution)/shard_map/psum | solution.py:24
  18.3 166.5 %copy-start.2 = (f32[16,4096]{1,0:T(8,128)S(1)}, f32[16,4096]{1,0:T(8,128)}, u32[]{:S(2)}) copy-start(f32[16,4096]{1,0:T(8,128)} %param.10) | copy-start | bytes 786436
  18.3 166.5 %all-reduce.7.cloned.1.call-start = ((), (), s32[]{:S(2)}) async-start(), calls=%async_computation.2 | async-start | bytes 524288 | tf_op jit(solution)/shard_map/psum | solution.py:30
  59.7 255.6 %all-reduce.9.cloned.1.call-start = ((), (), s32[]{:S(2)}) async-start(), calls=%async_computation.3 | async-start | bytes 524288 | tf_op jit(solution)/shard_map/psum | solution.py:34
  187.5 164.6 %copy-start.1 = (f32[2,16,1024]{2,1,0:T(8,128)S(1)}, f32[2,16,1024]{2,1,0:T(8,128)}, u32[]{:S(2)}) copy-start(f32[2,16,1024]{2,1,0:T(8,128)} %all-reduce.5.cloned.1.call-done) | copy-start | bytes 393220
  189.3 162.8 %all-reduce.11.cloned.1.call-start = ((), (), s32[]{:S(2)}) async-start(), calls=%async_computation.4 | async-start | bytes 262144 | tf_op jit(solution)/shard_map/psum | solution.py:41
  321.6 58.1 %reduce-scatter.2.cloned.1.call-start = ((), (), s32[]{:S(2)}) async-start(), calls=%async_computation.5 | async-start | bytes 163840 | tf_op jit(solution)/shard_map/reduce_scatter | solution.py:44
Sparse Core Ops, SparseCore 0:
  18.5 34.0 all-reduce.4
  59.8 124.9 all-reduce.6
  191.2 124.0 all-reduce.8
  321.7 30.3 all-reduce.10
  360.4 19.1 reduce-scatter.1
where the time goes:
time: 386 us
  waiting for transfers between devices  334 us (87%)
  matrix products  35.1 us (9%)
  between operations  13.9 us (4%)
    psum x1, waiting for transfers between devices, body(): sep_whole = lax.psum(back_terms, ('leaf', 'row', 'col'))  126 us
    psum x1, waiting for transfers between devices, body(): total = lax.psum(contrib, ('leaf', 'row', 'col'))  125 us
    psum x1, waiting for transfers between devices, body(): forward = lax.psum(partial_fwd, 'col')  34.1 us
    psum x1, waiting for transfers between devices, body(): pull_total = lax.psum(pull_terms, 'col')  30.5 us
    reduce_scatter x1, waiting for transfers between devices, body(): lax.psum_scatter(column_terms, 'row', scatter_dimension=2, tiled=True)  18 us
    dot_general x1, matrix products, body(): jnp.einsum('sij,srj->sri', leaf_inverse, leaf_rhs, precision=HIGH)  11.1 us
    dot_general x1, matrix products, body(): jnp.einsum('sij,sri->srj', leaf_inverse, reduced, precision=HIGH)  8.18 us
  transfers between devices with their start and end apart: 5, of which 5 were waited for; matrix products, arithmetic and copies ran while one was open for 0% of the time, Pallas kernels for 0%

commit v1 on v0

v1 whole, which is shorter than its diff:
```python
import functools

import jax
import jax.numpy as jnp
from jax import lax
from jax.sharding import PartitionSpec as P

BLOCK = 128
CORES = 2

HIGH = lax.Precision.HIGHEST


def swap(value, axes, size, mask):
    return lax.ppermute(value, axes, [(i, i ^ mask) for i in range(size)])


def picked(value, dim, index, count):
    return jnp.stack(
        [lax.dynamic_index_in_dim(value, index ^ m, dim, keepdims=False) for m in range(count)], dim
    )


def halves(value, core):
    half = value.shape[0] // CORES
    mine = lax.dynamic_slice_in_dim(value, core * half, half, 0)
    other = lax.dynamic_slice_in_dim(value, (1 - core) * half, half, 0)
    return mine, other


def sum_over_col(terms, cols, core):
    mine, other = halves(terms, core)
    mine = mine + swap(other, "col", cols, 1)
    step = CORES
    while step < cols:
        mine = mine + swap(mine, "col", cols, step)
        step *= 2
    other = swap(mine, "col", cols, 1)
    return jnp.where(
        core == 0, jnp.concatenate([mine, other]), jnp.concatenate([other, mine])
    )


def body(sizes, leaf_rhs, leaf_inverse, update_rows, update_map, sep_rhs, sep_inverse):
    leaves, rows, cols = sizes
    chips = leaves * cols // CORES
    subs, nrhs, _ = leaf_rhs.shape
    width = sep_rhs.shape[1]
    blocks_total = width // BLOCK
    blocks_here = update_rows.shape[1] // BLOCK
    sep_rows = sep_inverse.shape[0]
    leaf, row, col = (lax.axis_index(a) for a in ("leaf", "row", "col"))
    core = col % CORES
    plane = leaf * (cols // CORES) + col // CORES

    maps = lax.all_gather(update_map, "leaf")
    maps = maps.reshape(leaves, subs, cols // CORES, CORES, blocks_here)
    maps = maps.transpose(0, 2, 3, 1, 4).reshape(chips, CORES, subs, blocks_here)
    onehot = (maps[..., None] == jnp.arange(blocks_total, dtype=jnp.int32)).astype(jnp.float32)

    partial_fwd = jnp.einsum("sij,srj->sri", leaf_inverse, leaf_rhs, precision=HIGH)
    forward = sum_over_col(partial_fwd, cols, core)
    coupled = jnp.einsum("sun,srn->sru", update_rows, forward, precision=HIGH)
    coupled = coupled + sum(swap(coupled, "row", rows, k) for k in range(1, rows))
    plane_axes, plane_size = ("leaf", "col"), leaves * cols
    pieces = jnp.stack(
        [coupled] + [swap(coupled, plane_axes, plane_size, CORES * m) for m in range(1, chips)]
    )
    others = swap(pieces, "col", cols, 1)
    pieces = jnp.stack([pieces, others], 1).reshape(
        chips, CORES, subs, nrhs, blocks_here, BLOCK
    )
    spread = picked(picked(onehot, 0, plane, chips), 1, core, CORES)
    contrib = jnp.einsum("pqsrkc,pqskb->rbc", pieces, spread, precision=HIGH)
    updated = sep_rhs - contrib.reshape(nrhs, width)

    sep_forward = jnp.einsum("ij,rj->ri", sep_inverse, updated, precision=HIGH)
    back_terms = jnp.einsum("ij,ri->rj", sep_inverse, sep_forward, precision=HIGH)
    pulls = jnp.einsum(
        "rbc,pqskb->qpsrkc",
        back_terms.reshape(nrhs, blocks_total, BLOCK),
        spread,
        precision=HIGH,
    ).reshape(CORES, chips, subs, nrhs, blocks_here * BLOCK)
    own = back_terms.reshape(nrhs, leaves, rows, cols // CORES, CORES, sep_rows)
    own = own.transpose(4, 1, 3, 0, 2, 5).reshape(CORES, chips, nrhs, rows, sep_rows)
    own = picked(picked(own, 0, core, CORES), 1, plane, chips)
    pulls = pulls[0] + swap(pulls[1], "col", cols, 1)
    own = own[0] + swap(own[1], "col", cols, 1)
    pulled = pulls[0] + sum(
        swap(pulls[m], plane_axes, plane_size, CORES * m) for m in range(1, chips)
    )
    own = own[0] + sum(swap(own[m], plane_axes, plane_size, CORES * m) for m in range(1, chips))
    pulled = pulled + sum(swap(pulled, "row", rows, k) for k in range(1, rows))
    own = picked(own, 1, row, rows)
    sep_solution = own[:, 0] + sum(swap(own[:, k], "row", rows, k) for k in range(1, rows))

    pull_terms = jnp.einsum("sun,sru->srn", update_rows, pulled, precision=HIGH)
    reduced = forward - sum_over_col(pull_terms, cols, core)
    terms = jnp.einsum("sij,sri->srj", leaf_inverse, reduced, precision=HIGH)
    terms = picked(terms.reshape(subs, nrhs, rows, -1), 2, row, rows)
    leaf_solution = terms[:, :, 0] + sum(
        swap(terms[:, :, k], "row", rows, k) for k in range(1, rows)
    )
    return (leaf_solution, sep_solution)


def solution(mesh):
    sizes = tuple(mesh.shape[a] for a in ("leaf", "row", "col"))
    in_specs = (
        P("leaf", None, "col"),
        P("leaf", "row", "col"),
        P("leaf", "col", "row"),
        P("leaf", None),
        P(),
        P(("leaf", "row", "col"), None),
    )
    out_specs = (P("leaf", None, ("col", "row")), P(None, ("leaf", "row", "col")))
    return jax.shard_map(
        functools.partial(body, sizes), mesh=mesh, in_specs=in_specs, out_specs=out_specs, check_vma=False
    )
```

time: 386 us -> 104 us (0.27)
  waiting for transfers between devices: 334 us -> 30.2 us
  starting transfers between devices: 0.39 us -> 33.5 us
  between operations: 13.9 us -> 1.15 us
  matrix products: 35.1 us -> 30.6 us
  blocking collectives: 0 us -> 4.43 us
    psum x4 -> x0, waiting for transfers between devices: 315 us -> none  [the longest x1 126 us: body(): sep_whole = lax.psum(back_terms, ('leaf', 'row', 'col'))]
    ppermute x0 -> x30, starting transfers between devices: none -> 33.5 us  [swap(): return lax.ppermute(value, axes, [(i, i ^ mask) for i in range(size)])]
    ppermute x0 -> x30, waiting for transfers between devices: none -> 30.2 us  [swap(): return lax.ppermute(value, axes, [(i, i ^ mask) for i in range(size)])]
    reduce_scatter x1 -> x0, waiting for transfers between devices: 18 us -> none  [body(): lax.psum_scatter(column_terms, 'row', scatter_dimension=2, tiled=True)]
    all_gather x0 -> x1, blocking collectives: none -> 4.43 us  [body(): maps = lax.all_gather(update_map, 'leaf')]
  transfers between devices with their start and end apart: 5 -> 30, of which waited for: 5 -> 19; matrix products, arithmetic and copies ran while one was open for 0% -> 8% of each run, Pallas kernels for 0% -> 0%
where the time goes in v1:
time: 104 us
  starting transfers between devices  33.5 us (32%)
  matrix products  30.6 us (29%)
  waiting for transfers between devices  30.2 us (29%)
  blocking collectives  4.43 us (4%)
  local copies, waits for them, and re-layouts  2.59 us (2%)
  other arithmetic  1.57 us (2%)
  between operations  1.15 us (1%)
    ppermute x30, starting transfers between devices, swap(): return lax.ppermute(value, axes, [(i, i ^ mask) for i in range(size)])  33.5 us
    ppermute x30, waiting for transfers between devices, swap(): return lax.ppermute(value, axes, [(i, i ^ mask) for i in range(size)])  30.2 us
    dot_general x1, matrix products, body(): jnp.einsum('sij,srj->sri', leaf_inverse, leaf_rhs, precision=HIGH)  9.4 us
    dot_general x1, matrix products, body(): terms = jnp.einsum('sij,sri->srj', leaf_inverse, reduced, precision=HIGH)  6.41 us
    dot_general x1, matrix products, body(): coupled = jnp.einsum('sun,srn->sru', update_rows, forward, precision=HIGH)  5.67 us
    dot_general x1, matrix products, body(): pull_terms = jnp.einsum('sun,sru->srn', update_rows, pulled, precision=HIGH)  4.5 us
    all_gather x1, blocking collectives, body(): maps = lax.all_gather(update_map, 'leaf')  4.43 us
  transfers between devices with their start and end apart: 30, of which 19 were waited for; matrix products, arithmetic and copies ran while one was open for 8% of the time, Pallas kernels for 0%

profile of v1, /device:TPU:0, one launch (start us, length us, event | category | flops | bytes accessed | tf_op | source)
XLA Modules:
  0.0 104.0 jit_solution(2651352460755438539)
XLA Ops:
  0.7 9.4 %fusion.43 = f32[2,16,1024]{2,1,0:T(8,128)S(1)} fusion(f32[2,16,1024]{2,1,0:T(8,128)} %param.6, f32[2,1024,1024]{2,1,0:T(8,128)} %param.7), kind=kOutput, calls=%fused_computation.94 | convolution fusion | flops 402653184 | bytes 8650752 | tf_op jit(solution)/shard_map/sij,srj->sri/dot_general | solution.py:61
  10.6 0.9 collective-permute-done
  11.5 2.9 %collective-permute-start.1 = (f32[1,16,1024]{2,1,0:T(8,128)S(1)}, f32[1,16,1024]{2,1,0:T(8,128)S(1)}, u32[]{:S(2)}, u32[]{:S(2)}) collective-permute-start(f32[1,16,1024]{2,1,0:T(8,128)S(1)} %dynamic-slice_add_fusion.1), channel_id=1, source_target_pairs={{0,2},{1,3},{2,0},{3,1},{4,6},{5,7},{6,4},{7,5},{8,10},{9,11},{10,... | collective-permute-start | bytes 196616 | tf_op jit(solution)/shard_map/ppermute | solution.py:15
  14.5 2.4 %collective-permute-done.1 = f32[1,16,1024]{2,1,0:T(8,128)S(1)} collective-permute-done((f32[1,16,1024]{2,1,0:T(8,128)S(1)}, f32[1,16,1024]{2,1,0:T(8,128)S(1)}, u32[]{:S(2)}, u32[]{:S(2)}) %collective-permute-start.1) | collective-permute-done | bytes 65568 | tf_op jit(solution)/shard_map/ppermute | solution.py:15
  17.0 4.4 %all-gather.1 = s32[2,2,16]{2,1,0:T(2,128)S(1)} all-gather(s32[1,2,16]{2,1,0:T(2,128)S(1)} %bitcast.107), channel_id=2, replica_groups=mesh['leaf'=2,'row'=4,'col'=4] {'leaf'}, dimensions={0}, use_global_device_ids=true | all-gather | bytes 384 | tf_op jit(solution)/shard_map/all_gather | solution.py:56
  21.6 5.7 %fusion.22 = f32[2,16,512]{2,1,0:T(8,128)S(1)} fusion(f32[2,512,1024]{2,1,0:T(8,128)} %param.8, f32[1,16,1024]{2,1,0:T(8,128)S(1)} %collective-permute-done.2, f32[1,16,1024]{2,1,0:T(8,128)S(1)} %add.137, pred[]{:T(512)S(6)} %eq.21), kind=kOutput, calls=%fused_computation.37 | convolution fusion | flops 201424896 | bytes 4390913 | tf_op jit(solution)/shard_map/sun,srn->sru/dot_general | solution.py:63
  27.3 1.9 %collective-permute-start.3 = (f32[2,16,512]{2,1,0:T(8,128)S(1)}, f32[2,16,512]{2,1,0:T(8,128)S(1)}, u32[]{:S(2)}, u32[]{:S(2)}) collective-permute-start(f32[2,16,512]{2,1,0:T(8,128)S(1)} %fusion.22), channel_id=1, source_target_pairs={{0,4},{4,0},{8,12},{12,8},{1,5},{5,1},{9,13},{13,9},{2,6},{6,2},{1... | collective-permute-start | bytes 196616 | tf_op jit(solution)/shard_map/ppermute | solution.py:15
  29.2 2.6 %collective-permute-start.4 = (f32[2,16,512]{2,1,0:T(8,128)S(1)}, f32[2,16,512]{2,1,0:T(8,128)S(1)}, u32[]{:S(2)}, u32[]{:S(2)}) collective-permute-start(f32[2,16,512]{2,1,0:T(8,128)S(1)} %fusion.22), channel_id=1, source_target_pairs={{0,8},{4,12},{8,0},{12,4},{1,9},{5,13},{9,1},{13,5},{2,10},{6,14},... | collective-permute-start | bytes 196616 | tf_op jit(solution)/shard_map/ppermute | solution.py:15
  32.0 4.0 %collective-permute-done.4 = f32[2,16,512]{2,1,0:T(8,128)S(1)} collective-permute-done((f32[2,16,512]{2,1,0:T(8,128)S(1)}, f32[2,16,512]{2,1,0:T(8,128)S(1)}, u32[]{:S(2)}, u32[]{:S(2)}) %collective-permute-start.4) | collective-permute-done | bytes 65568 | tf_op jit(solution)/shard_map/ppermute | solution.py:15
  36.0 1.9 %collective-permute-done.5 = f32[2,16,512]{2,1,0:T(8,128)S(1)} collective-permute-done((f32[2,16,512]{2,1,0:T(8,128)S(1)}, f32[2,16,512]{2,1,0:T(8,128)S(1)}, u32[]{:S(2)}, u32[]{:S(2)}) %collective-permute-start.5) | collective-permute-done | bytes 65568 | tf_op jit(solution)/shard_map/ppermute | solution.py:15
  37.9 1.6 %collective-permute-start.6 = (f32[2,16,512]{2,1,0:T(8,128)S(1)}, f32[2,16,512]{2,1,0:T(8,128)S(1)}, u32[]{:S(2)}, u32[]{:S(2)}) collective-permute-start(f32[2,16,512]{2,1,0:T(8,128)S(1)} %add_add_fusion), channel_id=1, source_target_pairs={{0,2},{1,3},{2,0},{3,1},{16,18},{17,19},{18,16},{19,17},{4,6},{5,7... | collective-permute-start | bytes 196616 | tf_op jit(solution)/shard_map/ppermute | solution.py:15
  39.5 1.5 %collective-permute-start.7 = (f32[2,16,512]{2,1,0:T(8,128)S(1)}, f32[2,16,512]{2,1,0:T(8,128)S(1)}, u32[]{:S(2)}, u32[]{:S(2)}) collective-permute-start(f32[2,16,512]{2,1,0:T(8,128)S(1)} %add_add_fusion), channel_id=1, source_target_pairs={{0,16},{1,17},{2,18},{3,19},{16,0},{17,1},{18,2},{19,3},{4,20},{5,... | collective-permute-start | bytes 196616 | tf_op jit(solution)/shard_map/ppermute | solution.py:15
  41.5 1.4 %collective-permute-done.6 = f32[2,16,512]{2,1,0:T(8,128)S(1)} collective-permute-done((f32[2,16,512]{2,1,0:T(8,128)S(1)}, f32[2,16,512]{2,1,0:T(8,128)S(1)}, u32[]{:S(2)}, u32[]{:S(2)}) %collective-permute-start.6) | collective-permute-done | bytes 65568 | tf_op jit(solution)/shard_map/ppermute | solution.py:15
  42.9 0.8 collective-permute-done.7
  43.8 2.4 %collective-permute-done.8 = f32[2,16,512]{2,1,0:T(8,128)S(1)} collective-permute-done((f32[2,16,512]{2,1,0:T(8,128)S(1)}, f32[2,16,512]{2,1,0:T(8,128)S(1)}, u32[]{:S(2)}, u32[]{:S(2)}) %collective-permute-start.8) | collective-permute-done | bytes 65568 | tf_op jit(solution)/shard_map/ppermute | solution.py:15
  46.8 1.0 collective-permute-done.9
  48.1 1.1 %fusion = f32[32,16,128,1,1,1]{2,0,5,1,4,3:T(8,128)S(1)} fusion(f32[4,1,2,16,4,128]{5,0,2,3,1,4:T(4,128)S(1)} %copy.31, f32[1,1,2,16,4,128]{5,0,2,3,1,4:T(1,128)S(1)} %copy.30, f32[1,1,2,16,4,128]{5,0,2,3,1,4:T(1,128)S(1)} %copy.29, f32[1,1,2,16,4,128]{5,0,2,3,1,4:T(1,128)S(1)} %copy.28, f32[1,1,2,16,4,128]{5,0,2,3,1,4:T(1,128)S(1)} %copy.27, ...), kind=kOutput, calls=%fused_computation.1 | convolution fusion | flops 50857984 | bytes 794624 | tf_op jit(solution)/shard_map/pqsrkc,pqskb->rbc/dot_general | solution.py:74
  49.2 1.7 %fusion.10 = f32[16,128]{1,0:T(8,128)S(1)} fusion(f32[128,4096]{1,0:T(8,128)S(1)} %copy-done, f32[16,4096]{1,0:T(8,128)S(1)} %copy-done.1, f32[2,8,32,128]{3,2,1,0:T(8,128)S(1)} %bitcast.98), kind=kOutput, calls=%fused_computation.20 | convolution fusion | flops 100728832 | bytes 2629632 | tf_op jit(solution)/shard_map/ij,rj->ri/dot_general | solution.py:77
  50.9 1.1 %fusion.44 = f32[16,4096]{1,0:T(8,128)S(1)} fusion(f32[16,128]{1,0:T(8,128)S(1)} %fusion.10, f32[128,4096]{1,0:T(8,128)S(1)} %copy-done), kind=kOutput, calls=%fused_computation.95 | convolution fusion | flops 100663296 | bytes 2367488 | tf_op jit(solution)/shard_map/ij,ri->rj/dot_general | solution.py:78
  52.5 0.7 convolution_bitcast_fusion
  53.2 0.8 squeeze.79
  54.4 1.4 %collective-permute-done.10 = f32[4,2,16,512]{3,2,1,0:T(8,128)S(1)} collective-permute-done((f32[4,2,16,512]{3,2,1,0:T(8,128)}, f32[4,2,16,512]{3,2,1,0:T(8,128)S(1)}, u32[]{:S(2)}, u32[]{:S(2)}) %collective-permute-start.10) | collective-permute-done | bytes 262176 | tf_op jit(solution)/shard_map/ppermute | solution.py:15
  55.8 0.6 collective-permute-start.11
  56.4 0.8 collective-permute-start.12
  57.2 2.2 %collective-permute-start.13 = (f32[2,16,512]{2,1,0:T(8,128)S(1)}, f32[2,16,512]{2,1,0:T(8,128)S(1)}, u32[]{:S(2)}, u32[]{:S(2)}) collective-permute-start(f32[2,16,512]{2,1,0:T(8,128)S(1)} %get-tuple-element.11), channel_id=1, source_target_pairs={{0,18},{1,19},{2,16},{3,17},{16,2},{17,3},{18,0},{19,1},{4,22},{5,... | collective-permute-start | bytes 196616 | tf_op jit(solution)/shard_map/ppermute | solution.py:15
  59.5 0.7 collective-permute-done.11
  60.2 1.1 %collective-permute-done.12 = f32[2,16,512]{2,1,0:T(8,128)S(1)} collective-permute-done((f32[2,16,512]{2,1,0:T(8,128)S(1)}, f32[2,16,512]{2,1,0:T(8,128)S(1)}, u32[]{:S(2)}, u32[]{:S(2)}) %collective-permute-start.12) | collective-permute-done | bytes 65568 | tf_op jit(solution)/shard_map/ppermute | solution.py:15
  61.3 1.4 %collective-permute-done.13 = f32[2,16,512]{2,1,0:T(8,128)S(1)} collective-permute-done((f32[2,16,512]{2,1,0:T(8,128)S(1)}, f32[2,16,512]{2,1,0:T(8,128)S(1)}, u32[]{:S(2)}, u32[]{:S(2)}) %collective-permute-start.13) | collective-permute-done | bytes 65568 | tf_op jit(solution)/shard_map/ppermute | solution.py:15
  62.7 1.8 %collective-permute-start.15 = (f32[2,16,512]{2,1,0:T(8,128)S(1)}, f32[2,16,512]{2,1,0:T(8,128)S(1)}, u32[]{:S(2)}, u32[]{:S(2)}) collective-permute-start(f32[2,16,512]{2,1,0:T(8,128)S(1)} %fusion.27), channel_id=1, source_target_pairs={{0,8},{4,12},{8,0},{12,4},{1,9},{5,13},{9,1},{13,5},{2,10},{6,14},... | collective-permute-start | bytes 196616 | tf_op jit(solution)/shard_map/ppermute | solution.py:15
  64.6 2.5 %collective-permute-start.16 = (f32[2,16,512]{2,1,0:T(8,128)S(1)}, f32[2,16,512]{2,1,0:T(8,128)S(1)}, u32[]{:S(2)}, u32[]{:S(2)}) collective-permute-start(f32[2,16,512]{2,1,0:T(8,128)S(1)} %fusion.27), channel_id=1, source_target_pairs={{0,12},{4,8},{8,4},{12,0},{1,13},{5,9},{9,5},{13,1},{2,14},{6,10},... | collective-permute-start | bytes 196616 | tf_op jit(solution)/shard_map/ppermute | solution.py:15
  67.1 2.3 %collective-permute-done.15 = f32[2,16,512]{2,1,0:T(8,128)S(1)} collective-permute-done((f32[2,16,512]{2,1,0:T(8,128)S(1)}, f32[2,16,512]{2,1,0:T(8,128)S(1)}, u32[]{:S(2)}, u32[]{:S(2)}) %collective-permute-start.15) | collective-permute-done | bytes 65568 | tf_op jit(solution)/shard_map/ppermute | solution.py:15
  69.5 1.2 %collective-permute-done.16 = f32[2,16,512]{2,1,0:T(8,128)S(1)} collective-permute-done((f32[2,16,512]{2,1,0:T(8,128)S(1)}, f32[2,16,512]{2,1,0:T(8,128)S(1)}, u32[]{:S(2)}, u32[]{:S(2)}) %collective-permute-start.16) | collective-permute-done | bytes 65568 | tf_op jit(solution)/shard_map/ppermute | solution.py:15
  70.7 4.5 %fusion.28 = f32[2,16,1024]{2,1,0:T(8,128)S(1)} fusion(f32[2,512,1024]{2,1,0:T(8,128)} %param.8, f32[2,16,512]{2,1,0:T(8,128)S(1)} %fusion.27, f32[2,16,512]{2,1,0:T(8,128)S(1)} %collective-permute-done.16, f32[2,16,512]{2,1,0:T(8,128)S(1)} %collective-permute-done.14, f32[2,16,512]{2,1,0:T(8,128)S(1)} %collective-permute-done.15), kind=kOutput, calls=%fused_computation.48 | convolution fusion | flops 201375744 | bytes 4587520 | tf_op jit(solution)/shard_map/sun,sru->srn/dot_general | solution.py:98
  75.3 1.1 %collective-permute-start.24 = (f32[16,4,128]{2,0,1:T(8,128)S(1)}, f32[16,4,128]{2,0,1:T(8,128)S(1)}, u32[]{:S(2)}, u32[]{:S(2)}) collective-permute-start(f32[16,4,128]{2,0,1:T(8,128)S(1)} %get-tuple-element.15), channel_id=1, source_target_pairs={{0,2},{1,3},{2,0},{3,1},{16,18},{17,19},{18,16},{19,17},{4,6},{5,7... | collective-permute-start | bytes 98312 | tf_op jit(solution)/shard_map/ppermute | solution.py:15
  76.4 1.5 %collective-permute-start.25 = (f32[16,4,128]{2,0,1:T(8,128)S(1)}, f32[16,4,128]{2,0,1:T(8,128)S(1)}, u32[]{:S(2)}, u32[]{:S(2)}) collective-permute-start(f32[16,4,128]{2,0,1:T(8,128)S(1)} %get-tuple-element.13), channel_id=1, source_target_pairs={{0,16},{1,17},{2,18},{3,19},{16,0},{17,1},{18,2},{19,3},{4,20},{5,... | collective-permute-start | bytes 98312 | tf_op jit(solution)/shard_map/ppermute | solution.py:15
  77.9 1.0 collective-permute-start.26
  78.9 1.1 %collective-permute-start.18 = (f32[1,16,1024]{2,1,0:T(8,128)S(1)}, f32[1,16,1024]{2,1,0:T(8,128)S(1)}, u32[]{:S(2)}, u32[]{:S(2)}) collective-permute-start(f32[1,16,1024]{2,1,0:T(8,128)S(1)} %dynamic-slice_add_fusion), channel_id=1, source_target_pairs={{0,2},{1,3},{2,0},{3,1},{4,6},{5,7},{6,4},{7,5},{8,10},{9,11},{10,... | collective-permute-start | bytes 196616 | tf_op jit(solution)/shard_map/ppermute | solution.py:15
  80.3 2.4 %collective-permute-done.26 = f32[16,4,128]{2,0,1:T(8,128)S(1)} collective-permute-done((f32[16,4,128]{2,0,1:T(8,128)S(1)}, f32[16,4,128]{2,0,1:T(8,128)S(1)}, u32[]{:S(2)}, u32[]{:S(2)}) %collective-permute-start.26) | collective-permute-done | bytes 32800 | tf_op jit(solution)/shard_map/ppermute | solution.py:15
  82.7 0.7 collective-permute-done.18
  83.5 0.7 collective-permute-start.27
  84.2 2.4 %collective-permute-start.28 = (f32[16,128]{1,0:T(8,128)S(1)}, f32[16,128]{1,0:T(8,128)S(1)}, u32[]{:S(2)}, u32[]{:S(2)}) collective-permute-start(f32[16,128]{1,0:T(8,128)S(1)} %get-tuple-element.20), channel_id=1, source_target_pairs={{0,8},{4,12},{8,0},{12,4},{1,9},{5,13},{9,1},{13,5},{2,10},{6,14},... | collective-permute-start | bytes 24584 | tf_op jit(solution)/shard_map/ppermute | solution.py:15
  86.6 1.4 %collective-permute-start.29 = (f32[16,128]{1,0:T(8,128)S(1)}, f32[16,128]{1,0:T(8,128)S(1)}, u32[]{:S(2)}, u32[]{:S(2)}) collective-permute-start(f32[16,128]{1,0:T(8,128)S(1)} %get-tuple-element.21), channel_id=1, source_target_pairs={{0,12},{4,8},{8,4},{12,0},{1,13},{5,9},{9,5},{13,1},{2,14},{6,10},... | collective-permute-start | bytes 24584 | tf_op jit(solution)/shard_map/ppermute | solution.py:15
  88.0 6.4 %fusion.15 = f32[2,16,1024]{2,1,0:T(8,128)S(1)} fusion(f32[2,1024,1024]{2,1,0:T(8,128)} %param.7, f32[1,16,1024]{2,1,0:T(8,128)S(1)} %collective-permute-done.19, f32[1,16,1024]{2,1,0:T(8,128)S(1)} %add.155, f32[1,16,1024]{2,1,0:T(8,128)S(1)} %collective-permute-done.2, f32[1,16,1024]{2,1,0:T(8,128)S(1)} %add.137, pred[]{:T(512)S(6)} %eq.21), kind=kOutput, calls=%fused_computation.31 | convolution fusion | flops 402882560 | bytes 8781825 | tf_op jit(solution)/shard_map/sij,sri->srj/dot_general | solution.py:100
  94.7 3.0 %collective-permute-start.21 = (f32[2,16,256]{2,1,0:T(8,128)S(1)}, f32[2,16,256]{2,1,0:T(8,128)S(1)}, u32[]{:S(2)}, u32[]{:S(2)}) collective-permute-start(f32[2,16,256]{2,1,0:T(8,128)S(1)} %bitcast.104), channel_id=1, source_target_pairs={{0,8},{4,12},{8,0},{12,4},{1,9},{5,13},{9,1},{13,5},{2,10},{6,14},... | collective-permute-start | bytes 98312 | tf_op jit(solution)/shard_map/ppermute | solution.py:15
  97.7 1.4 %collective-permute-start.22 = (f32[2,16,256]{2,1,0:T(8,128)S(1)}, f32[2,16,256]{2,1,0:T(8,128)S(1)}, u32[]{:S(2)}, u32[]{:S(2)}) collective-permute-start(f32[2,16,256]{2,1,0:T(8,128)S(1)} %bitcast.105), channel_id=1, source_target_pairs={{0,12},{4,8},{8,4},{12,0},{1,13},{5,9},{9,5},{13,1},{2,14},{6,10},... | collective-permute-start | bytes 98312 | tf_op jit(solution)/shard_map/ppermute | solution.py:15
  99.1 0.6 bitcast_add_fusion.1
  100.1 3.3 %collective-permute-done.22 = f32[2,16,256]{2,1,0:T(8,128)S(1)} collective-permute-done((f32[2,16,256]{2,1,0:T(8,128)S(1)}, f32[2,16,256]{2,1,0:T(8,128)S(1)}, u32[]{:S(2)}, u32[]{:S(2)}) %collective-permute-start.22) | collective-permute-done | bytes 32800 | tf_op jit(solution)/shard_map/ppermute | solution.py:15
  103.4 0.6 bitcast_add_fusion
  (77 shorter events, 4.5 us)
Async XLA Ops:
  0.6 48.6 %copy-start = (f32[128,4096]{1,0:T(8,128)S(1)}, f32[128,4096]{1,0:T(8,128)}, u32[]{:S(2)}) copy-start(f32[128,4096]{1,0:T(8,128)} %param.11) | copy-start | bytes 6291460
  0.7 16.3 %copy-start.2 = (s32[2,16]{1,0:T(2,128)S(1)}, s32[2,16]{1,0:T(2,128)}, u32[]{:S(2)}) copy-start(s32[2,16]{1,0:T(2,128)} %param.9) | copy-start | bytes 388
  10.1 1.4 %collective-permute-start = (f32[1,16,1024]{2,1,0:T(8,128)S(1)}, f32[1,16,1024]{2,1,0:T(8,128)S(1)}, u32[]{:S(2)}, u32[]{:S(2)}) collective-permute-start(f32[1,16,1024]{2,1,0:T(8,128)S(1)} %constant_dynamic-slice_fusion.13), channel_id=1, source_target_pairs={{0,1},{1,0},{2,3},{3,2},{4,5},{5,4},{6,7},{7,6},{8,9},{9,8},{10,11... | collective-permute-start | bytes 196616 | tf_op jit(solution)/shard_map/ppermute | solution.py:15
  11.5 5.3 %collective-permute-start.1 = (f32[1,16,1024]{2,1,0:T(8,128)S(1)}, f32[1,16,1024]{2,1,0:T(8,128)S(1)}, u32[]{:S(2)}, u32[]{:S(2)}) collective-permute-start(f32[1,16,1024]{2,1,0:T(8,128)S(1)} %dynamic-slice_add_fusion.1), channel_id=1, source_target_pairs={{0,2},{1,3},{2,0},{3,1},{4,6},{5,7},{6,4},{7,5},{8,10},{9,11},{10,... | collective-permute-start | bytes 196616 | tf_op jit(solution)/shard_map/ppermute | solution.py:15
  16.9 4.7 %collective-permute-start.2 = (f32[1,16,1024]{2,1,0:T(8,128)S(1)}, f32[1,16,1024]{2,1,0:T(8,128)S(1)}, u32[]{:S(2)}, u32[]{:S(2)}) collective-permute-start(f32[1,16,1024]{2,1,0:T(8,128)S(1)} %add.137), channel_id=1, source_target_pairs={{0,1},{1,0},{2,3},{3,2},{4,5},{5,4},{6,7},{7,6},{8,9},{9,8},{10,11... | collective-permute-start | bytes 196616 | tf_op jit(solution)/shard_map/ppermute | solution.py:15
  27.3 21.9 %copy-start.1 = (f32[16,4096]{1,0:T(8,128)S(1)}, f32[16,4096]{1,0:T(8,128)}, u32[]{:S(2)}) copy-start(f32[16,4096]{1,0:T(8,128)} %param.10) | copy-start | bytes 786436
  27.3 4.7 %collective-permute-start.3 = (f32[2,16,512]{2,1,0:T(8,128)S(1)}, f32[2,16,512]{2,1,0:T(8,128)S(1)}, u32[]{:S(2)}, u32[]{:S(2)}) collective-permute-start(f32[2,16,512]{2,1,0:T(8,128)S(1)} %fusion.22), channel_id=1, source_target_pairs={{0,4},{4,0},{8,12},{12,8},{1,5},{5,1},{9,13},{13,9},{2,6},{6,2},{1... | collective-permute-start | bytes 196616 | tf_op jit(solution)/shard_map/ppermute | solution.py:15
  29.2 6.7 %collective-permute-start.4 = (f32[2,16,512]{2,1,0:T(8,128)S(1)}, f32[2,16,512]{2,1,0:T(8,128)S(1)}, u32[]{:S(2)}, u32[]{:S(2)}) collective-permute-start(f32[2,16,512]{2,1,0:T(8,128)S(1)} %fusion.22), channel_id=1, source_target_pairs={{0,8},{4,12},{8,0},{12,4},{1,9},{5,13},{9,1},{13,5},{2,10},{6,14},... | collective-permute-start | bytes 196616 | tf_op jit(solution)/shard_map/ppermute | solution.py:15
  31.8 6.1 %collective-permute-start.5 = (f32[2,16,512]{2,1,0:T(8,128)S(1)}, f32[2,16,512]{2,1,0:T(8,128)S(1)}, u32[]{:S(2)}, u32[]{:S(2)}) collective-permute-start(f32[2,16,512]{2,1,0:T(8,128)S(1)} %fusion.22), channel_id=1, source_target_pairs={{0,12},{4,8},{8,4},{12,0},{1,13},{5,9},{9,5},{13,1},{2,14},{6,10},... | collective-permute-start | bytes 196616 | tf_op jit(solution)/shard_map/ppermute | solution.py:15
  37.9 5.0 %collective-permute-start.6 = (f32[2,16,512]{2,1,0:T(8,128)S(1)}, f32[2,16,512]{2,1,0:T(8,128)S(1)}, u32[]{:S(2)}, u32[]{:S(2)}) collective-permute-start(f32[2,16,512]{2,1,0:T(8,128)S(1)} %add_add_fusion), channel_id=1, source_target_pairs={{0,2},{1,3},{2,0},{3,1},{16,18},{17,19},{18,16},{19,17},{4,6},{5,7... | collective-permute-start | bytes 196616 | tf_op jit(solution)/shard_map/ppermute | solution.py:15
  39.5 4.3 %collective-permute-start.7 = (f32[2,16,512]{2,1,0:T(8,128)S(1)}, f32[2,16,512]{2,1,0:T(8,128)S(1)}, u32[]{:S(2)}, u32[]{:S(2)}) collective-permute-start(f32[2,16,512]{2,1,0:T(8,128)S(1)} %add_add_fusion), channel_id=1, source_target_pairs={{0,16},{1,17},{2,18},{3,19},{16,0},{17,1},{18,2},{19,3},{4,20},{5,... | collective-permute-start | bytes 196616 | tf_op jit(solution)/shard_map/ppermute | solution.py:15
  41.0 5.2 %collective-permute-start.8 = (f32[2,16,512]{2,1,0:T(8,128)S(1)}, f32[2,16,512]{2,1,0:T(8,128)S(1)}, u32[]{:S(2)}, u32[]{:S(2)}) collective-permute-start(f32[2,16,512]{2,1,0:T(8,128)S(1)} %add_add_fusion), channel_id=1, source_target_pairs={{0,18},{1,19},{2,16},{3,17},{16,2},{17,3},{18,0},{19,1},{4,22},{5,... | collective-permute-start | bytes 196616 | tf_op jit(solution)/shard_map/ppermute | solution.py:15
  46.2 1.6 %collective-permute-start.9 = (f32[4,2,16,512]{3,2,1,0:T(8,128)S(1)}, f32[4,2,16,512]{3,2,1,0:T(8,128)S(1)}, u32[]{:S(2)}, u32[]{:S(2)}) collective-permute-start(f32[4,2,16,512]{3,2,1,0:T(8,128)S(1)} %pad_maximum_fusion), channel_id=1, source_target_pairs={{0,1},{1,0},{2,3},{3,2},{4,5},{5,4},{6,7},{7,6},{8,9},{9,8},{10,11... | collective-permute-start | bytes 786440 | tf_op jit(solution)/shard_map/ppermute | solution.py:15
  54.0 1.7 %collective-permute-start.10 = (f32[4,2,16,512]{3,2,1,0:T(8,128)}, f32[4,2,16,512]{3,2,1,0:T(8,128)S(1)}, u32[]{:S(2)}, u32[]{:S(2)}) collective-permute-start(f32[4,2,16,512]{3,2,1,0:T(8,128)} %squeeze.79), channel_id=1, source_target_pairs={{0,1},{1,0},{2,3},{3,2},{4,5},{5,4},{6,7},{7,6},{8,9},{9,8},{10,11... | collective-permute-start | bytes 786440 | tf_op jit(solution)/shard_map/ppermute | solution.py:15
  55.8 4.3 %collective-permute-start.11 = (f32[2,16,512]{2,1,0:T(8,128)S(1)}, f32[2,16,512]{2,1,0:T(8,128)S(1)}, u32[]{:S(2)}, u32[]{:S(2)}) collective-permute-start(f32[2,16,512]{2,1,0:T(8,128)S(1)} %get-tuple-element.12), channel_id=1, source_target_pairs={{0,2},{1,3},{2,0},{3,1},{16,18},{17,19},{18,16},{19,17},{4,6},{5,7... | collective-permute-start | bytes 196616 | tf_op jit(solution)/shard_map/ppermute | solution.py:15
  56.4 4.9 %collective-permute-start.12 = (f32[2,16,512]{2,1,0:T(8,128)S(1)}, f32[2,16,512]{2,1,0:T(8,128)S(1)}, u32[]{:S(2)}, u32[]{:S(2)}) collective-permute-start(f32[2,16,512]{2,1,0:T(8,128)S(1)} %get-tuple-element.10), channel_id=1, source_target_pairs={{0,16},{1,17},{2,18},{3,19},{16,0},{17,1},{18,2},{19,3},{4,20},{5,... | collective-permute-start | bytes 196616 | tf_op jit(solution)/shard_map/ppermute | solution.py:15
  57.2 5.5 %collective-permute-start.13 = (f32[2,16,512]{2,1,0:T(8,128)S(1)}, f32[2,16,512]{2,1,0:T(8,128)S(1)}, u32[]{:S(2)}, u32[]{:S(2)}) collective-permute-start(f32[2,16,512]{2,1,0:T(8,128)S(1)} %get-tuple-element.11), channel_id=1, source_target_pairs={{0,18},{1,19},{2,16},{3,17},{16,2},{17,3},{18,0},{19,1},{4,22},{5,... | collective-permute-start | bytes 196616 | tf_op jit(solution)/shard_map/ppermute | solution.py:15
  59.4 7.7 %collective-permute-start.23 = (f32[4,16,4,128]{3,1,2,0:T(8,128)S(1)}, f32[4,16,4,128]{3,1,2,0:T(8,128)S(1)}, u32[]{:S(2)}, u32[]{:S(2)}) collective-permute-start(f32[4,16,4,128]{3,1,2,0:T(8,128)S(1)} %slice_bitcast_fusion), channel_id=1, source_target_pairs={{0,1},{1,0},{2,3},{3,2},{4,5},{5,4},{6,7},{7,6},{8,9},{9,8},{10,11... | collective-permute-start | bytes 393224 | tf_op jit(solution)/shard_map/ppermute | solution.py:15
  62.7 4.5 %collective-permute-start.14 = (f32[2,16,512]{2,1,0:T(8,128)S(1)}, f32[2,16,512]{2,1,0:T(8,128)S(1)}, u32[]{:S(2)}, u32[]{:S(2)}) collective-permute-start(f32[2,16,512]{2,1,0:T(8,128)S(1)} %fusion.27), channel_id=1, source_target_pairs={{0,4},{4,0},{8,12},{12,8},{1,5},{5,1},{9,13},{13,9},{2,6},{6,2},{1... | collective-permute-start | bytes 196616 | tf_op jit(solution)/shard_map/ppermute | solution.py:15
  62.7 6.8 %collective-permute-start.15 = (f32[2,16,512]{2,1,0:T(8,128)S(1)}, f32[2,16,512]{2,1,0:T(8,128)S(1)}, u32[]{:S(2)}, u32[]{:S(2)}) collective-permute-start(f32[2,16,512]{2,1,0:T(8,128)S(1)} %fusion.27), channel_id=1, source_target_pairs={{0,8},{4,12},{8,0},{12,4},{1,9},{5,13},{9,1},{13,5},{2,10},{6,14},... | collective-permute-start | bytes 196616 | tf_op jit(solution)/shard_map/ppermute | solution.py:15
  64.6 6.2 %collective-permute-start.16 = (f32[2,16,512]{2,1,0:T(8,128)S(1)}, f32[2,16,512]{2,1,0:T(8,128)S(1)}, u32[]{:S(2)}, u32[]{:S(2)}) collective-permute-start(f32[2,16,512]{2,1,0:T(8,128)S(1)} %fusion.27), channel_id=1, source_target_pairs={{0,12},{4,8},{8,4},{12,0},{1,13},{5,9},{9,5},{13,1},{2,14},{6,10},... | collective-permute-start | bytes 196616 | tf_op jit(solution)/shard_map/ppermute | solution.py:15
  75.2 3.7 %collective-permute-start.17 = (f32[1,16,1024]{2,1,0:T(8,128)S(1)}, f32[1,16,1024]{2,1,0:T(8,128)S(1)}, u32[]{:S(2)}, u32[]{:S(2)}) collective-permute-start(f32[1,16,1024]{2,1,0:T(8,128)S(1)} %constant_dynamic-slice_fusion.6), channel_id=1, source_target_pairs={{0,1},{1,0},{2,3},{3,2},{4,5},{5,4},{6,7},{7,6},{8,9},{9,8},{10,11... | collective-permute-start | bytes 196616 | tf_op jit(solution)/shard_map/ppermute | solution.py:15
  75.3 4.6 %collective-permute-start.24 = (f32[16,4,128]{2,0,1:T(8,128)S(1)}, f32[16,4,128]{2,0,1:T(8,128)S(1)}, u32[]{:S(2)}, u32[]{:S(2)}) collective-permute-start(f32[16,4,128]{2,0,1:T(8,128)S(1)} %get-tuple-element.15), channel_id=1, source_target_pairs={{0,2},{1,3},{2,0},{3,1},{16,18},{17,19},{18,16},{19,17},{4,6},{5,7... | collective-permute-start | bytes 98312 | tf_op jit(solution)/shard_map/ppermute | solution.py:15
  76.4 3.9 %collective-permute-start.25 = (f32[16,4,128]{2,0,1:T(8,128)S(1)}, f32[16,4,128]{2,0,1:T(8,128)S(1)}, u32[]{:S(2)}, u32[]{:S(2)}) collective-permute-start(f32[16,4,128]{2,0,1:T(8,128)S(1)} %get-tuple-element.13), channel_id=1, source_target_pairs={{0,16},{1,17},{2,18},{3,19},{16,0},{17,1},{18,2},{19,3},{4,20},{5,... | collective-permute-start | bytes 98312 | tf_op jit(solution)/shard_map/ppermute | solution.py:15
  77.9 4.8 %collective-permute-start.26 = (f32[16,4,128]{2,0,1:T(8,128)S(1)}, f32[16,4,128]{2,0,1:T(8,128)S(1)}, u32[]{:S(2)}, u32[]{:S(2)}) collective-permute-start(f32[16,4,128]{2,0,1:T(8,128)S(1)} %get-tuple-element.14), channel_id=1, source_target_pairs={{0,18},{1,19},{2,16},{3,17},{16,2},{17,3},{18,0},{19,1},{4,22},{5,... | collective-permute-start | bytes 98312 | tf_op jit(solution)/shard_map/ppermute | solution.py:15
  78.9 4.5 %collective-permute-start.18 = (f32[1,16,1024]{2,1,0:T(8,128)S(1)}, f32[1,16,1024]{2,1,0:T(8,128)S(1)}, u32[]{:S(2)}, u32[]{:S(2)}) collective-permute-start(f32[1,16,1024]{2,1,0:T(8,128)S(1)} %dynamic-slice_add_fusion), channel_id=1, source_target_pairs={{0,2},{1,3},{2,0},{3,1},{4,6},{5,7},{6,4},{7,5},{8,10},{9,11},{10,... | collective-permute-start | bytes 196616 | tf_op jit(solution)/shard_map/ppermute | solution.py:15
  83.4 4.6 %collective-permute-start.19 = (f32[1,16,1024]{2,1,0:T(8,128)S(1)}, f32[1,16,1024]{2,1,0:T(8,128)S(1)}, u32[]{:S(2)}, u32[]{:S(2)}) collective-permute-start(f32[1,16,1024]{2,1,0:T(8,128)S(1)} %add.155), channel_id=1, source_target_pairs={{0,1},{1,0},{2,3},{3,2},{4,5},{5,4},{6,7},{7,6},{8,9},{9,8},{10,11... | collective-permute-start | bytes 196616 | tf_op jit(solution)/shard_map/ppermute | solution.py:15
  83.5 14.2 %collective-permute-start.27 = (f32[16,128]{1,0:T(8,128)S(1)}, f32[16,128]{1,0:T(8,128)S(1)}, u32[]{:S(2)}, u32[]{:S(2)}) collective-permute-start(f32[16,128]{1,0:T(8,128)S(1)} %get-tuple-element.22), channel_id=1, source_target_pairs={{0,4},{4,0},{8,12},{12,8},{1,5},{5,1},{9,13},{13,9},{2,6},{6,2},{1... | collective-permute-start | bytes 24584 | tf_op jit(solution)/shard_map/ppermute | solution.py:15
  84.2 14.9 %collective-permute-start.28 = (f32[16,128]{1,0:T(8,128)S(1)}, f32[16,128]{1,0:T(8,128)S(1)}, u32[]{:S(2)}, u32[]{:S(2)}) collective-permute-start(f32[16,128]{1,0:T(8,128)S(1)} %get-tuple-element.20), channel_id=1, source_target_pairs={{0,8},{4,12},{8,0},{12,4},{1,9},{5,13},{9,1},{13,5},{2,10},{6,14},... | collective-permute-start | bytes 24584 | tf_op jit(solution)/shard_map/ppermute | solution.py:15
  86.6 12.5 %collective-permute-start.29 = (f32[16,128]{1,0:T(8,128)S(1)}, f32[16,128]{1,0:T(8,128)S(1)}, u32[]{:S(2)}, u32[]{:S(2)}) collective-permute-start(f32[16,128]{1,0:T(8,128)S(1)} %get-tuple-element.21), channel_id=1, source_target_pairs={{0,12},{4,8},{8,4},{12,0},{1,13},{5,9},{9,5},{13,1},{2,14},{6,10},... | collective-permute-start | bytes 24584 | tf_op jit(solution)/shard_map/ppermute | solution.py:15
  94.6 5.1 %collective-permute-start.20 = (f32[2,16,256]{2,1,0:T(8,128)S(1)}, f32[2,16,256]{2,1,0:T(8,128)S(1)}, u32[]{:S(2)}, u32[]{:S(2)}) collective-permute-start(f32[2,16,256]{2,1,0:T(8,128)S(1)} %bitcast.103), channel_id=1, source_target_pairs={{0,4},{4,0},{8,12},{12,8},{1,5},{5,1},{9,13},{13,9},{2,6},{6,2},{1... | collective-permute-start | bytes 98312 | tf_op jit(solution)/shard_map/ppermute | solution.py:15
  94.7 5.4 %collective-permute-start.21 = (f32[2,16,256]{2,1,0:T(8,128)S(1)}, f32[2,16,256]{2,1,0:T(8,128)S(1)}, u32[]{:S(2)}, u32[]{:S(2)}) collective-permute-start(f32[2,16,256]{2,1,0:T(8,128)S(1)} %bitcast.104), channel_id=1, source_target_pairs={{0,8},{4,12},{8,0},{12,4},{1,9},{5,13},{9,1},{13,5},{2,10},{6,14},... | collective-permute-start | bytes 98312 | tf_op jit(solution)/shard_map/ppermute | solution.py:15
  97.7 5.7 %collective-permute-start.22 = (f32[2,16,256]{2,1,0:T(8,128)S(1)}, f32[2,16,256]{2,1,0:T(8,128)S(1)}, u32[]{:S(2)}, u32[]{:S(2)}) collective-permute-start(f32[2,16,256]{2,1,0:T(8,128)S(1)} %bitcast.105), channel_id=1, source_target_pairs={{0,12},{4,8},{8,4},{12,0},{1,13},{5,9},{9,5},{13,1},{2,14},{6,10},... | collective-permute-start | bytes 98312 | tf_op jit(solution)/shard_map/ppermute | solution.py:15

commit v2 on v1

v2 whole, which is shorter than its diff:
```python
import functools

import jax
import jax.numpy as jnp
from jax import lax
from jax.experimental import pallas as pl
from jax.experimental.pallas import tpu as pltpu
from jax.sharding import PartitionSpec as P

BLOCK = 128
CORES = 2
MIB = 1 << 20

F32, BF16 = jnp.float32, jnp.bfloat16
HBM = pl.BlockSpec(memory_space=pltpu.HBM)
SCALARS = pl.BlockSpec(memory_space=pltpu.SMEM)
WHOLE = pl.BlockSpec(memory_space=pltpu.VMEM)


def in_hbm(value):
    return pltpu.with_memory_space_constraint(value, pltpu.HBM)


def split(value):
    high = value.astype(BF16)
    return high, (value - high.astype(F32)).astype(BF16)


def dot3(value, matrix, dims):
    rows = value.shape[0]
    high, low = split(matrix)
    parts = jnp.concatenate(split(value))
    main = lax.dot_general(parts, high, dims, preferred_element_type=F32)
    rest = lax.dot_general(parts[:rows], low, dims, preferred_element_type=F32)
    return main[:rows] + (main[rows:] + rest)


ROWS_OF = (((1,), (1,)), ((), ()))
COLUMNS_OF = (((1,), (0,)), ((), ()))


def sub_of(slot, half, core):
    return core * half + slot if slot < half else (1 - core) * half + (slot - half)


def chunk_of(rows):
    return min(rows, 512)


def leaf_kernel(rhs, inverse, out, held, land, sems, rhs_sem):
    subs, rows, _ = inverse.shape
    chunk = chunk_of(rows)
    steps = rows // chunk

    def fetch(sub, step):
        part = pl.ds(step * chunk, chunk)
        return pltpu.make_async_copy(
            inverse.at[sub, part], land.at[sub, part], sems.at[sub * steps + step]
        )

    first = pltpu.make_async_copy(rhs, held, rhs_sem)
    first.start()
    for sub in range(subs):
        for step in range(steps):
            fetch(sub, step).start()
    first.wait()
    for sub in range(subs):
        for step in range(steps):
            part = pl.ds(step * chunk, chunk)
            fetch(sub, step).wait()
            out[sub, :, part] = dot3(held[sub], land[sub, part], ROWS_OF)


def couple_kernel(place, mine, other, update, out):
    half, up = mine.shape[0], update.shape[1]
    for slot in range(2 * half):
        value = mine[slot] if slot < half else other[slot - half]
        sub = sub_of(slot, half, place[0])
        out[:, slot * up : (slot + 1) * up] = dot3(value, update[sub], ROWS_OF)


def spots(sizes, half, place, maps, chips, side, here):
    lines = sizes[3]
    core = place[0] if side == 0 else 1 - place[0]
    for chip in range(chips):
        first = ((place[2] ^ (chip % lines)) * CORES + core) * here
        for slot in range(2 * half):
            sub = sub_of(slot, half, core)
            for k in range(here):
                at = (slot * here + k) * BLOCK
                yield chip, slice(at, at + BLOCK), maps[chip // lines, sub, first + k]


def scatter_kernel(sizes, half, place, maps, near, rhs, out):
    here = near.shape[2] // (2 * half * BLOCK)
    for b in range(out.shape[0]):
        out[b] = rhs[:, b * BLOCK : (b + 1) * BLOCK]
    for chip, lanes, block in spots(sizes, half, place, maps, near.shape[0], 0, here):
        out[block] -= near[chip, :, lanes]


def separator_kernel(sizes, half, inside, place, maps, far, start, sep, keep, send, *rest):
    _, rows, cols, lines = sizes
    held = rest[-1]
    core, plane = place[0], place[1]
    chips = far.shape[0]
    total = held.shape[0]
    here = far.shape[2] // (2 * half * BLOCK)

    held[...] = start[...]
    for chip, lanes, block in spots(sizes, half, place, maps, chips, 1, here):
        held[block] -= far[chip, :, lanes]
    updated = jnp.concatenate([held[b] for b in range(total)], 1)
    forward = dot3(updated, sep[...], ROWS_OF)
    terms = dot3(forward, sep[...], COLUMNS_OF)
    for b in range(total):
        held[b] = terms[:, b * BLOCK : (b + 1) * BLOCK]
    for side, out in ((1, send), (0, keep)):
        for chip, lanes, block in spots(sizes, half, place, maps, chips, side, here):
            out[chip, :, lanes] = held[block]
    if not inside:
        rest[0][...] = terms
        return
    wide = sep.shape[0] // BLOCK
    for side, out in ((1, send), (0, keep)):
        for chip in range(chips):
            other = plane ^ chip
            col = (other % lines) * CORES + (core if side == 0 else 1 - core)
            for row in range(rows):
                for w in range(wide):
                    block = ((other // lines * rows + row) * cols + col) * wide + w
                    at = (2 * half * here + row * wide + w) * BLOCK
                    out[chip, :, at : at + BLOCK] = held[block]


def pull_kernel(place, pulled, update, mine, other):
    half, up = mine.shape[0], update.shape[1]
    for slot in [*range(half, 2 * half), *range(half)]:
        out, at = (mine, slot) if slot < half else (other, slot - half)
        value = pulled[:, slot * up : (slot + 1) * up]
        out[at] = dot3(value, update[sub_of(slot, half, place[0])], COLUMNS_OF)


def solve_kernel(place, mine, other, pull_mine, pull_other, inverse, out):
    half = mine.shape[0]
    for slot in range(2 * half):
        if slot < half:
            value = mine[slot] - pull_mine[slot]
        else:
            value = other[slot - half] - pull_other[slot - half]
        sub = sub_of(slot, half, place[0])
        out[sub] = dot3(value, inverse[sub], COLUMNS_OF)


def finish_kernel(*refs):
    *parts, leaf_out, sep_out = refs
    share = leaf_out.shape[2]
    done = sum(part[...] for part in parts[1:]) + parts[0][...]
    for sub in range(leaf_out.shape[0]):
        leaf_out[sub] = done[:, sub * share : (sub + 1) * share]
    sep_out[...] = done[:, leaf_out.shape[0] * share :]


def swap(value, axes, size, mask):
    return lax.ppermute(value, axes, [(i, i ^ mask) for i in range(size)])


def picked(value, dim, index, count):
    return jnp.stack(
        [lax.dynamic_index_in_dim(value, index ^ m, dim, keepdims=False) for m in range(count)], dim
    )


def halves(value, core):
    half = value.shape[0] // CORES
    return tuple(lax.dynamic_slice_in_dim(value, c * half, half, 0) for c in (core, 1 - core))


def sum_over_lines(mine, cols):
    step = CORES
    while step < cols:
        mine = mine + swap(mine, "col", cols, step)
        step *= 2
    return mine, swap(mine, "col", cols, 1)


def call(kernel, out_shape, in_specs, limit, cost, scratch=()):
    flops, nbytes = cost
    return pl.pallas_call(
        kernel,
        out_shape=out_shape,
        in_specs=in_specs,
        scratch_shapes=scratch,
        compiler_params=pltpu.CompilerParams(vmem_limit_bytes=limit * MIB),
        cost_estimate=pl.CostEstimate(flops=flops, bytes_accessed=nbytes, transcendentals=0),
    )


def body(sizes, leaf_rhs, leaf_inverse, update_rows, update_map, sep_rhs, sep_inverse):
    leaves, rows, cols = sizes
    lines = cols // CORES
    chips = leaves * lines
    subs, nrhs, _ = leaf_rhs.shape
    half = subs // CORES
    width = sep_rhs.shape[1]
    sep_rows = sep_inverse.shape[0]
    _, leaf_rows, leaf_cols = leaf_inverse.shape
    up = update_rows.shape[1]
    leaf, row, col = (lax.axis_index(a) for a in ("leaf", "row", "col"))
    core, line = col % CORES, col // CORES
    plane = leaf * lines + line
    place = jnp.stack([core, plane, line]).astype(jnp.int32)
    plane_axes, plane_size = ("leaf", "col"), leaves * cols

    vec = jax.ShapeDtypeStruct((half, nrhs, leaf_rows), F32)
    leaf_flops = 2 * nrhs * leaf_inverse.size
    forward = call(
        leaf_kernel,
        jax.ShapeDtypeStruct((subs, nrhs, leaf_rows), F32),
        [HBM, HBM],
        24,
        (leaf_flops, 4 * leaf_inverse.size),
        (
            pltpu.VMEM(leaf_rhs.shape, F32),
            pltpu.VMEM(leaf_inverse.shape, F32),
            pltpu.SemaphoreType.DMA((subs * (leaf_rows // chunk_of(leaf_rows)),)),
            pltpu.SemaphoreType.DMA,
        ),
    )(in_hbm(leaf_rhs), in_hbm(leaf_inverse))
    forward, leaf_inverse, update_rows, sep_inverse, sep_rhs = lax.optimization_barrier(
        (forward, leaf_inverse, update_rows, sep_inverse, sep_rhs)
    )
    mine, other = halves(forward, core)
    mine = mine + swap(other, "col", cols, 1)
    mine, update_map = lax.optimization_barrier((mine, update_map))
    maps = [update_map] + [swap(update_map, "leaf", leaves, m) for m in range(1, leaves)]
    mine, other = sum_over_lines(mine, cols)
    mine, other, maps = lax.optimization_barrier((mine, other, maps))
    maps = jnp.stack(maps)
    update_cost = (2 * nrhs * update_rows.size, 4 * update_rows.size)
    coupled = call(
        couple_kernel,
        jax.ShapeDtypeStruct((nrhs, subs * up), F32),
        [SCALARS] + [WHOLE] * 3,
        12,
        update_cost,
    )(place, mine, other, update_rows)
    coupled = coupled + sum(swap(coupled, "row", rows, k) for k in range(1, rows))
    near = jnp.stack(
        [coupled] + [swap(coupled, plane_axes, plane_size, CORES * m) for m in range(1, chips)]
    )
    far = swap(near, "col", cols, 1)

    shape = (leaves, rows, cols, lines)
    start = call(
        functools.partial(scatter_kernel, shape, half),
        jax.ShapeDtypeStruct((width // BLOCK, nrhs, BLOCK), F32),
        [SCALARS, SCALARS, WHOLE, WHOLE],
        4,
        (2 * nrhs * width, 12 * nrhs * width),
    )(place, maps, near, sep_rhs)
    inside = sep_rows % BLOCK == 0
    own_width = rows * sep_rows
    length = subs * up + (own_width if inside else 0)
    piece = jax.ShapeDtypeStruct((chips, nrhs, length), F32)
    keep, send, *back = call(
        functools.partial(separator_kernel, shape, half, inside),
        (piece, piece) + (() if inside else (jax.ShapeDtypeStruct((nrhs, width), F32),)),
        [SCALARS, SCALARS] + [WHOLE] * 3,
        12,
        (4 * nrhs * sep_inverse.size, 4 * sep_inverse.size),
        (pltpu.VMEM((width // BLOCK, nrhs, BLOCK), F32),),
    )(place, maps, far, start, sep_inverse)
    if not inside:
        own = back[0].reshape(nrhs, leaves, rows, lines, CORES, sep_rows)
        own = own.transpose(4, 1, 3, 0, 2, 5).reshape(CORES, chips, nrhs, own_width)
        own = picked(picked(own, 0, core, CORES), 1, plane, chips)
        keep = jnp.concatenate([keep, own[0]], 2)
        send = jnp.concatenate([send, own[1]], 2)
    keep = keep + swap(send, "col", cols, 1)
    pulled = keep[0] + sum(swap(keep[m], plane_axes, plane_size, CORES * m) for m in range(1, chips))
    own = pulled[:, subs * up :].reshape(nrhs, rows, sep_rows)
    pulled = pulled[:, : subs * up]
    pulled = pulled + sum(swap(pulled, "row", rows, k) for k in range(1, rows))

    pull_mine, pull_other = call(
        pull_kernel, (vec, vec), [SCALARS, WHOLE, WHOLE], 12, update_cost
    )(place, pulled, update_rows)
    pull_mine = pull_mine + swap(pull_other, "col", cols, 1)
    pull_mine, pull_other = sum_over_lines(pull_mine, cols)
    terms = call(
        solve_kernel,
        jax.ShapeDtypeStruct((subs, nrhs, leaf_cols), F32),
        [SCALARS] + [WHOLE] * 5,
        16,
        (leaf_flops, 4 * leaf_inverse.size),
    )(place, mine, other, pull_mine, pull_other, leaf_inverse)

    share = leaf_cols // rows

    def last(k):
        at = row ^ k
        leaf_part = lax.dynamic_slice_in_dim(terms, at * share, share, 2)
        own_part = lax.dynamic_index_in_dim(own, at, 1, keepdims=False)
        return jnp.concatenate([*leaf_part, own_part], 1)

    parts = [last(0)] + [swap(last(k), "row", rows, k) for k in range(1, rows)]
    if inside and share % BLOCK == 0:
        return call(
            finish_kernel,
            (
                jax.ShapeDtypeStruct((subs, nrhs, share), F32),
                jax.ShapeDtypeStruct((nrhs, sep_rows), F32),
            ),
            [WHOLE] * rows,
            4,
            (parts[0].size * rows, 4 * parts[0].size * rows),
        )(*parts)
    done = sum(parts[1:]) + parts[0]
    leaf_solution = jnp.stack([done[:, s * share : (s + 1) * share] for s in range(subs)])
    return (leaf_solution, done[:, subs * share :])


def solution(mesh):
    sizes = tuple(mesh.shape[a] for a in ("leaf", "row", "col"))
    in_specs = (
        P("leaf", None, "col"),
        P("leaf", "row", "col"),
        P("leaf", "col", "row"),
        P("leaf", None),
        P(),
        P(("leaf", "row", "col"), None),
    )
    out_specs = (P("leaf", None, ("col", "row")), P(None, ("leaf", "row", "col")))
    return jax.shard_map(
        functools.partial(body, sizes), mesh=mesh, in_specs=in_specs, out_specs=out_specs, check_vma=False
    )
```

time: 104 us -> 82.5 us (0.79)
  matrix products: 30.6 us -> 0 us
  Pallas kernels: 0 us -> 15 us
  starting transfers between devices: 33.5 us -> 26.5 us
  blocking collectives: 4.43 us -> 0 us
  waiting for transfers between devices: 30.2 us -> 34 us
  local copies, waits for them, and re-layouts: 2.59 us -> 5.69 us
  other arithmetic: 1.57 us -> 0.26 us
    dot_general x8 -> x0, matrix products: 30.6 us -> none  [the longest x1 9.4 us: body(): jnp.einsum('sij,srj->sri', leaf_inverse, leaf_rhs, precision=HIGH)]
    pallas_call x0 -> x7, Pallas kernels: none -> 15 us  [the longest x1 5.73 us: body(): call(leaf_kernel, jax.ShapeDtypeStruct((subs, nrhs, leaf_rows), F32), [HB...]
    ppermute x30 -> x24, starting transfers between devices: 33.5 us -> 26.5 us  [swap(): return lax.ppermute(value, axes, [(i, i ^ mask) for i in range(size)])]
    unnamed x10 -> x12, local copies, waits for them, and re-layouts: 0.08 us -> 5.59 us
    all_gather x1 -> x0, blocking collectives: 4.43 us -> none  [body(): maps = lax.all_gather(update_map, 'leaf')]
    ppermute x30 -> x24, waiting for transfers between devices: 30.2 us -> 34 us  [swap(): return lax.ppermute(value, axes, [(i, i ^ mask) for i in range(size)])]
    add x10 -> x7, other arithmetic: 1.35 us -> 0.13 us  [the longest x1 0.04 us: body(): keep = keep + swap(send, 'col', cols, 1)]
  transfers between devices with their start and end apart: 30 -> 24, of which waited for: 19 -> 21; matrix products, arithmetic and copies ran while one was open for 8% -> 0% of each run, Pallas kernels for 0% -> 1%
where the time goes in v2:
time: 82.5 us; the launch traced here: 82.3 us
  waiting for transfers between devices  34 us (41%)
  starting transfers between devices  26.5 us (32%)
  Pallas kernels  15 us (18%)
  local copies, waits for them, and re-layouts  5.69 us (7%)
  between operations  0.85 us (1%)
    ppermute x24, waiting for transfers between devices, swap(): return lax.ppermute(value, axes, [(i, i ^ mask) for i in range(size)])  34 us
    ppermute x24, starting transfers between devices, swap(): return lax.ppermute(value, axes, [(i, i ^ mask) for i in range(size)])  26.5 us
    pallas_call x1, Pallas kernels, body(): call(leaf_kernel, jax.ShapeDtypeStruct((subs, nrhs, leaf_rows), F32), [HB...  5.73 us
    unnamed x12, local copies, waits for them, and re-layouts  5.59 us
    pallas_call x1, Pallas kernels, body(): call(functools.partial(separator_kernel, shape, half, inside), (piece, pi...  2.4 us
    pallas_call x1, Pallas kernels, body(): call(solve_kernel, jax.ShapeDtypeStruct((subs, nrhs, leaf_cols), F32), [S...  2.13 us
    pallas_call x1, Pallas kernels, body(): call(couple_kernel, jax.ShapeDtypeStruct((nrhs, subs * up), F32), [SCALAR...  1.87 us
  transfers between devices with their start and end apart: 24, of which 21 were waited for; matrix products, arithmetic and copies ran while one was open for 0% of the time, Pallas kernels for 1%

profile of v2, /device:TPU:0, one launch (start us, length us, event | category | flops | bytes accessed | tf_op | source)
XLA Modules:
  0.0 82.3 jit_solution(10804081368719549634)
XLA Ops:
  0.7 5.7 %shard_map.77 = f32[2,16,1024]{2,1,0:T(8,128)S(1)} custom-call(f32[2,16,1024]{2,1,0:T(8,128)} %rhs.1, f32[2,1024,1024]{2,1,0:T(8,128)} %inverse.2), custom_call_target="tpu_custom_call" | custom-call | flops 67108864 | bytes 8388608 | tf_op jit(solution)/shard_map/pallas_call | solution.py:217
  6.4 0.5 collective-permute-start
  7.0 0.9 %collective-permute-done = f32[1,16,1024]{2,1,0:T(8,128)S(1)} collective-permute-done((f32[1,16,1024]{2,1,0:T(8,128)S(1)}, f32[1,16,1024]{2,1,0:T(8,128)S(1)}, u32[]{:S(2)}, u32[]{:S(2)}) %collective-permute-start) | collective-permute-done | bytes 65568 | tf_op jit(solution)/shard_map/ppermute | solution.py:165
  7.9 2.9 %collective-permute-start.1 = (f32[1,16,1024]{2,1,0:T(8,128)S(1)}, f32[1,16,1024]{2,1,0:T(8,128)S(1)}, u32[]{:S(2)}, u32[]{:S(2)}) collective-permute-start(f32[1,16,1024]{2,1,0:T(8,128)S(1)} %dynamic-slice_add_fusion), channel_id=1, source_target_pairs={{0,2},{1,3},{2,0},{3,1},{4,6},{5,7},{6,4},{7,5},{8,10},{9,11},{10,... | collective-permute-start | bytes 196616 | tf_op jit(solution)/shard_map/ppermute | solution.py:165
  10.8 1.5 %collective-permute-start.3 = (s32[2,16]{1,0:T(2,128)S(1)}, s32[2,16]{1,0:T(2,128)S(1)}, u32[]{:S(2)}, u32[]{:S(2)}) collective-permute-start(s32[2,16]{1,0:T(2,128)S(1)} %copy-done.5), channel_id=1, source_target_pairs={{0,16},{16,0},{1,17},{17,1},{2,18},{18,2},{3,19},{19,3},{4,20},{20... | collective-permute-start | bytes 392 | tf_op jit(solution)/shard_map/ppermute | solution.py:165
  12.3 0.9 %collective-permute-done.1 = f32[1,16,1024]{2,1,0:T(8,128)S(1)} collective-permute-done((f32[1,16,1024]{2,1,0:T(8,128)S(1)}, f32[1,16,1024]{2,1,0:T(8,128)S(1)}, u32[]{:S(2)}, u32[]{:S(2)}) %collective-permute-start.1) | collective-permute-done | bytes 65568 | tf_op jit(solution)/shard_map/ppermute | solution.py:165
  13.4 1.0 %collective-permute-done.3 = s32[2,16]{1,0:T(2,128)S(1)} collective-permute-done((s32[2,16]{1,0:T(2,128)S(1)}, s32[2,16]{1,0:T(2,128)S(1)}, u32[]{:S(2)}, u32[]{:S(2)}) %collective-permute-start.3) | collective-permute-done | bytes 160 | tf_op jit(solution)/shard_map/ppermute | solution.py:165
  14.4 0.2 collective-permute-done.2.other
  14.6 2.2 %copy-done.1 = f32[2,512,1024]{2,1,0:T(8,128)S(1)} copy-done((f32[2,512,1024]{2,1,0:T(8,128)S(1)}, f32[2,512,1024]{2,1,0:T(8,128)}, u32[]{:S(2)}) %copy-start.1) | copy-done | bytes 4194328
  16.8 1.9 %shard_map.78 = f32[16,1024]{1,0:T(8,128)S(1)} custom-call(s32[3]{0:T(128)S(1)} %pad_add_fusion.1.place, f32[1,16,1024]{2,1,0:T(8,128)S(1)} %add.87.mine, f32[1,16,1024]{2,1,0:T(8,128)S(1)} %collective-permute-done.2.other, f32[2,512,1024]{2,1,0:T(8,128)S(1)} %copy-done.1), custom_call_target="tpu_custom_call" | custom-call | flops 33554432 | bytes 4194304 | tf_op jit(solution)/shard_map/pallas_call | solution.py:241
  18.6 1.9 %collective-permute-start.4 = (f32[16,1024]{1,0:T(8,128)S(1)}, f32[16,1024]{1,0:T(8,128)S(1)}, u32[]{:S(2)}, u32[]{:S(2)}) collective-permute-start(f32[16,1024]{1,0:T(8,128)S(1)} %shard_map.78), channel_id=1, source_target_pairs={{0,4},{4,0},{8,12},{12,8},{1,5},{5,1},{9,13},{13,9},{2,6},{6,2},{1... | collective-permute-start | bytes 196616 | tf_op jit(solution)/shard_map/ppermute | solution.py:165
  20.6 2.6 %collective-permute-start.5 = (f32[16,1024]{1,0:T(8,128)S(1)}, f32[16,1024]{1,0:T(8,128)S(1)}, u32[]{:S(2)}, u32[]{:S(2)}) collective-permute-start(f32[16,1024]{1,0:T(8,128)S(1)} %shard_map.78), channel_id=1, source_target_pairs={{0,8},{4,12},{8,0},{12,4},{1,9},{5,13},{9,1},{13,5},{2,10},{6,14},... | collective-permute-start | bytes 196616 | tf_op jit(solution)/shard_map/ppermute | solution.py:165
  23.1 5.0 %collective-permute-done.5 = f32[16,1024]{1,0:T(8,128)S(1)} collective-permute-done((f32[16,1024]{1,0:T(8,128)S(1)}, f32[16,1024]{1,0:T(8,128)S(1)}, u32[]{:S(2)}, u32[]{:S(2)}) %collective-permute-start.5) | collective-permute-done | bytes 65568 | tf_op jit(solution)/shard_map/ppermute | solution.py:165
  28.1 1.2 %collective-permute-done.6 = f32[16,1024]{1,0:T(8,128)S(1)} collective-permute-done((f32[16,1024]{1,0:T(8,128)S(1)}, f32[16,1024]{1,0:T(8,128)S(1)}, u32[]{:S(2)}, u32[]{:S(2)}) %collective-permute-start.6) | collective-permute-done | bytes 65568 | tf_op jit(solution)/shard_map/ppermute | solution.py:165
  29.3 1.6 %collective-permute-start.7 = (f32[16,1024]{1,0:T(8,128)S(1)}, f32[16,1024]{1,0:T(8,128)S(1)}, u32[]{:S(2)}, u32[]{:S(2)}) collective-permute-start(f32[16,1024]{1,0:T(8,128)S(1)} %add_add_fusion.1), channel_id=1, source_target_pairs={{0,2},{1,3},{2,0},{3,1},{16,18},{17,19},{18,16},{19,17},{4,6},{5,7... | collective-permute-start | bytes 196616 | tf_op jit(solution)/shard_map/ppermute | solution.py:165
  30.9 1.5 %collective-permute-start.8 = (f32[16,1024]{1,0:T(8,128)S(1)}, f32[16,1024]{1,0:T(8,128)S(1)}, u32[]{:S(2)}, u32[]{:S(2)}) collective-permute-start(f32[16,1024]{1,0:T(8,128)S(1)} %add_add_fusion.1), channel_id=1, source_target_pairs={{0,16},{1,17},{2,18},{3,19},{16,0},{17,1},{18,2},{19,3},{4,20},{5,... | collective-permute-start | bytes 196616 | tf_op jit(solution)/shard_map/ppermute | solution.py:165
  32.4 0.5 collective-permute-start.9
  32.9 0.8 collective-permute-done.7
  33.7 1.5 %collective-permute-done.8 = f32[16,1024]{1,0:T(8,128)S(1)} collective-permute-done((f32[16,1024]{1,0:T(8,128)S(1)}, f32[16,1024]{1,0:T(8,128)S(1)}, u32[]{:S(2)}, u32[]{:S(2)}) %collective-permute-start.8) | collective-permute-done | bytes 65568 | tf_op jit(solution)/shard_map/ppermute | solution.py:165
  35.2 2.4 %collective-permute-done.9 = f32[16,1024]{1,0:T(8,128)S(1)} collective-permute-done((f32[16,1024]{1,0:T(8,128)S(1)}, f32[16,1024]{1,0:T(8,128)S(1)}, u32[]{:S(2)}, u32[]{:S(2)}) %collective-permute-start.9) | collective-permute-done | bytes 65568 | tf_op jit(solution)/shard_map/ppermute | solution.py:165
  37.7 0.7 shard_map.79.start
  38.4 0.8 collective-permute-done.10.far
  39.2 2.4 %shard_map.80 = (f32[4,16,1536]{2,1,0:T(8,128)S(1)}, f32[4,16,1536]{2,1,0:T(8,128)S(1)}) custom-call(s32[3]{0:T(128)S(1)} %pad_add_fusion.1.place, s32[2,2,16]{2,1,0:T(2,128)S(1)} %pad_add_fusion.maps, f32[4,16,1024]{2,1,0:T(8,128)S(1)} %collective-permute-done.10.far, f32[32,16,128]{2,1,0:T(8,128)S(1)} %shard_map.79.start, f32[128,4096]{1,0:T(8,128)S(1)} %copy-done.3), custom_call_target="tpu_custom_call" | custom-call | flops 33554432 | bytes 2097152 | tf_op jit(solution)/shard_map/pallas_call | solution.py:266
  41.6 0.2 collective-permute-start.11
  41.8 1.6 %collective-permute-done.11 = f32[4,16,1536]{2,1,0:T(8,128)S(1)} collective-permute-done((f32[4,16,1536]{2,1,0:T(8,128)S(1)}, f32[4,16,1536]{2,1,0:T(8,128)S(1)}, u32[]{:S(2)}, u32[]{:S(2)}) %collective-permute-start.11) | collective-permute-done | bytes 393248 | tf_op jit(solution)/shard_map/ppermute | solution.py:165
  43.5 0.6 collective-permute-start.12
  44.0 0.8 collective-permute-start.13
  44.8 2.2 %collective-permute-start.14 = (f32[16,1536]{1,0:T(8,128)S(1)}, f32[16,1536]{1,0:T(8,128)S(1)}, u32[]{:S(2)}, u32[]{:S(2)}) collective-permute-start(f32[16,1536]{1,0:T(8,128)S(1)} %get-tuple-element.33), channel_id=1, source_target_pairs={{0,18},{1,19},{2,16},{3,17},{16,2},{17,3},{18,0},{19,1},{4,22},{5,... | collective-permute-start | bytes 294920 | tf_op jit(solution)/shard_map/ppermute | solution.py:165
  47.0 1.3 %collective-permute-done.12 = f32[16,1536]{1,0:T(8,128)S(1)} collective-permute-done((f32[16,1536]{1,0:T(8,128)S(1)}, f32[16,1536]{1,0:T(8,128)S(1)}, u32[]{:S(2)}, u32[]{:S(2)}) %collective-permute-start.12) | collective-permute-done | bytes 98336 | tf_op jit(solution)/shard_map/ppermute | solution.py:165
  48.4 1.2 %collective-permute-done.13 = f32[16,1536]{1,0:T(8,128)S(1)} collective-permute-done((f32[16,1536]{1,0:T(8,128)S(1)}, f32[16,1536]{1,0:T(8,128)S(1)}, u32[]{:S(2)}, u32[]{:S(2)}) %collective-permute-start.13) | collective-permute-done | bytes 98336 | tf_op jit(solution)/shard_map/ppermute | solution.py:165
  49.6 2.0 %collective-permute-done.14 = f32[16,1536]{1,0:T(8,128)S(1)} collective-permute-done((f32[16,1536]{1,0:T(8,128)S(1)}, f32[16,1536]{1,0:T(8,128)S(1)}, u32[]{:S(2)}, u32[]{:S(2)}) %collective-permute-start.14) | collective-permute-done | bytes 98336 | tf_op jit(solution)/shard_map/ppermute | solution.py:165
  51.7 0.9 %collective-permute-start.15 = (f32[16,1024]{1,0:T(8,128)S(1)}, f32[16,1024]{1,0:T(8,128)S(1)}, u32[]{:S(2)}, u32[]{:S(2)}) collective-permute-start(f32[16,1024]{1,0:T(8,128)S(1)} %slice.28), channel_id=1, source_target_pairs={{0,4},{4,0},{8,12},{12,8},{1,5},{5,1},{9,13},{13,9},{2,6},{6,2},{1... | collective-permute-start | bytes 196616 | tf_op jit(solution)/shard_map/ppermute | solution.py:165
  52.6 1.7 %collective-permute-start.16 = (f32[16,1024]{1,0:T(8,128)S(1)}, f32[16,1024]{1,0:T(8,128)S(1)}, u32[]{:S(2)}, u32[]{:S(2)}) collective-permute-start(f32[16,1024]{1,0:T(8,128)S(1)} %slice.28), channel_id=1, source_target_pairs={{0,8},{4,12},{8,0},{12,4},{1,9},{5,13},{9,1},{13,5},{2,10},{6,14},... | collective-permute-start | bytes 196616 | tf_op jit(solution)/shard_map/ppermute | solution.py:165
  54.3 1.8 %collective-permute-start.17 = (f32[16,1024]{1,0:T(8,128)S(1)}, f32[16,1024]{1,0:T(8,128)S(1)}, u32[]{:S(2)}, u32[]{:S(2)}) collective-permute-start(f32[16,1024]{1,0:T(8,128)S(1)} %slice.28), channel_id=1, source_target_pairs={{0,12},{4,8},{8,4},{12,0},{1,13},{5,9},{9,5},{13,1},{2,14},{6,10},... | collective-permute-start | bytes 196616 | tf_op jit(solution)/shard_map/ppermute | solution.py:165
  56.2 2.9 %collective-permute-done.16 = f32[16,1024]{1,0:T(8,128)S(1)} collective-permute-done((f32[16,1024]{1,0:T(8,128)S(1)}, f32[16,1024]{1,0:T(8,128)S(1)}, u32[]{:S(2)}, u32[]{:S(2)}) %collective-permute-start.16) | collective-permute-done | bytes 65568 | tf_op jit(solution)/shard_map/ppermute | solution.py:165
  59.1 1.4 %collective-permute-done.17 = f32[16,1024]{1,0:T(8,128)S(1)} collective-permute-done((f32[16,1024]{1,0:T(8,128)S(1)}, f32[16,1024]{1,0:T(8,128)S(1)}, u32[]{:S(2)}, u32[]{:S(2)}) %collective-permute-start.17) | collective-permute-done | bytes 65568 | tf_op jit(solution)/shard_map/ppermute | solution.py:165
  60.5 1.5 %shard_map.81 = (f32[1,16,1024]{2,1,0:T(8,128)S(1)}, f32[1,16,1024]{2,1,0:T(8,128)S(1)}) custom-call(s32[3]{0:T(128)S(1)} %pad_add_fusion.1.place, f32[16,1024]{1,0:T(8,128)S(1)} %add_add_fusion.pulled, f32[2,512,1024]{2,1,0:T(8,128)S(1)} %copy-done.2), custom_call_target="tpu_custom_call" | custom-call | flops 33554432 | bytes 4194304 | tf_op jit(solution)/shard_map/pallas_call | solution.py:286
  62.0 1.3 %collective-permute-done.18 = f32[1,16,1024]{2,1,0:T(8,128)S(1)} collective-permute-done((f32[1,16,1024]{2,1,0:T(8,128)S(1)}, f32[1,16,1024]{2,1,0:T(8,128)S(1)}, u32[]{:S(2)}, u32[]{:S(2)}) %collective-permute-start.18) | collective-permute-done | bytes 65568 | tf_op jit(solution)/shard_map/ppermute | solution.py:165
  63.3 0.7 collective-permute-start.19
  63.9 3.7 %collective-permute-done.19 = f32[1,16,1024]{2,1,0:T(8,128)S(1)} collective-permute-done((f32[1,16,1024]{2,1,0:T(8,128)S(1)}, f32[1,16,1024]{2,1,0:T(8,128)S(1)}, u32[]{:S(2)}, u32[]{:S(2)}) %collective-permute-start.19) | collective-permute-done | bytes 65568 | tf_op jit(solution)/shard_map/ppermute | solution.py:165
  67.7 1.2 %collective-permute-done.20.pull_other = f32[1,16,1024]{2,1,0:T(8,128)S(1)} collective-permute-done((f32[1,16,1024]{2,1,0:T(8,128)S(1)}, f32[1,16,1024]{2,1,0:T(8,128)S(1)}, u32[]{:S(2)}, u32[]{:S(2)}) %collective-permute-start.20) | collective-permute-done | bytes 65568 | tf_op jit(solution)/shard_map/ppermute | solution.py:165
  68.9 3.4 %copy-done = f32[2,1024,1024]{2,1,0:T(8,128)S(1)} copy-done((f32[2,1024,1024]{2,1,0:T(8,128)S(1)}, f32[2,1024,1024]{2,1,0:T(8,128)}, u32[]{:S(2)}) %copy-start) | copy-done | bytes 8388632
  72.3 2.1 %shard_map.82 = f32[2,16,1024]{2,1,0:T(8,128)S(1)} custom-call(s32[3]{0:T(128)S(1)} %pad_add_fusion.1.place, f32[1,16,1024]{2,1,0:T(8,128)S(1)} %add.87.mine, f32[1,16,1024]{2,1,0:T(8,128)S(1)} %collective-permute-done.2.other, f32[1,16,1024]{2,1,0:T(8,128)S(1)} %add.99.pull_mine, f32[1,16,1024]{2,1,0:T(8,128)S(1)} %collective-permute-done.20.pull_other, ...), custom_call_target="tpu_custom_call" | custom-call | flops 67108864 | bytes 8388608 | tf_op jit(solution)/shard_map/pallas_call | solution.py:291
  74.5 1.9 %collective-permute-start.23 = (f32[16,640]{1,0:T(8,128)S(1)}, f32[16,640]{1,0:T(8,128)S(1)}, u32[]{:S(2)}, u32[]{:S(2)}) collective-permute-start(f32[16,640]{1,0:T(8,128)S(1)} %pad_maximum_fusion.4), channel_id=1, source_target_pairs={{0,12},{4,8},{8,4},{12,0},{1,13},{5,9},{9,5},{13,1},{2,14},{6,10},... | collective-permute-start | bytes 122888 | tf_op jit(solution)/shard_map/ppermute | solution.py:165
  76.4 2.5 %collective-permute-start.21 = (f32[16,640]{1,0:T(8,128)S(1)}, f32[16,640]{1,0:T(8,128)S(1)}, u32[]{:S(2)}, u32[]{:S(2)}) collective-permute-start(f32[16,640]{1,0:T(8,128)S(1)} %pad_maximum_fusion.2), channel_id=1, source_target_pairs={{0,4},{4,0},{8,12},{12,8},{1,5},{5,1},{9,13},{13,9},{2,6},{6,2},{1... | collective-permute-start | bytes 122888 | tf_op jit(solution)/shard_map/ppermute | solution.py:165
  78.9 1.5 %collective-permute-done.23.refs_3_ = f32[16,640]{1,0:T(8,128)S(1)} collective-permute-done((f32[16,640]{1,0:T(8,128)S(1)}, f32[16,640]{1,0:T(8,128)S(1)}, u32[]{:S(2)}, u32[]{:S(2)}) %collective-permute-start.23) | collective-permute-done | bytes 40992 | tf_op jit(solution)/shard_map/ppermute | solution.py:165
  80.5 1.2 %collective-permute-done.22.refs_2_ = f32[16,640]{1,0:T(8,128)S(1)} collective-permute-done((f32[16,640]{1,0:T(8,128)S(1)}, f32[16,640]{1,0:T(8,128)S(1)}, u32[]{:S(2)}, u32[]{:S(2)}) %collective-permute-start.22) | collective-permute-done | bytes 40992 | tf_op jit(solution)/shard_map/ppermute | solution.py:165
  81.7 0.6 shard_map.83
  (41 shorter events, 0.6 us)
Async XLA Ops:
  0.6 10.2 %copy-start.5 = (s32[2,16]{1,0:T(2,128)S(1)}, s32[2,16]{1,0:T(2,128)}, u32[]{:S(2)}) copy-start(s32[2,16]{1,0:T(2,128)} %param.9) | copy-start | bytes 388
  0.7 38.5 %copy-start.3 = (f32[128,4096]{1,0:T(8,128)S(1)}, f32[128,4096]{1,0:T(8,128)}, u32[]{:S(2)}) copy-start(f32[128,4096]{1,0:T(8,128)} %sep) | copy-start | bytes 6291460
  6.4 31.3 %copy-start.4 = (f32[16,4096]{1,0:T(8,128)S(1)}, f32[16,4096]{1,0:T(8,128)}, u32[]{:S(2)}) copy-start(f32[16,4096]{1,0:T(8,128)} %rhs.2) | copy-start | bytes 786436
  6.4 1.4 %collective-permute-start = (f32[1,16,1024]{2,1,0:T(8,128)S(1)}, f32[1,16,1024]{2,1,0:T(8,128)S(1)}, u32[]{:S(2)}, u32[]{:S(2)}) collective-permute-start(f32[1,16,1024]{2,1,0:T(8,128)S(1)} %constant_dynamic-slice_fusion.4), channel_id=1, source_target_pairs={{0,1},{1,0},{2,3},{3,2},{4,5},{5,4},{6,7},{7,6},{8,9},{9,8},{10,11... | collective-permute-start | bytes 196616 | tf_op jit(solution)/shard_map/ppermute | solution.py:165
  7.9 5.3 %collective-permute-start.1 = (f32[1,16,1024]{2,1,0:T(8,128)S(1)}, f32[1,16,1024]{2,1,0:T(8,128)S(1)}, u32[]{:S(2)}, u32[]{:S(2)}) collective-permute-start(f32[1,16,1024]{2,1,0:T(8,128)S(1)} %dynamic-slice_add_fusion), channel_id=1, source_target_pairs={{0,2},{1,3},{2,0},{3,1},{4,6},{5,7},{6,4},{7,5},{8,10},{9,11},{10,... | collective-permute-start | bytes 196616 | tf_op jit(solution)/shard_map/ppermute | solution.py:165
  10.8 3.6 %collective-permute-start.3 = (s32[2,16]{1,0:T(2,128)S(1)}, s32[2,16]{1,0:T(2,128)S(1)}, u32[]{:S(2)}, u32[]{:S(2)}) collective-permute-start(s32[2,16]{1,0:T(2,128)S(1)} %copy-done.5), channel_id=1, source_target_pairs={{0,16},{16,0},{1,17},{17,1},{2,18},{18,2},{3,19},{19,3},{4,20},{20... | collective-permute-start | bytes 392 | tf_op jit(solution)/shard_map/ppermute | solution.py:165
  13.2 1.3 %collective-permute-start.2 = (f32[1,16,1024]{2,1,0:T(8,128)S(1)}, f32[1,16,1024]{2,1,0:T(8,128)S(1)}, u32[]{:S(2)}, u32[]{:S(2)}) collective-permute-start(f32[1,16,1024]{2,1,0:T(8,128)S(1)} %add.87.mine), channel_id=1, source_target_pairs={{0,1},{1,0},{2,3},{3,2},{4,5},{5,4},{6,7},{7,6},{8,9},{9,8},{10,11... | collective-permute-start | bytes 196616 | tf_op jit(solution)/shard_map/ppermute | solution.py:165
  14.6 2.2 %copy-start.1 = (f32[2,512,1024]{2,1,0:T(8,128)S(1)}, f32[2,512,1024]{2,1,0:T(8,128)}, u32[]{:S(2)}) copy-start(f32[2,512,1024]{2,1,0:T(8,128)} %update.1) | copy-start | bytes 12582916
  18.6 41.9 %copy-start.2 = (f32[2,512,1024]{2,1,0:T(8,128)S(1)}, f32[2,512,1024]{2,1,0:T(8,128)}, u32[]{:S(2)}) copy-start(f32[2,512,1024]{2,1,0:T(8,128)} %update.1) | copy-start | bytes 12582916
  18.6 4.5 %collective-permute-start.4 = (f32[16,1024]{1,0:T(8,128)S(1)}, f32[16,1024]{1,0:T(8,128)S(1)}, u32[]{:S(2)}, u32[]{:S(2)}) collective-permute-start(f32[16,1024]{1,0:T(8,128)S(1)} %shard_map.78), channel_id=1, source_target_pairs={{0,4},{4,0},{8,12},{12,8},{1,5},{5,1},{9,13},{13,9},{2,6},{6,2},{1... | collective-permute-start | bytes 196616 | tf_op jit(solution)/shard_map/ppermute | solution.py:165
  20.6 7.5 %collective-permute-start.5 = (f32[16,1024]{1,0:T(8,128)S(1)}, f32[16,1024]{1,0:T(8,128)S(1)}, u32[]{:S(2)}, u32[]{:S(2)}) collective-permute-start(f32[16,1024]{1,0:T(8,128)S(1)} %shard_map.78), channel_id=1, source_target_pairs={{0,8},{4,12},{8,0},{12,4},{1,9},{5,13},{9,1},{13,5},{2,10},{6,14},... | collective-permute-start | bytes 196616 | tf_op jit(solution)/shard_map/ppermute | solution.py:165
  23.1 6.2 %collective-permute-start.6 = (f32[16,1024]{1,0:T(8,128)S(1)}, f32[16,1024]{1,0:T(8,128)S(1)}, u32[]{:S(2)}, u32[]{:S(2)}) collective-permute-start(f32[16,1024]{1,0:T(8,128)S(1)} %shard_map.78), channel_id=1, source_target_pairs={{0,12},{4,8},{8,4},{12,0},{1,13},{5,9},{9,5},{13,1},{2,14},{6,10},... | collective-permute-start | bytes 196616 | tf_op jit(solution)/shard_map/ppermute | solution.py:165
  29.3 4.3 %collective-permute-start.7 = (f32[16,1024]{1,0:T(8,128)S(1)}, f32[16,1024]{1,0:T(8,128)S(1)}, u32[]{:S(2)}, u32[]{:S(2)}) collective-permute-start(f32[16,1024]{1,0:T(8,128)S(1)} %add_add_fusion.1), channel_id=1, source_target_pairs={{0,2},{1,3},{2,0},{3,1},{16,18},{17,19},{18,16},{19,17},{4,6},{5,7... | collective-permute-start | bytes 196616 | tf_op jit(solution)/shard_map/ppermute | solution.py:165
  30.9 4.3 %collective-permute-start.8 = (f32[16,1024]{1,0:T(8,128)S(1)}, f32[16,1024]{1,0:T(8,128)S(1)}, u32[]{:S(2)}, u32[]{:S(2)}) collective-permute-start(f32[16,1024]{1,0:T(8,128)S(1)} %add_add_fusion.1), channel_id=1, source_target_pairs={{0,16},{1,17},{2,18},{3,19},{16,0},{17,1},{18,2},{19,3},{4,20},{5,... | collective-permute-start | bytes 196616 | tf_op jit(solution)/shard_map/ppermute | solution.py:165
  32.4 5.2 %collective-permute-start.9 = (f32[16,1024]{1,0:T(8,128)S(1)}, f32[16,1024]{1,0:T(8,128)S(1)}, u32[]{:S(2)}, u32[]{:S(2)}) collective-permute-start(f32[16,1024]{1,0:T(8,128)S(1)} %add_add_fusion.1), channel_id=1, source_target_pairs={{0,18},{1,19},{2,16},{3,17},{16,2},{17,3},{18,0},{19,1},{4,22},{5,... | collective-permute-start | bytes 196616 | tf_op jit(solution)/shard_map/ppermute | solution.py:165
  37.6 1.6 %collective-permute-start.10 = (f32[4,16,1024]{2,1,0:T(8,128)S(1)}, f32[4,16,1024]{2,1,0:T(8,128)S(1)}, u32[]{:S(2)}, u32[]{:S(2)}) collective-permute-start(f32[4,16,1024]{2,1,0:T(8,128)S(1)} %pad_maximum_fusion.near), channel_id=1, source_target_pairs={{0,1},{1,0},{2,3},{3,2},{4,5},{5,4},{6,7},{7,6},{8,9},{9,8},{10,11... | collective-permute-start | bytes 786440 | tf_op jit(solution)/shard_map/ppermute | solution.py:165
  41.6 1.8 %collective-permute-start.11 = (f32[4,16,1536]{2,1,0:T(8,128)S(1)}, f32[4,16,1536]{2,1,0:T(8,128)S(1)}, u32[]{:S(2)}, u32[]{:S(2)}) collective-permute-start(f32[4,16,1536]{2,1,0:T(8,128)S(1)} %get-tuple-element.28), channel_id=1, source_target_pairs={{0,1},{1,0},{2,3},{3,2},{4,5},{5,4},{6,7},{7,6},{8,9},{9,8},{10,11... | collective-permute-start | bytes 1179656 | tf_op jit(solution)/shard_map/ppermute | solution.py:165
  43.5 4.9 %collective-permute-start.12 = (f32[16,1536]{1,0:T(8,128)S(1)}, f32[16,1536]{1,0:T(8,128)S(1)}, u32[]{:S(2)}, u32[]{:S(2)}) collective-permute-start(f32[16,1536]{1,0:T(8,128)S(1)} %get-tuple-element.34), channel_id=1, source_target_pairs={{0,2},{1,3},{2,0},{3,1},{16,18},{17,19},{18,16},{19,17},{4,6},{5,7... | collective-permute-start | bytes 294920 | tf_op jit(solution)/shard_map/ppermute | solution.py:165
  44.0 5.6 %collective-permute-start.13 = (f32[16,1536]{1,0:T(8,128)S(1)}, f32[16,1536]{1,0:T(8,128)S(1)}, u32[]{:S(2)}, u32[]{:S(2)}) collective-permute-start(f32[16,1536]{1,0:T(8,128)S(1)} %get-tuple-element.32), channel_id=1, source_target_pairs={{0,16},{1,17},{2,18},{3,19},{16,0},{17,1},{18,2},{19,3},{4,20},{5,... | collective-permute-start | bytes 294920 | tf_op jit(solution)/shard_map/ppermute | solution.py:165
  44.8 6.9 %collective-permute-start.14 = (f32[16,1536]{1,0:T(8,128)S(1)}, f32[16,1536]{1,0:T(8,128)S(1)}, u32[]{:S(2)}, u32[]{:S(2)}) collective-permute-start(f32[16,1536]{1,0:T(8,128)S(1)} %get-tuple-element.33), channel_id=1, source_target_pairs={{0,18},{1,19},{2,16},{3,17},{16,2},{17,3},{18,0},{19,1},{4,22},{5,... | collective-permute-start | bytes 294920 | tf_op jit(solution)/shard_map/ppermute | solution.py:165
  51.7 4.5 %collective-permute-start.15 = (f32[16,1024]{1,0:T(8,128)S(1)}, f32[16,1024]{1,0:T(8,128)S(1)}, u32[]{:S(2)}, u32[]{:S(2)}) collective-permute-start(f32[16,1024]{1,0:T(8,128)S(1)} %slice.28), channel_id=1, source_target_pairs={{0,4},{4,0},{8,12},{12,8},{1,5},{5,1},{9,13},{13,9},{2,6},{6,2},{1... | collective-permute-start | bytes 196616 | tf_op jit(solution)/shard_map/ppermute | solution.py:165
  52.6 6.5 %collective-permute-start.16 = (f32[16,1024]{1,0:T(8,128)S(1)}, f32[16,1024]{1,0:T(8,128)S(1)}, u32[]{:S(2)}, u32[]{:S(2)}) collective-permute-start(f32[16,1024]{1,0:T(8,128)S(1)} %slice.28), channel_id=1, source_target_pairs={{0,8},{4,12},{8,0},{12,4},{1,9},{5,13},{9,1},{13,5},{2,10},{6,14},... | collective-permute-start | bytes 196616 | tf_op jit(solution)/shard_map/ppermute | solution.py:165
  54.3 6.1 %collective-permute-start.17 = (f32[16,1024]{1,0:T(8,128)S(1)}, f32[16,1024]{1,0:T(8,128)S(1)}, u32[]{:S(2)}, u32[]{:S(2)}) collective-permute-start(f32[16,1024]{1,0:T(8,128)S(1)} %slice.28), channel_id=1, source_target_pairs={{0,12},{4,8},{8,4},{12,0},{1,13},{5,9},{9,5},{13,1},{2,14},{6,10},... | collective-permute-start | bytes 196616 | tf_op jit(solution)/shard_map/ppermute | solution.py:165
  62.0 1.3 %collective-permute-start.18 = (f32[1,16,1024]{2,1,0:T(8,128)S(1)}, f32[1,16,1024]{2,1,0:T(8,128)S(1)}, u32[]{:S(2)}, u32[]{:S(2)}) collective-permute-start(f32[1,16,1024]{2,1,0:T(8,128)S(1)} %get-tuple-element.30), channel_id=1, source_target_pairs={{0,1},{1,0},{2,3},{3,2},{4,5},{5,4},{6,7},{7,6},{8,9},{9,8},{10,11... | collective-permute-start | bytes 196616 | tf_op jit(solution)/shard_map/ppermute | solution.py:165
  63.3 4.3 %collective-permute-start.19 = (f32[1,16,1024]{2,1,0:T(8,128)S(1)}, f32[1,16,1024]{2,1,0:T(8,128)S(1)}, u32[]{:S(2)}, u32[]{:S(2)}) collective-permute-start(f32[1,16,1024]{2,1,0:T(8,128)S(1)} %add.98), channel_id=1, source_target_pairs={{0,2},{1,3},{2,0},{3,1},{4,6},{5,7},{6,4},{7,5},{8,10},{9,11},{10,... | collective-permute-start | bytes 196616 | tf_op jit(solution)/shard_map/ppermute | solution.py:165
  67.6 1.3 %collective-permute-start.20 = (f32[1,16,1024]{2,1,0:T(8,128)S(1)}, f32[1,16,1024]{2,1,0:T(8,128)S(1)}, u32[]{:S(2)}, u32[]{:S(2)}) collective-permute-start(f32[1,16,1024]{2,1,0:T(8,128)S(1)} %add.99.pull_mine), channel_id=1, source_target_pairs={{0,1},{1,0},{2,3},{3,2},{4,5},{5,4},{6,7},{7,6},{8,9},{9,8},{10,11... | collective-permute-start | bytes 196616 | tf_op jit(solution)/shard_map/ppermute | solution.py:165
  68.9 3.4 %copy-start = (f32[2,1024,1024]{2,1,0:T(8,128)S(1)}, f32[2,1024,1024]{2,1,0:T(8,128)}, u32[]{:S(2)}) copy-start(f32[2,1024,1024]{2,1,0:T(8,128)} %inverse.2) | copy-start | bytes 25165828
  74.5 6.0 %collective-permute-start.23 = (f32[16,640]{1,0:T(8,128)S(1)}, f32[16,640]{1,0:T(8,128)S(1)}, u32[]{:S(2)}, u32[]{:S(2)}) collective-permute-start(f32[16,640]{1,0:T(8,128)S(1)} %pad_maximum_fusion.4), channel_id=1, source_target_pairs={{0,12},{4,8},{8,4},{12,0},{1,13},{5,9},{9,5},{13,1},{2,14},{6,10},... | collective-permute-start | bytes 122888 | tf_op jit(solution)/shard_map/ppermute | solution.py:165
  76.4 5.3 %collective-permute-start.22 = (f32[16,640]{1,0:T(8,128)S(1)}, f32[16,640]{1,0:T(8,128)S(1)}, u32[]{:S(2)}, u32[]{:S(2)}) collective-permute-start(f32[16,640]{1,0:T(8,128)S(1)} %pad_maximum_fusion.3), channel_id=1, source_target_pairs={{0,8},{4,12},{8,0},{12,4},{1,9},{5,13},{9,1},{13,5},{2,10},{6,14},... | collective-permute-start | bytes 122888 | tf_op jit(solution)/shard_map/ppermute | solution.py:165
  76.4 5.3 %collective-permute-start.21 = (f32[16,640]{1,0:T(8,128)S(1)}, f32[16,640]{1,0:T(8,128)S(1)}, u32[]{:S(2)}, u32[]{:S(2)}) collective-permute-start(f32[16,640]{1,0:T(8,128)S(1)} %pad_maximum_fusion.2), channel_id=1, source_target_pairs={{0,4},{4,0},{8,12},{12,8},{1,5},{5,1},{9,13},{13,9},{2,6},{6,2},{1... | collective-permute-start | bytes 122888 | tf_op jit(solution)/shard_map/ppermute | solution.py:165

commit v3 on v2

v3 whole, which is shorter than its diff:
```python
import functools

import jax
import jax.numpy as jnp
from jax import lax
from jax.experimental import pallas as pl
from jax.experimental.pallas import tpu as pltpu
from jax.sharding import PartitionSpec as P

BLOCK = 128
CORES = 2
MIB = 1 << 20

F32, BF16 = jnp.float32, jnp.bfloat16
HBM = pl.BlockSpec(memory_space=pltpu.HBM)
WHOLE = pl.BlockSpec(memory_space=pltpu.VMEM)


def in_hbm(value):
    return pltpu.with_memory_space_constraint(value, pltpu.HBM)


def in_vmem(value):
    return pltpu.with_memory_space_constraint(value, pltpu.VMEM)


def split(value):
    high = value.astype(BF16)
    return high, (value - high.astype(F32)).astype(BF16)


def dot3(value, halves, dims):
    rows = value.shape[0]
    high, low = halves
    parts = jnp.concatenate(split(value))
    main = lax.dot_general(parts, high, dims, preferred_element_type=F32)
    rest = lax.dot_general(parts[:rows], low, dims, preferred_element_type=F32)
    return main[:rows] + (main[rows:] + rest)


ROWS_OF = (((1,), (1,)), ((), ()))
COLUMNS_OF = (((1,), (0,)), ((), ()))


def sub_of(slot, half, core):
    return core * half + slot if slot < half else (1 - core) * half + (slot - half)


def chunk_of(rows):
    return min(rows, 512)


def leaf_kernel(rhs, inverse, mine, other, held, land, sems, rhs_sem):
    subs, rows, _ = inverse.shape
    half = subs // CORES
    core = lax.axis_index("col") % CORES
    chunk = chunk_of(rows)
    steps = rows // chunk
    order = [*range(half, subs), *range(half)]

    def fetch(slot, step):
        part = pl.ds(step * chunk, chunk)
        return pltpu.make_async_copy(
            inverse.at[sub_of(slot, half, core), part], land.at[slot, part], sems.at[slot * steps + step]
        )

    first = pltpu.make_async_copy(rhs, held, rhs_sem)
    first.start()
    for slot in order:
        for step in range(steps):
            fetch(slot, step).start()
    first.wait()
    for slot in order:
        out, at = (mine, slot) if slot < half else (other, slot - half)
        value = held[sub_of(slot, half, core)]
        for step in range(steps):
            part = pl.ds(step * chunk, chunk)
            fetch(slot, step).wait()
            out[at, :, part] = dot3(value, split(land[slot, part]), ROWS_OF)


def couple_kernel(first, vectors, update, out):
    subs, up, _ = update.shape
    core = lax.axis_index("col") % CORES
    for i in range(vectors.shape[0]):
        matrix = update[sub_of(first + i, subs // CORES, core)]
        out[:, i * up : (i + 1) * up] = dot3(vectors[i], split(matrix), ROWS_OF)


def load_kernel(value, out, sems):
    count = sems.shape[0]
    step = value.shape[0] // count
    copies = [
        pltpu.make_async_copy(
            value.at[pl.ds(i * step, step)], out.at[pl.ds(i * step, step)], sems.at[i]
        )
        for i in range(count)
    ]
    for copy in copies:
        copy.start()
    for copy in copies:
        copy.wait()


def numbers_of(pieces, numbers, sems):
    _, subs, _ = numbers.shape
    at = pieces.shape[2] - BLOCK
    return [
        pltpu.make_async_copy(
            pieces.at[chip, pl.ds(0, subs), pl.ds(at, BLOCK)], numbers.at[chip], sems.at[chip]
        )
        for chip in range(pieces.shape[0])
    ]


def spots(lines, side, numbers, length):
    chips, subs, _ = numbers.shape
    here = length // (subs * BLOCK)
    col = lax.axis_index("col")
    core = (col + side) % CORES
    for chip in range(chips):
        first = ((col // CORES ^ (chip % lines)) * CORES + core) * here
        for slot in range(subs):
            sub = sub_of(slot, subs // CORES, core)
            for k in range(here):
                at = (slot * here + k) * BLOCK
                block = numbers[chip, sub, first + k].astype(jnp.int32)
                yield chip, slice(at, at + BLOCK), block


def scatter_kernel(lines, near, rhs, out, numbers, sems):
    copies = numbers_of(near, numbers, sems)
    for copy in copies:
        copy.start()
    for b in range(out.shape[0]):
        out[b] = rhs[:, b * BLOCK : (b + 1) * BLOCK]
    for copy in copies:
        copy.wait()
    for chip, lanes, block in spots(lines, 0, numbers, near.shape[2] - BLOCK):
        out[block] -= near[chip, :, lanes]


def separator_kernel(sizes, inside, near, far, start, sep, keep, send, *rest):
    leaves, rows, cols, lines = sizes
    *back, held, high, low, ours, theirs, our_sems, their_sems = rest
    chips = far.shape[0]
    total = held.shape[0]
    length = far.shape[2] - BLOCK

    copies = numbers_of(far, theirs, their_sems) + numbers_of(near, ours, our_sems)
    for copy in copies:
        copy.start()
    held[...] = start[...]
    high[...], low[...] = split(sep[...])
    for copy in copies:
        copy.wait()
    for chip, lanes, block in spots(lines, 1, theirs, length):
        held[block] -= far[chip, :, lanes]
    updated = jnp.concatenate([held[b] for b in range(total)], 1)
    forward = dot3(updated, (high[...], low[...]), ROWS_OF)
    terms = dot3(forward, (high[...], low[...]), COLUMNS_OF)
    for b in range(total):
        held[b] = terms[:, b * BLOCK : (b + 1) * BLOCK]
    for side, numbers, out in ((1, theirs, send), (0, ours, keep)):
        for chip, lanes, block in spots(lines, side, numbers, length):
            out[chip, :, lanes] = held[block]
    if not inside:
        back[0][...] = terms
        return
    wide = sep.shape[0] // BLOCK
    me = lax.axis_index("col")
    plane = lax.axis_index("leaf") * lines + me // CORES
    for side, out in ((1, send), (0, keep)):
        for chip in range(chips):
            other = plane ^ chip
            col = (other % lines) * CORES + (me + side) % CORES
            for row in range(rows):
                for w in range(wide):
                    block = ((other // lines * rows + row) * cols + col) * wide + w
                    at = length + (row * wide + w) * BLOCK
                    out[chip, :, at : at + BLOCK] = held[block]


def pull_kernel(first, pulled, update, out):
    subs, up, _ = update.shape
    core = lax.axis_index("col") % CORES
    for i in range(out.shape[0]):
        slot = first + i
        value = pulled[:, slot * up : (slot + 1) * up]
        matrix = update[sub_of(slot, subs // CORES, core)]
        out[i] = dot3(value, split(matrix), COLUMNS_OF)


def reduced_of(mine, other, pull_mine, pull_other):
    half = mine.shape[0]
    core = lax.axis_index("col") % CORES
    for slot in range(2 * half):
        if slot < half:
            value = mine[slot] - pull_mine[slot]
        else:
            value = other[slot - half] - pull_other[slot - half]
        yield slot, sub_of(slot, half, core), value


def solve_kernel(mine, other, pull_mine, pull_other, inverse, out):
    for _, sub, value in reduced_of(mine, other, pull_mine, pull_other):
        out[sub] = dot3(value, split(inverse[sub]), COLUMNS_OF)


def solve_parts_kernel(rows, masks, mine, other, pull_mine, pull_other, own, inverse, *outs):
    subs, _, width = inverse.shape
    share = width // rows
    sep_rows = own.shape[1] // rows
    row = lax.axis_index("row")
    for slot, sub, value in reduced_of(mine, other, pull_mine, pull_other):
        for mask, out in zip(masks, outs, strict=True):
            columns = pl.ds(pl.multiple_of((row ^ mask) * share, share), share)
            terms = dot3(value, split(inverse[sub, :, columns]), COLUMNS_OF)
            out[:, slot * share : (slot + 1) * share] = terms
    for mask, out in zip(masks, outs, strict=True):
        columns = pl.ds(pl.multiple_of((row ^ mask) * sep_rows, sep_rows), sep_rows)
        out[:, subs * share :] = own[:, columns]


def finish_kernel(*refs):
    *parts, leaf_out, sep_out = refs
    subs, _, share = leaf_out.shape
    core = lax.axis_index("col") % CORES
    done = parts[0][...]
    for part in parts[1:]:
        done = done + part[...]
    for slot in range(subs):
        leaf_out[sub_of(slot, subs // CORES, core)] = done[:, slot * share : (slot + 1) * share]
    sep_out[...] = done[:, subs * share :]


def swap(value, axes, size, mask):
    return lax.ppermute(value, axes, [(i, i ^ mask) for i in range(size)])


def picked(value, dim, index, count):
    return jnp.stack(
        [lax.dynamic_index_in_dim(value, index ^ m, dim, keepdims=False) for m in range(count)], dim
    )


def beside(arrived, value):
    value = pl.pallas_call(
        load_kernel,
        out_shape=pltpu.VMEM(value.shape, value.dtype),
        in_specs=[HBM],
        out_specs=pl.BlockSpec(memory_space=pl.ANY),
        scratch_shapes=[pltpu.SemaphoreType.DMA((value.shape[0],))],
        compiler_params=pltpu.CompilerParams(vmem_limit_bytes=MIB),
        cost_estimate=pl.CostEstimate(flops=0, bytes_accessed=4 * value.size, transcendentals=0),
    )(in_hbm(value))
    return lax.optimization_barrier((arrived, value))


def sum_over_lines(mine, cols, arrived=None):
    step = CORES
    while step < cols:
        first = arrived is not None and step == CORES
        mine = mine + (arrived if first else swap(mine, "col", cols, step))
        step *= 2
    return mine, swap(mine, "col", cols, 1)


def call(kernel, out_shape, in_specs, limit, cost, scratch=()):
    flops, nbytes = cost
    return pl.pallas_call(
        kernel,
        out_shape=out_shape,
        in_specs=in_specs,
        scratch_shapes=scratch,
        compiler_params=pltpu.CompilerParams(vmem_limit_bytes=limit * MIB),
        cost_estimate=pl.CostEstimate(flops=flops, bytes_accessed=nbytes, transcendentals=0),
    )


def body(sizes, leaf_rhs, leaf_inverse, update_rows, update_map, sep_rhs, sep_inverse):
    leaves, rows, cols = sizes
    lines = cols // CORES
    chips = leaves * lines
    subs, nrhs, _ = leaf_rhs.shape
    half = subs // CORES
    width = sep_rhs.shape[1]
    sep_rows = sep_inverse.shape[0]
    _, leaf_rows, leaf_cols = leaf_inverse.shape
    up = update_rows.shape[1]
    leaf, row, col = (lax.axis_index(a) for a in ("leaf", "row", "col"))
    core, line = col % CORES, col // CORES
    plane = leaf * lines + line
    plane_axes, plane_size = ("leaf", "col"), leaves * cols

    vec = jax.ShapeDtypeStruct((half, nrhs, leaf_rows), F32)
    leaf_flops = 2 * nrhs * leaf_inverse.size
    mine, other = call(
        leaf_kernel,
        (pltpu.VMEM(vec.shape, F32), pltpu.VMEM(vec.shape, F32)),
        [HBM, HBM],
        61,
        (leaf_flops, 4 * leaf_inverse.size),
        (
            pltpu.VMEM(leaf_rhs.shape, F32),
            pltpu.VMEM(leaf_inverse.shape, F32),
            pltpu.SemaphoreType.DMA((subs * (leaf_rows // chunk_of(leaf_rows)),)),
            pltpu.SemaphoreType.DMA,
        ),
    )(in_hbm(leaf_rhs), in_hbm(leaf_inverse))

    mine = mine + swap(other, "col", cols, 1)
    arrived, update = beside(swap(mine, "col", cols, CORES), update_rows)
    mine, other = sum_over_lines(mine, cols, arrived)
    coupled = [
        call(
            functools.partial(couple_kernel, first),
            jax.ShapeDtypeStruct((nrhs, half * up), F32),
            [WHOLE, WHOLE],
            12,
            (nrhs * update_rows.size, 2 * update_rows.size),
        )(vectors, in_vmem(update))
        for first, vectors in ((0, mine), (half, other))
    ]
    coupled = jnp.concatenate(coupled, 1)
    coupled = coupled + sum(swap(coupled, "row", rows, k) for k in range(1, rows))
    numbers = jnp.pad(
        update_map.astype(F32), ((0, nrhs - subs), (0, BLOCK - update_map.shape[1]))
    )
    coupled = jnp.concatenate([coupled, numbers], 1)
    near = jnp.stack(
        [coupled] + [swap(coupled, plane_axes, plane_size, CORES * m) for m in range(1, chips)]
    )
    far = swap(near, "col", cols, 1)

    shape = (leaves, rows, cols, lines)
    start = call(
        functools.partial(scatter_kernel, lines),
        jax.ShapeDtypeStruct((width // BLOCK, nrhs, BLOCK), F32),
        [WHOLE, WHOLE],
        4,
        (2 * nrhs * width, 12 * nrhs * width),
        (pltpu.SMEM((chips, subs, BLOCK), F32), pltpu.SemaphoreType.DMA((chips,))),
    )(near, sep_rhs)
    inside = sep_rows % BLOCK == 0
    own_width = rows * sep_rows
    length = subs * up + (own_width if inside else 0)
    piece = jax.ShapeDtypeStruct((chips, nrhs, length), F32)
    keep, send, *back = call(
        functools.partial(separator_kernel, shape, inside),
        (piece, piece) + (() if inside else (jax.ShapeDtypeStruct((nrhs, width), F32),)),
        [WHOLE] * 4,
        12,
        (4 * nrhs * sep_inverse.size, 4 * sep_inverse.size),
        (
            pltpu.VMEM((width // BLOCK, nrhs, BLOCK), F32),
            pltpu.VMEM(sep_inverse.shape, BF16),
            pltpu.VMEM(sep_inverse.shape, BF16),
            pltpu.SMEM((chips, subs, BLOCK), F32),
            pltpu.SMEM((chips, subs, BLOCK), F32),
            pltpu.SemaphoreType.DMA((chips,)),
            pltpu.SemaphoreType.DMA((chips,)),
        ),
    )(near, far, start, sep_inverse)
    if not inside:
        own = back[0].reshape(nrhs, leaves, rows, lines, CORES, sep_rows)
        own = own.transpose(4, 1, 3, 0, 2, 5).reshape(CORES, chips, nrhs, own_width)
        own = picked(picked(own, 0, core, CORES), 1, plane, chips)
        keep = jnp.concatenate([keep, own[0]], 2)
        send = jnp.concatenate([send, own[1]], 2)
    keep = keep + swap(send, "col", cols, 1)
    pulled = keep[0] + sum(swap(keep[m], plane_axes, plane_size, CORES * m) for m in range(1, chips))
    own = pulled[:, subs * up :]
    pulled = pulled[:, : subs * up]
    pulled = pulled + sum(swap(pulled, "row", rows, k) for k in range(1, rows))

    pull_other, pull_mine = (
        call(
            functools.partial(pull_kernel, first),
            vec,
            [WHOLE, WHOLE],
            12,
            (nrhs * update_rows.size, 2 * update_rows.size),
        )(pulled, update_rows)
        for first in (half, 0)
    )
    pull_mine = pull_mine + swap(pull_other, "col", cols, 1)
    pull_mine, pull_other = sum_over_lines(pull_mine, cols)
    share = leaf_cols // rows
    if inside and share % BLOCK == 0:
        near_part, far_parts = (
            call(
                functools.partial(solve_parts_kernel, rows, masks),
                (jax.ShapeDtypeStruct((nrhs, subs * share + sep_rows), F32),) * len(masks),
                [WHOLE] * 6,
                16,
                (leaf_flops * len(masks) // rows, 4 * leaf_inverse.size * len(masks) // rows),
            )(mine, other, pull_mine, pull_other, own, leaf_inverse)
            for masks in ((0,), tuple(range(1, rows)))
        )
        parts = [*near_part] + [swap(part, "row", rows, k) for k, part in enumerate(far_parts, 1)]
        return call(
            finish_kernel,
            (
                jax.ShapeDtypeStruct((subs, nrhs, share), F32),
                jax.ShapeDtypeStruct((nrhs, sep_rows), F32),
            ),
            [WHOLE] * rows,
            4,
            (parts[0].size * rows, 4 * parts[0].size * rows),
        )(*parts)
    terms = call(
        solve_kernel,
        jax.ShapeDtypeStruct((subs, nrhs, leaf_cols), F32),
        [WHOLE] * 5,
        16,
        (leaf_flops, 4 * leaf_inverse.size),
    )(mine, other, pull_mine, pull_other, leaf_inverse)

    def last(k):
        leaf_part = lax.dynamic_slice_in_dim(terms, (row ^ k) * share, share, 2)
        own_part = lax.dynamic_slice_in_dim(own, (row ^ k) * sep_rows, sep_rows, 1)
        return jnp.concatenate([*leaf_part, own_part], 1)

    parts = [last(0)] + [swap(last(k), "row", rows, k) for k in range(1, rows)]
    done = sum(parts[1:]) + parts[0]
    leaf_solution = jnp.stack([done[:, s * share : (s + 1) * share] for s in range(subs)])
    return (leaf_solution, done[:, subs * share :])


def solution(mesh):
    sizes = tuple(mesh.shape[a] for a in ("leaf", "row", "col"))
    in_specs = (
        P("leaf", None, "col"),
        P("leaf", "row", "col"),
        P("leaf", "col", "row"),
        P("leaf", None),
        P(),
        P(("leaf", "row", "col"), None),
    )
    out_specs = (P("leaf", None, ("col", "row")), P(None, ("leaf", "row", "col")))
    return jax.shard_map(
        functools.partial(body, sizes), mesh=mesh, in_specs=in_specs, out_specs=out_specs, check_vma=False
    )
```

time: 82.5 us -> 74.1 us (0.90)
  local copies, waits for them, and re-layouts: 5.69 us -> 0.07 us
  starting transfers between devices: 26.5 us -> 25 us
  waiting for transfers between devices: 34 us -> 32.8 us
    unnamed x12, local copies, waits for them, and re-layouts: 5.59 us -> 0.04 us
    ppermute x24 -> x23, starting transfers between devices: 26.5 us -> 25 us  [swap(): return lax.ppermute(value, axes, [(i, i ^ mask) for i in range(size)])]
    ppermute x24 -> x23, waiting for transfers between devices: 34 us -> 32.8 us  [swap(): return lax.ppermute(value, axes, [(i, i ^ mask) for i in range(size)])]
    pallas_call x6 -> x10, Pallas kernels: 14.3 us -> 14.3 us  [the longest x1 4.49 us: body(): call(leaf_kernel, (pltpu.VMEM(vec.shape, F32), pltpu.VMEM(vec.shape, F32)...]
  transfers between devices with their start and end apart: 24 -> 23, of which waited for: 21 -> 20; matrix products, arithmetic and copies ran while one was open for 0% -> 0% of each run, Pallas kernels for 1% -> 6%
where the time goes in v3:
time: 74.1 us; the launch traced here: 73.9 us
  waiting for transfers between devices  32.8 us (44%)
  starting transfers between devices  25 us (34%)
  Pallas kernels  14.9 us (20%)
  between operations  0.84 us (1%)
    ppermute x23, waiting for transfers between devices, swap(): return lax.ppermute(value, axes, [(i, i ^ mask) for i in range(size)])  32.8 us
    ppermute x23, starting transfers between devices, swap(): return lax.ppermute(value, axes, [(i, i ^ mask) for i in range(size)])  25 us
    pallas_call x1, Pallas kernels, body(): call(leaf_kernel, (pltpu.VMEM(vec.shape, F32), pltpu.VMEM(vec.shape, F32)...  4.49 us
    pallas_call x1, Pallas kernels, body(): call(functools.partial(separator_kernel, shape, inside), (piece, piece) +...  2.56 us
    pallas_call x1, Pallas kernels, beside(): pl.pallas_call(load_kernel, out_shape=pltpu.VMEM(value.shape, value.dtype...  2.24 us
    pallas_call x2, Pallas kernels, body(): call(functools.partial(solve_parts_kernel, rows, masks), (jax.ShapeDtypeS...  1.92 us
  transfers between devices with their start and end apart: 23, of which 20 were waited for; matrix products, arithmetic and copies ran while one was open for 0% of the time, Pallas kernels for 6%

profile of v3, /device:TPU:0, one launch (start us, length us, event | category | flops | bytes accessed | tf_op | source)
XLA Modules:
  0.0 73.9 jit_solution(7209607288949031179)
XLA Ops:
  0.6 4.5 %shard_map.77 = (f32[1,16,1024]{2,1,0:T(8,128)S(1)}, f32[1,16,1024]{2,1,0:T(8,128)S(1)}) custom-call(f32[2,16,1024]{2,1,0:T(8,128)} %rhs.2, f32[2,1024,1024]{2,1,0:T(8,128)} %inverse.5), custom_call_target="tpu_custom_call" | custom-call | flops 67108864 | bytes 8388608 | tf_op jit(solution)/shard_map/pallas_call | solution.py:298
  5.1 0.5 collective-permute-start
  5.6 0.9 %collective-permute-done = f32[1,16,1024]{2,1,0:T(8,128)S(1)} collective-permute-done((f32[1,16,1024]{2,1,0:T(8,128)S(1)}, f32[1,16,1024]{2,1,0:T(8,128)S(1)}, u32[]{:S(2)}, u32[]{:S(2)}) %collective-permute-start) | collective-permute-done | bytes 65568 | tf_op jit(solution)/shard_map/ppermute | solution.py:238
  6.6 2.9 %collective-permute-start.1 = (f32[1,16,1024]{2,1,0:T(8,128)S(1)}, f32[1,16,1024]{2,1,0:T(8,128)S(1)}, u32[]{:S(2)}, u32[]{:S(2)}) collective-permute-start(f32[1,16,1024]{2,1,0:T(8,128)S(1)} %add.44), channel_id=1, source_target_pairs={{0,2},{1,3},{2,0},{3,1},{4,6},{5,7},{6,4},{7,5},{8,10},{9,11},{10,... | collective-permute-start | bytes 196616 | tf_op jit(solution)/shard_map/ppermute | solution.py:238
  9.5 2.2 %shard_map.78.update = f32[2,512,1024]{2,1,0:T(8,128)S(1)} custom-call(f32[2,512,1024]{2,1,0:T(8,128)} %update.3), custom_call_target="tpu_custom_call" | custom-call | bytes 4194304 | tf_op jit(solution)/shard_map/pallas_call | solution.py:248
  11.7 0.2 collective-permute-done.1
  12.0 0.7 shard_map.79
  12.7 0.5 collective-permute-done.2.vectors.other
  13.3 0.7 shard_map.80
  14.0 2.0 %collective-permute-start.3 = (f32[16,1024]{1,0:T(8,128)S(1)}, f32[16,1024]{1,0:T(8,128)S(1)}, u32[]{:S(2)}, u32[]{:S(2)}) collective-permute-start(f32[16,1024]{1,0:T(8,128)S(1)} %pad_maximum_fusion.1), channel_id=1, source_target_pairs={{0,4},{4,0},{8,12},{12,8},{1,5},{5,1},{9,13},{13,9},{2,6},{6,2},{1... | collective-permute-start | bytes 196616 | tf_op jit(solution)/shard_map/ppermute | solution.py:238
  15.9 2.6 %collective-permute-start.4 = (f32[16,1024]{1,0:T(8,128)S(1)}, f32[16,1024]{1,0:T(8,128)S(1)}, u32[]{:S(2)}, u32[]{:S(2)}) collective-permute-start(f32[16,1024]{1,0:T(8,128)S(1)} %pad_maximum_fusion.1), channel_id=1, source_target_pairs={{0,8},{4,12},{8,0},{12,4},{1,9},{5,13},{9,1},{13,5},{2,10},{6,14},... | collective-permute-start | bytes 196616 | tf_op jit(solution)/shard_map/ppermute | solution.py:238
  18.6 4.9 %collective-permute-done.4 = f32[16,1024]{1,0:T(8,128)S(1)} collective-permute-done((f32[16,1024]{1,0:T(8,128)S(1)}, f32[16,1024]{1,0:T(8,128)S(1)}, u32[]{:S(2)}, u32[]{:S(2)}) %collective-permute-start.4) | collective-permute-done | bytes 65568 | tf_op jit(solution)/shard_map/ppermute | solution.py:238
  23.5 1.2 %collective-permute-done.5 = f32[16,1024]{1,0:T(8,128)S(1)} collective-permute-done((f32[16,1024]{1,0:T(8,128)S(1)}, f32[16,1024]{1,0:T(8,128)S(1)}, u32[]{:S(2)}, u32[]{:S(2)}) %collective-permute-start.5) | collective-permute-done | bytes 65568 | tf_op jit(solution)/shard_map/ppermute | solution.py:238
  24.7 1.6 %collective-permute-start.6 = (f32[16,1152]{1,0:T(8,128)S(1)}, f32[16,1152]{1,0:T(8,128)S(1)}, u32[]{:S(2)}, u32[]{:S(2)}) collective-permute-start(f32[16,1152]{1,0:T(8,128)S(1)} %get-tuple-element.24), channel_id=1, source_target_pairs={{0,2},{1,3},{2,0},{3,1},{16,18},{17,19},{18,16},{19,17},{4,6},{5,7... | collective-permute-start | bytes 221192 | tf_op jit(solution)/shard_map/ppermute | solution.py:238
  26.3 1.5 %collective-permute-start.7 = (f32[16,1152]{1,0:T(8,128)S(1)}, f32[16,1152]{1,0:T(8,128)S(1)}, u32[]{:S(2)}, u32[]{:S(2)}) collective-permute-start(f32[16,1152]{1,0:T(8,128)S(1)} %get-tuple-element.24), channel_id=1, source_target_pairs={{0,16},{1,17},{2,18},{3,19},{16,0},{17,1},{18,2},{19,3},{4,20},{5,... | collective-permute-start | bytes 221192 | tf_op jit(solution)/shard_map/ppermute | solution.py:238
  27.8 0.5 collective-permute-start.8
  28.3 0.9 %collective-permute-done.6 = f32[16,1152]{1,0:T(8,128)S(1)} collective-permute-done((f32[16,1152]{1,0:T(8,128)S(1)}, f32[16,1152]{1,0:T(8,128)S(1)}, u32[]{:S(2)}, u32[]{:S(2)}) %collective-permute-start.6) | collective-permute-done | bytes 73760 | tf_op jit(solution)/shard_map/ppermute | solution.py:238
  29.2 1.5 %collective-permute-done.7 = f32[16,1152]{1,0:T(8,128)S(1)} collective-permute-done((f32[16,1152]{1,0:T(8,128)S(1)}, f32[16,1152]{1,0:T(8,128)S(1)}, u32[]{:S(2)}, u32[]{:S(2)}) %collective-permute-start.7) | collective-permute-done | bytes 73760 | tf_op jit(solution)/shard_map/ppermute | solution.py:238
  30.7 2.4 %collective-permute-done.8 = f32[16,1152]{1,0:T(8,128)S(1)} collective-permute-done((f32[16,1152]{1,0:T(8,128)S(1)}, f32[16,1152]{1,0:T(8,128)S(1)}, u32[]{:S(2)}, u32[]{:S(2)}) %collective-permute-start.8) | collective-permute-done | bytes 73760 | tf_op jit(solution)/shard_map/ppermute | solution.py:238
  33.2 0.8 %shard_map.81.start = f32[32,16,128]{2,1,0:T(8,128)S(1)} custom-call(f32[4,16,1152]{2,1,0:T(8,128)S(1)} %pad_maximum_fusion.near, f32[16,4096]{1,0:T(8,128)S(1)} %copy-done.2), custom_call_target="tpu_custom_call" | custom-call | flops 131072 | bytes 786432 | tf_op jit(solution)/shard_map/pallas_call | solution.py:337
  34.0 0.7 collective-permute-done.9.far
  34.7 2.6 %shard_map.82 = (f32[4,16,1536]{2,1,0:T(8,128)S(1)}, f32[4,16,1536]{2,1,0:T(8,128)S(1)}) custom-call(f32[4,16,1152]{2,1,0:T(8,128)S(1)} %pad_maximum_fusion.near, f32[4,16,1152]{2,1,0:T(8,128)S(1)} %collective-permute-done.9.far, f32[32,16,128]{2,1,0:T(8,128)S(1)} %shard_map.81.start, f32[128,4096]{1,0:T(8,128)S(1)} %copy-done.1), custom_call_target="tpu_custom_call" | custom-call | flops 33554432 | bytes 2097152 | tf_op jit(solution)/shard_map/pallas_call | solution.py:349
  37.3 0.2 collective-permute-start.10
  37.5 1.6 %collective-permute-done.10 = f32[4,16,1536]{2,1,0:T(8,128)S(1)} collective-permute-done((f32[4,16,1536]{2,1,0:T(8,128)S(1)}, f32[4,16,1536]{2,1,0:T(8,128)S(1)}, u32[]{:S(2)}, u32[]{:S(2)}) %collective-permute-start.10) | collective-permute-done | bytes 393248 | tf_op jit(solution)/shard_map/ppermute | solution.py:238
  39.2 0.6 collective-permute-start.11
  39.8 0.8 %collective-permute-start.12 = (f32[16,1536]{1,0:T(8,128)S(1)}, f32[16,1536]{1,0:T(8,128)S(1)}, u32[]{:S(2)}, u32[]{:S(2)}) collective-permute-start(f32[16,1536]{1,0:T(8,128)S(1)} %get-tuple-element.20), channel_id=1, source_target_pairs={{0,16},{1,17},{2,18},{3,19},{16,0},{17,1},{18,2},{19,3},{4,20},{5,... | collective-permute-start | bytes 294920 | tf_op jit(solution)/shard_map/ppermute | solution.py:238
  40.6 2.1 %collective-permute-start.13 = (f32[16,1536]{1,0:T(8,128)S(1)}, f32[16,1536]{1,0:T(8,128)S(1)}, u32[]{:S(2)}, u32[]{:S(2)}) collective-permute-start(f32[16,1536]{1,0:T(8,128)S(1)} %get-tuple-element.21), channel_id=1, source_target_pairs={{0,18},{1,19},{2,16},{3,17},{16,2},{17,3},{18,0},{19,1},{4,22},{5,... | collective-permute-start | bytes 294920 | tf_op jit(solution)/shard_map/ppermute | solution.py:238
  42.7 1.3 %collective-permute-done.11 = f32[16,1536]{1,0:T(8,128)S(1)} collective-permute-done((f32[16,1536]{1,0:T(8,128)S(1)}, f32[16,1536]{1,0:T(8,128)S(1)}, u32[]{:S(2)}, u32[]{:S(2)}) %collective-permute-start.11) | collective-permute-done | bytes 98336 | tf_op jit(solution)/shard_map/ppermute | solution.py:238
  44.1 1.2 %collective-permute-done.12 = f32[16,1536]{1,0:T(8,128)S(1)} collective-permute-done((f32[16,1536]{1,0:T(8,128)S(1)}, f32[16,1536]{1,0:T(8,128)S(1)}, u32[]{:S(2)}, u32[]{:S(2)}) %collective-permute-start.12) | collective-permute-done | bytes 98336 | tf_op jit(solution)/shard_map/ppermute | solution.py:238
  45.3 2.0 %collective-permute-done.13 = f32[16,1536]{1,0:T(8,128)S(1)} collective-permute-done((f32[16,1536]{1,0:T(8,128)S(1)}, f32[16,1536]{1,0:T(8,128)S(1)}, u32[]{:S(2)}, u32[]{:S(2)}) %collective-permute-start.13) | collective-permute-done | bytes 98336 | tf_op jit(solution)/shard_map/ppermute | solution.py:238
  47.4 0.9 %collective-permute-start.14 = (f32[16,1024]{1,0:T(8,128)S(1)}, f32[16,1024]{1,0:T(8,128)S(1)}, u32[]{:S(2)}, u32[]{:S(2)}) collective-permute-start(f32[16,1024]{1,0:T(8,128)S(1)} %slice.28), channel_id=1, source_target_pairs={{0,4},{4,0},{8,12},{12,8},{1,5},{5,1},{9,13},{13,9},{2,6},{6,2},{1... | collective-permute-start | bytes 196616 | tf_op jit(solution)/shard_map/ppermute | solution.py:238
  48.3 1.7 %collective-permute-start.15 = (f32[16,1024]{1,0:T(8,128)S(1)}, f32[16,1024]{1,0:T(8,128)S(1)}, u32[]{:S(2)}, u32[]{:S(2)}) collective-permute-start(f32[16,1024]{1,0:T(8,128)S(1)} %slice.28), channel_id=1, source_target_pairs={{0,8},{4,12},{8,0},{12,4},{1,9},{5,13},{9,1},{13,5},{2,10},{6,14},... | collective-permute-start | bytes 196616 | tf_op jit(solution)/shard_map/ppermute | solution.py:238
  50.0 1.8 %collective-permute-start.16 = (f32[16,1024]{1,0:T(8,128)S(1)}, f32[16,1024]{1,0:T(8,128)S(1)}, u32[]{:S(2)}, u32[]{:S(2)}) collective-permute-start(f32[16,1024]{1,0:T(8,128)S(1)} %slice.28), channel_id=1, source_target_pairs={{0,12},{4,8},{8,4},{12,0},{1,13},{5,9},{9,5},{13,1},{2,14},{6,10},... | collective-permute-start | bytes 196616 | tf_op jit(solution)/shard_map/ppermute | solution.py:238
  51.9 2.9 %collective-permute-done.15 = f32[16,1024]{1,0:T(8,128)S(1)} collective-permute-done((f32[16,1024]{1,0:T(8,128)S(1)}, f32[16,1024]{1,0:T(8,128)S(1)}, u32[]{:S(2)}, u32[]{:S(2)}) %collective-permute-start.15) | collective-permute-done | bytes 65568 | tf_op jit(solution)/shard_map/ppermute | solution.py:238
  54.8 1.4 %collective-permute-done.16 = f32[16,1024]{1,0:T(8,128)S(1)} collective-permute-done((f32[16,1024]{1,0:T(8,128)S(1)}, f32[16,1024]{1,0:T(8,128)S(1)}, u32[]{:S(2)}, u32[]{:S(2)}) %collective-permute-start.16) | collective-permute-done | bytes 65568 | tf_op jit(solution)/shard_map/ppermute | solution.py:238
  56.2 0.5 shard_map.84
  56.7 0.5 shard_map.83
  57.2 0.8 %collective-permute-done.17 = f32[1,16,1024]{2,1,0:T(8,128)S(1)} collective-permute-done((f32[1,16,1024]{2,1,0:T(8,128)S(1)}, f32[1,16,1024]{2,1,0:T(8,128)S(1)}, u32[]{:S(2)}, u32[]{:S(2)}) %collective-permute-start.17) | collective-permute-done | bytes 65568 | tf_op jit(solution)/shard_map/ppermute | solution.py:238
  58.0 0.7 collective-permute-start.18
  58.6 3.7 %collective-permute-done.18 = f32[1,16,1024]{2,1,0:T(8,128)S(1)} collective-permute-done((f32[1,16,1024]{2,1,0:T(8,128)S(1)}, f32[1,16,1024]{2,1,0:T(8,128)S(1)}, u32[]{:S(2)}, u32[]{:S(2)}) %collective-permute-start.18) | collective-permute-done | bytes 65568 | tf_op jit(solution)/shard_map/ppermute | solution.py:238
  62.4 1.2 %collective-permute-done.19.pull_other = f32[1,16,1024]{2,1,0:T(8,128)S(1)} collective-permute-done((f32[1,16,1024]{2,1,0:T(8,128)S(1)}, f32[1,16,1024]{2,1,0:T(8,128)S(1)}, u32[]{:S(2)}, u32[]{:S(2)}) %collective-permute-start.19) | collective-permute-done | bytes 65568 | tf_op jit(solution)/shard_map/ppermute | solution.py:238
  63.6 1.4 %shard_map.86 = (f32[16,640]{1,0:T(8,128)S(1)}, f32[16,640]{1,0:T(8,128)S(1)}, f32[16,640]{1,0:T(8,128)S(1)}) custom-call(f32[1,16,1024]{2,1,0:T(8,128)S(1)} %add.45.vectors.mine, f32[1,16,1024]{2,1,0:T(8,128)S(1)} %collective-permute-done.2.vectors.other, f32[1,16,1024]{2,1,0:T(8,128)S(1)} %add.57.pull_mine, ...), custom_call_target="tpu_custom_call" | custom-call | flops 50331648 | bytes 6291456 | tf_op jit(solution)/shard_map/pallas_call | solution.py:392
  65.0 2.5 %collective-permute-start.21 = (f32[16,640]{1,0:T(8,128)S(1)}, f32[16,640]{1,0:T(8,128)S(1)}, u32[]{:S(2)}, u32[]{:S(2)}) collective-permute-start(f32[16,640]{1,0:T(8,128)S(1)} %get-tuple-element.18), channel_id=1, source_target_pairs={{0,8},{4,12},{8,0},{12,4},{1,9},{5,13},{9,1},{13,5},{2,10},{6,14},... | collective-permute-start | bytes 122888 | tf_op jit(solution)/shard_map/ppermute | solution.py:238
  67.5 1.9 %collective-permute-start.22 = (f32[16,640]{1,0:T(8,128)S(1)}, f32[16,640]{1,0:T(8,128)S(1)}, u32[]{:S(2)}, u32[]{:S(2)}) collective-permute-start(f32[16,640]{1,0:T(8,128)S(1)} %get-tuple-element.19), channel_id=1, source_target_pairs={{0,12},{4,8},{8,4},{12,0},{1,13},{5,9},{9,5},{13,1},{2,14},{6,10},... | collective-permute-start | bytes 122888 | tf_op jit(solution)/shard_map/ppermute | solution.py:238
  69.4 0.6 shard_map.85.refs_0_
  70.0 0.5 collective-permute-done.21.refs_2_
  70.5 2.8 %collective-permute-done.22.refs_3_ = f32[16,640]{1,0:T(8,128)S(1)} collective-permute-done((f32[16,640]{1,0:T(8,128)S(1)}, f32[16,640]{1,0:T(8,128)S(1)}, u32[]{:S(2)}, u32[]{:S(2)}) %collective-permute-start.22) | collective-permute-done | bytes 40992 | tf_op jit(solution)/shard_map/ppermute | solution.py:238
  73.3 0.6 shard_map.87
  (37 shorter events, 0.5 us)
Async XLA Ops:
  5.1 1.4 %collective-permute-start = (f32[1,16,1024]{2,1,0:T(8,128)S(1)}, f32[1,16,1024]{2,1,0:T(8,128)S(1)}, u32[]{:S(2)}, u32[]{:S(2)}) collective-permute-start(f32[1,16,1024]{2,1,0:T(8,128)S(1)} %get-tuple-element.12), channel_id=1, source_target_pairs={{0,1},{1,0},{2,3},{3,2},{4,5},{5,4},{6,7},{7,6},{8,9},{9,8},{10,11... | collective-permute-start | bytes 196616 | tf_op jit(solution)/shard_map/ppermute | solution.py:238
  6.6 5.3 %collective-permute-start.1 = (f32[1,16,1024]{2,1,0:T(8,128)S(1)}, f32[1,16,1024]{2,1,0:T(8,128)S(1)}, u32[]{:S(2)}, u32[]{:S(2)}) collective-permute-start(f32[1,16,1024]{2,1,0:T(8,128)S(1)} %add.44), channel_id=1, source_target_pairs={{0,2},{1,3},{2,0},{3,1},{4,6},{5,7},{6,4},{7,5},{8,10},{9,11},{10,... | collective-permute-start | bytes 196616 | tf_op jit(solution)/shard_map/ppermute | solution.py:238
  11.9 6.6 %copy-start.3 = (s32[2,16]{1,0:T(2,128)S(1)}, s32[2,16]{1,0:T(2,128)}, u32[]{:S(2)}) copy-start(s32[2,16]{1,0:T(2,128)} %param.9) | copy-start | bytes 388
  11.9 21.2 %copy-start.2 = (f32[16,4096]{1,0:T(8,128)S(1)}, f32[16,4096]{1,0:T(8,128)}, u32[]{:S(2)}) copy-start(f32[16,4096]{1,0:T(8,128)} %rhs.3) | copy-start | bytes 786436
  11.9 1.3 %collective-permute-start.2 = (f32[1,16,1024]{2,1,0:T(8,128)S(1)}, f32[1,16,1024]{2,1,0:T(8,128)S(1)}, u32[]{:S(2)}, u32[]{:S(2)}) collective-permute-start(f32[1,16,1024]{2,1,0:T(8,128)S(1)} %add.45.vectors.mine), channel_id=1, source_target_pairs={{0,1},{1,0},{2,3},{3,2},{4,5},{5,4},{6,7},{7,6},{8,9},{9,8},{10,11... | collective-permute-start | bytes 196616 | tf_op jit(solution)/shard_map/ppermute | solution.py:238
  12.7 22.0 %copy-start.1 = (f32[128,4096]{1,0:T(8,128)S(1)}, f32[128,4096]{1,0:T(8,128)}, u32[]{:S(2)}) copy-start(f32[128,4096]{1,0:T(8,128)} %sep.1) | copy-start | bytes 6291460
  13.9 42.3 %copy-start = (f32[2,512,1024]{2,1,0:T(8,128)S(1)}, f32[2,512,1024]{2,1,0:T(8,128)}, u32[]{:S(2)}) copy-start(f32[2,512,1024]{2,1,0:T(8,128)} %update.3) | copy-start | bytes 12582916
  14.0 4.6 %collective-permute-start.3 = (f32[16,1024]{1,0:T(8,128)S(1)}, f32[16,1024]{1,0:T(8,128)S(1)}, u32[]{:S(2)}, u32[]{:S(2)}) collective-permute-start(f32[16,1024]{1,0:T(8,128)S(1)} %pad_maximum_fusion.1), channel_id=1, source_target_pairs={{0,4},{4,0},{8,12},{12,8},{1,5},{5,1},{9,13},{13,9},{2,6},{6,2},{1... | collective-permute-start | bytes 196616 | tf_op jit(solution)/shard_map/ppermute | solution.py:238
  15.9 7.5 %collective-permute-start.4 = (f32[16,1024]{1,0:T(8,128)S(1)}, f32[16,1024]{1,0:T(8,128)S(1)}, u32[]{:S(2)}, u32[]{:S(2)}) collective-permute-start(f32[16,1024]{1,0:T(8,128)S(1)} %pad_maximum_fusion.1), channel_id=1, source_target_pairs={{0,8},{4,12},{8,0},{12,4},{1,9},{5,13},{9,1},{13,5},{2,10},{6,14},... | collective-permute-start | bytes 196616 | tf_op jit(solution)/shard_map/ppermute | solution.py:238
  18.5 6.2 %collective-permute-start.5 = (f32[16,1024]{1,0:T(8,128)S(1)}, f32[16,1024]{1,0:T(8,128)S(1)}, u32[]{:S(2)}, u32[]{:S(2)}) collective-permute-start(f32[16,1024]{1,0:T(8,128)S(1)} %pad_maximum_fusion.1), channel_id=1, source_target_pairs={{0,12},{4,8},{8,4},{12,0},{1,13},{5,9},{9,5},{13,1},{2,14},{6,10},... | collective-permute-start | bytes 196616 | tf_op jit(solution)/shard_map/ppermute | solution.py:238
  24.7 4.4 %collective-permute-start.6 = (f32[16,1152]{1,0:T(8,128)S(1)}, f32[16,1152]{1,0:T(8,128)S(1)}, u32[]{:S(2)}, u32[]{:S(2)}) collective-permute-start(f32[16,1152]{1,0:T(8,128)S(1)} %get-tuple-element.24), channel_id=1, source_target_pairs={{0,2},{1,3},{2,0},{3,1},{16,18},{17,19},{18,16},{19,17},{4,6},{5,7... | collective-permute-start | bytes 221192 | tf_op jit(solution)/shard_map/ppermute | solution.py:238
  26.3 4.4 %collective-permute-start.7 = (f32[16,1152]{1,0:T(8,128)S(1)}, f32[16,1152]{1,0:T(8,128)S(1)}, u32[]{:S(2)}, u32[]{:S(2)}) collective-permute-start(f32[16,1152]{1,0:T(8,128)S(1)} %get-tuple-element.24), channel_id=1, source_target_pairs={{0,16},{1,17},{2,18},{3,19},{16,0},{17,1},{18,2},{19,3},{4,20},{5,... | collective-permute-start | bytes 221192 | tf_op jit(solution)/shard_map/ppermute | solution.py:238
  27.8 5.3 %collective-permute-start.8 = (f32[16,1152]{1,0:T(8,128)S(1)}, f32[16,1152]{1,0:T(8,128)S(1)}, u32[]{:S(2)}, u32[]{:S(2)}) collective-permute-start(f32[16,1152]{1,0:T(8,128)S(1)} %get-tuple-element.24), channel_id=1, source_target_pairs={{0,18},{1,19},{2,16},{3,17},{16,2},{17,3},{18,0},{19,1},{4,22},{5,... | collective-permute-start | bytes 221192 | tf_op jit(solution)/shard_map/ppermute | solution.py:238
  33.1 1.6 %collective-permute-start.9 = (f32[4,16,1152]{2,1,0:T(8,128)S(1)}, f32[4,16,1152]{2,1,0:T(8,128)S(1)}, u32[]{:S(2)}, u32[]{:S(2)}) collective-permute-start(f32[4,16,1152]{2,1,0:T(8,128)S(1)} %pad_maximum_fusion.near), channel_id=1, source_target_pairs={{0,1},{1,0},{2,3},{3,2},{4,5},{5,4},{6,7},{7,6},{8,9},{9,8},{10,11... | collective-permute-start | bytes 884744 | tf_op jit(solution)/shard_map/ppermute | solution.py:238
  33.2 30.5 %slice-start = ((s8[8388608]{0:T(1024)(128)(4,1)}), s8[4194304]{0:T(1024)(128)(4,1)S(1)}, s32[]{:S(2)}) async-start(s8[8388608]{0:T(1024)(128)(4,1)} %bitcast.15), calls=%async_computation | async-start | bytes 8388608
  37.3 1.8 %collective-permute-start.10 = (f32[4,16,1536]{2,1,0:T(8,128)S(1)}, f32[4,16,1536]{2,1,0:T(8,128)S(1)}, u32[]{:S(2)}, u32[]{:S(2)}) collective-permute-start(f32[4,16,1536]{2,1,0:T(8,128)S(1)} %get-tuple-element.16), channel_id=1, source_target_pairs={{0,1},{1,0},{2,3},{3,2},{4,5},{5,4},{6,7},{7,6},{8,9},{9,8},{10,11... | collective-permute-start | bytes 1179656 | tf_op jit(solution)/shard_map/ppermute | solution.py:238
  39.2 4.9 %collective-permute-start.11 = (f32[16,1536]{1,0:T(8,128)S(1)}, f32[16,1536]{1,0:T(8,128)S(1)}, u32[]{:S(2)}, u32[]{:S(2)}) collective-permute-start(f32[16,1536]{1,0:T(8,128)S(1)} %get-tuple-element.22), channel_id=1, source_target_pairs={{0,2},{1,3},{2,0},{3,1},{16,18},{17,19},{18,16},{19,17},{4,6},{5,7... | collective-permute-start | bytes 294920 | tf_op jit(solution)/shard_map/ppermute | solution.py:238
  39.8 5.6 %collective-permute-start.12 = (f32[16,1536]{1,0:T(8,128)S(1)}, f32[16,1536]{1,0:T(8,128)S(1)}, u32[]{:S(2)}, u32[]{:S(2)}) collective-permute-start(f32[16,1536]{1,0:T(8,128)S(1)} %get-tuple-element.20), channel_id=1, source_target_pairs={{0,16},{1,17},{2,18},{3,19},{16,0},{17,1},{18,2},{19,3},{4,20},{5,... | collective-permute-start | bytes 294920 | tf_op jit(solution)/shard_map/ppermute | solution.py:238
  40.6 6.8 %collective-permute-start.13 = (f32[16,1536]{1,0:T(8,128)S(1)}, f32[16,1536]{1,0:T(8,128)S(1)}, u32[]{:S(2)}, u32[]{:S(2)}) collective-permute-start(f32[16,1536]{1,0:T(8,128)S(1)} %get-tuple-element.21), channel_id=1, source_target_pairs={{0,18},{1,19},{2,16},{3,17},{16,2},{17,3},{18,0},{19,1},{4,22},{5,... | collective-permute-start | bytes 294920 | tf_op jit(solution)/shard_map/ppermute | solution.py:238
  47.4 4.5 %collective-permute-start.14 = (f32[16,1024]{1,0:T(8,128)S(1)}, f32[16,1024]{1,0:T(8,128)S(1)}, u32[]{:S(2)}, u32[]{:S(2)}) collective-permute-start(f32[16,1024]{1,0:T(8,128)S(1)} %slice.28), channel_id=1, source_target_pairs={{0,4},{4,0},{8,12},{12,8},{1,5},{5,1},{9,13},{13,9},{2,6},{6,2},{1... | collective-permute-start | bytes 196616 | tf_op jit(solution)/shard_map/ppermute | solution.py:238
  48.3 6.5 %collective-permute-start.15 = (f32[16,1024]{1,0:T(8,128)S(1)}, f32[16,1024]{1,0:T(8,128)S(1)}, u32[]{:S(2)}, u32[]{:S(2)}) collective-permute-start(f32[16,1024]{1,0:T(8,128)S(1)} %slice.28), channel_id=1, source_target_pairs={{0,8},{4,12},{8,0},{12,4},{1,9},{5,13},{9,1},{13,5},{2,10},{6,14},... | collective-permute-start | bytes 196616 | tf_op jit(solution)/shard_map/ppermute | solution.py:238
  50.0 6.1 %collective-permute-start.16 = (f32[16,1024]{1,0:T(8,128)S(1)}, f32[16,1024]{1,0:T(8,128)S(1)}, u32[]{:S(2)}, u32[]{:S(2)}) collective-permute-start(f32[16,1024]{1,0:T(8,128)S(1)} %slice.28), channel_id=1, source_target_pairs={{0,12},{4,8},{8,4},{12,0},{1,13},{5,9},{9,5},{13,1},{2,14},{6,10},... | collective-permute-start | bytes 196616 | tf_op jit(solution)/shard_map/ppermute | solution.py:238
  56.2 7.4 %slice-start.1 = ((s8[8388608]{0:T(1024)(128)(4,1)}), s8[4194304]{0:T(1024)(128)(4,1)S(1)}, s32[]{:S(2)}) async-start(s8[8388608]{0:T(1024)(128)(4,1)} %bitcast.15), calls=%async_computation.1 | async-start | bytes 8388608
  56.7 1.3 %collective-permute-start.17 = (f32[1,16,1024]{2,1,0:T(8,128)S(1)}, f32[1,16,1024]{2,1,0:T(8,128)S(1)}, u32[]{:S(2)}, u32[]{:S(2)}) collective-permute-start(f32[1,16,1024]{2,1,0:T(8,128)S(1)} %shard_map.84), channel_id=1, source_target_pairs={{0,1},{1,0},{2,3},{3,2},{4,5},{5,4},{6,7},{7,6},{8,9},{9,8},{10,11... | collective-permute-start | bytes 196616 | tf_op jit(solution)/shard_map/ppermute | solution.py:238
  58.0 4.3 %collective-permute-start.18 = (f32[1,16,1024]{2,1,0:T(8,128)S(1)}, f32[1,16,1024]{2,1,0:T(8,128)S(1)}, u32[]{:S(2)}, u32[]{:S(2)}) collective-permute-start(f32[1,16,1024]{2,1,0:T(8,128)S(1)} %add.56), channel_id=1, source_target_pairs={{0,2},{1,3},{2,0},{3,1},{4,6},{5,7},{6,4},{7,5},{8,10},{9,11},{10,... | collective-permute-start | bytes 196616 | tf_op jit(solution)/shard_map/ppermute | solution.py:238
  62.3 1.3 %collective-permute-start.19 = (f32[1,16,1024]{2,1,0:T(8,128)S(1)}, f32[1,16,1024]{2,1,0:T(8,128)S(1)}, u32[]{:S(2)}, u32[]{:S(2)}) collective-permute-start(f32[1,16,1024]{2,1,0:T(8,128)S(1)} %add.57.pull_mine), channel_id=1, source_target_pairs={{0,1},{1,0},{2,3},{3,2},{4,5},{5,4},{6,7},{7,6},{8,9},{9,8},{10,11... | collective-permute-start | bytes 196616 | tf_op jit(solution)/shard_map/ppermute | solution.py:238
  65.0 5.0 %collective-permute-start.20 = (f32[16,640]{1,0:T(8,128)S(1)}, f32[16,640]{1,0:T(8,128)S(1)}, u32[]{:S(2)}, u32[]{:S(2)}) collective-permute-start(f32[16,640]{1,0:T(8,128)S(1)} %get-tuple-element.17), channel_id=1, source_target_pairs={{0,4},{4,0},{8,12},{12,8},{1,5},{5,1},{9,13},{13,9},{2,6},{6,2},{1... | collective-permute-start | bytes 122888 | tf_op jit(solution)/shard_map/ppermute | solution.py:238
  65.0 5.5 %collective-permute-start.21 = (f32[16,640]{1,0:T(8,128)S(1)}, f32[16,640]{1,0:T(8,128)S(1)}, u32[]{:S(2)}, u32[]{:S(2)}) collective-permute-start(f32[16,640]{1,0:T(8,128)S(1)} %get-tuple-element.18), channel_id=1, source_target_pairs={{0,8},{4,12},{8,0},{12,4},{1,9},{5,13},{9,1},{13,5},{2,10},{6,14},... | collective-permute-start | bytes 122888 | tf_op jit(solution)/shard_map/ppermute | solution.py:238
  67.5 5.8 %collective-permute-start.22 = (f32[16,640]{1,0:T(8,128)S(1)}, f32[16,640]{1,0:T(8,128)S(1)}, u32[]{:S(2)}, u32[]{:S(2)}) collective-permute-start(f32[16,640]{1,0:T(8,128)S(1)} %get-tuple-element.19), channel_id=1, source_target_pairs={{0,12},{4,8},{8,4},{12,0},{1,13},{5,9},{9,5},{13,1},{2,14},{6,10},... | collective-permute-start | bytes 122888 | tf_op jit(solution)/shard_map/ppermute | solution.py:238

commit v4 on v3

--- a/solution.py
+++ b/solution.py
@@ -42,8 +42,14 @@
 COLUMNS_OF = (((1,), (0,)), ((), ()))
 
 
-def sub_of(slot, half, core):
-    return core * half + slot if slot < half else (1 - core) * half + (slot - half)
+def role_of(col):
+    for shift in (1, 2, 4, 8):
+        col = col ^ (col >> shift)
+    return col & 1
+
+
+def sub_of(slot, half, role):
+    return role * half + slot if slot < half else (1 - role) * half + (slot - half)
 
 
 def chunk_of(rows):
@@ -53,7 +59,7 @@
 def leaf_kernel(rhs, inverse, mine, other, held, land, sems, rhs_sem):
     subs, rows, _ = inverse.shape
     half = subs // CORES
-    core = lax.axis_index("col") % CORES
+    role = role_of(lax.axis_index("col"))
     chunk = chunk_of(rows)
     steps = rows // chunk
     order = [*range(half, subs), *range(half)]
@@ -61,7 +67,7 @@
     def fetch(slot, step):
         part = pl.ds(step * chunk, chunk)
         return pltpu.make_async_copy(
-            inverse.at[sub_of(slot, half, core), part], land.at[slot, part], sems.at[slot * steps + step]
+            inverse.at[sub_of(slot, half, role), part], land.at[slot, part], sems.at[slot * steps + step]
         )
 
     first = pltpu.make_async_copy(rhs, held, rhs_sem)
@@ -72,7 +78,7 @@
     first.wait()
     for slot in order:
         out, at = (mine, slot) if slot < half else (other, slot - half)
-        value = held[sub_of(slot, half, core)]
+        value = held[sub_of(slot, half, role)]
         for step in range(steps):
             part = pl.ds(step * chunk, chunk)
             fetch(slot, step).wait()
@@ -81,9 +87,9 @@
 
 def couple_kernel(first, vectors, update, out):
     subs, up, _ = update.shape
-    core = lax.axis_index("col") % CORES
+    role = role_of(lax.axis_index("col"))
     for i in range(vectors.shape[0]):
-        matrix = update[sub_of(first + i, subs // CORES, core)]
+        matrix = update[sub_of(first + i, subs // CORES, role)]
         out[:, i * up : (i + 1) * up] = dot3(vectors[i], split(matrix), ROWS_OF)
 
 
@@ -113,18 +119,22 @@
     ]
 
 
+def core_of(col, side, chip):
+    return (col + side + (chip > 0)) % CORES
+
+
 def spots(lines, side, numbers, length):
     chips, subs, _ = numbers.shape
     here = length // (subs * BLOCK)
-    col = lax.axis_index("col")
-    core = (col + side) % CORES
+    me = lax.axis_index("col")
     for chip in range(chips):
-        first = ((col // CORES ^ (chip % lines)) * CORES + core) * here
+        col = (me // CORES ^ (chip % lines)) * CORES + core_of(me, side, chip)
+        role = role_of(col)
         for slot in range(subs):
-            sub = sub_of(slot, subs // CORES, core)
+            sub = sub_of(slot, subs // CORES, role)
             for k in range(here):
                 at = (slot * here + k) * BLOCK
-                block = numbers[chip, sub, first + k].astype(jnp.int32)
+                block = numbers[chip, sub, col * here + k].astype(jnp.int32)
                 yield chip, slice(at, at + BLOCK), block
 
 
@@ -173,7 +183,7 @@
     for side, out in ((1, send), (0, keep)):
         for chip in range(chips):
             other = plane ^ chip
-            col = (other % lines) * CORES + (me + side) % CORES
+            col = (other % lines) * CORES + core_of(me, side, chip)
             for row in range(rows):
                 for w in range(wide):
                     block = ((other // lines * rows + row) * cols + col) * wide + w
@@ -183,55 +193,56 @@
 
 def pull_kernel(first, pulled, update, out):
     subs, up, _ = update.shape
-    core = lax.axis_index("col") % CORES
+    role = role_of(lax.axis_index("col"))
     for i in range(out.shape[0]):
         slot = first + i
         value = pulled[:, slot * up : (slot + 1) * up]
-        matrix = update[sub_of(slot, subs // CORES, core)]
+        matrix = update[sub_of(slot, subs // CORES, role)]
         out[i] = dot3(value, split(matrix), COLUMNS_OF)
 
 
-def reduced_of(mine, other, pull_mine, pull_other):
+def solve_kernel(mine, other, pull_mine, pull_other, inverse, out):
     half = mine.shape[0]
-    core = lax.axis_index("col") % CORES
+    role = role_of(lax.axis_index("col"))
     for slot in range(2 * half):
         if slot < half:
             value = mine[slot] - pull_mine[slot]
         else:
             value = other[slot - half] - pull_other[slot - half]
-        yield slot, sub_of(slot, half, core), value
-
-
-def solve_kernel(mine, other, pull_mine, pull_other, inverse, out):
-    for _, sub, value in reduced_of(mine, other, pull_mine, pull_other):
+        sub = sub_of(slot, half, role)
         out[sub] = dot3(value, split(inverse[sub]), COLUMNS_OF)
 
 
-def solve_parts_kernel(rows, masks, mine, other, pull_mine, pull_other, own, inverse, *outs):
-    subs, _, width = inverse.shape
+def solve_parts_kernel(rows, masks, first, vectors, pull, own, inverse, *outs):
+    half, width = vectors.shape[0], inverse.shape[2]
     share = width // rows
     sep_rows = own.shape[1] // rows
-    row = lax.axis_index("row")
-    for slot, sub, value in reduced_of(mine, other, pull_mine, pull_other):
+    row, role = lax.axis_index("row"), role_of(lax.axis_index("col"))
+    for i in range(half):
+        value = vectors[i] - pull[i]
+        sub = sub_of(first + i, half, role)
         for mask, out in zip(masks, outs, strict=True):
             columns = pl.ds(pl.multiple_of((row ^ mask) * share, share), share)
             terms = dot3(value, split(inverse[sub, :, columns]), COLUMNS_OF)
-            out[:, slot * share : (slot + 1) * share] = terms
-    for mask, out in zip(masks, outs, strict=True):
-        columns = pl.ds(pl.multiple_of((row ^ mask) * sep_rows, sep_rows), sep_rows)
-        out[:, subs * share :] = own[:, columns]
+            out[:, i * share : (i + 1) * share] = terms
+    if first == 0:
+        for mask, out in zip(masks, outs, strict=True):
+            columns = pl.ds(pl.multiple_of((row ^ mask) * sep_rows, sep_rows), sep_rows)
+            out[:, half * share :] = own[:, columns]
 
 
 def finish_kernel(*refs):
     *parts, leaf_out, sep_out = refs
     subs, _, share = leaf_out.shape
-    core = lax.axis_index("col") % CORES
+    half, sep_rows = subs // CORES, sep_out.shape[1]
+    role = role_of(lax.axis_index("col"))
     done = parts[0][...]
     for part in parts[1:]:
         done = done + part[...]
     for slot in range(subs):
-        leaf_out[sub_of(slot, subs // CORES, core)] = done[:, slot * share : (slot + 1) * share]
-    sep_out[...] = done[:, subs * share :]
+        at = slot * share + (0 if slot < half else sep_rows)
+        leaf_out[sub_of(slot, half, role)] = done[:, at : at + share]
+    sep_out[...] = done[:, half * share : half * share + sep_rows]
 
 
 def swap(value, axes, size, mask):
@@ -261,7 +272,7 @@
     step = CORES
     while step < cols:
         first = arrived is not None and step == CORES
-        mine = mine + (arrived if first else swap(mine, "col", cols, step))
+        mine = mine + (arrived if first else swap(mine, "col", cols, step + 1))
         step *= 2
     return mine, swap(mine, "col", cols, 1)
 
@@ -310,7 +321,7 @@
     )(in_hbm(leaf_rhs), in_hbm(leaf_inverse))
 
     mine = mine + swap(other, "col", cols, 1)
-    arrived, update = beside(swap(mine, "col", cols, CORES), update_rows)
+    arrived, update = beside(swap(mine, "col", cols, CORES + 1), update_rows)
     mine, other = sum_over_lines(mine, cols, arrived)
     coupled = [
         call(
@@ -329,7 +340,7 @@
     )
     coupled = jnp.concatenate([coupled, numbers], 1)
     near = jnp.stack(
-        [coupled] + [swap(coupled, plane_axes, plane_size, CORES * m) for m in range(1, chips)]
+        [coupled] + [swap(coupled, plane_axes, plane_size, CORES * m + 1) for m in range(1, chips)]
     )
     far = swap(near, "col", cols, 1)
 
@@ -366,10 +377,11 @@
         own = back[0].reshape(nrhs, leaves, rows, lines, CORES, sep_rows)
         own = own.transpose(4, 1, 3, 0, 2, 5).reshape(CORES, chips, nrhs, own_width)
         own = picked(picked(own, 0, core, CORES), 1, plane, chips)
+        own = [jnp.concatenate([own[i][:1], own[1 - i][1:]]) for i in range(CORES)]
         keep = jnp.concatenate([keep, own[0]], 2)
         send = jnp.concatenate([send, own[1]], 2)
     keep = keep + swap(send, "col", cols, 1)
-    pulled = keep[0] + sum(swap(keep[m], plane_axes, plane_size, CORES * m) for m in range(1, chips))
+    pulled = keep[0] + sum(swap(keep[m], plane_axes, plane_size, CORES * m + 1) for m in range(1, chips))
     own = pulled[:, subs * up :]
     pulled = pulled[:, : subs * up]
     pulled = pulled + sum(swap(pulled, "row", rows, k) for k in range(1, rows))
@@ -388,17 +400,22 @@
     pull_mine, pull_other = sum_over_lines(pull_mine, cols)
     share = leaf_cols // rows
     if inside and share % BLOCK == 0:
-        near_part, far_parts = (
-            call(
-                functools.partial(solve_parts_kernel, rows, masks),
-                (jax.ShapeDtypeStruct((nrhs, subs * share + sep_rows), F32),) * len(masks),
-                [WHOLE] * 6,
-                16,
-                (leaf_flops * len(masks) // rows, 4 * leaf_inverse.size * len(masks) // rows),
-            )(mine, other, pull_mine, pull_other, own, leaf_inverse)
-            for masks in ((0,), tuple(range(1, rows)))
-        )
-        parts = [*near_part] + [swap(part, "row", rows, k) for k, part in enumerate(far_parts, 1)]
+        def parts_of(masks):
+            halves = [
+                call(
+                    functools.partial(solve_parts_kernel, rows, masks, first),
+                    (jax.ShapeDtypeStruct((nrhs, half * share + (0 if first else sep_rows)), F32),)
+                    * len(masks),
+                    [WHOLE] * 4,
+                    16,
+                    (leaf_flops * len(masks) // (2 * rows), 2 * leaf_inverse.size * len(masks) // rows),
+                )(vectors, pull, own, leaf_inverse)
+                for first, vectors, pull in ((0, mine, pull_mine), (half, other, pull_other))
+            ]
+            return [jnp.concatenate(pair, 1) for pair in zip(*halves, strict=True)]
+
+        far_parts = [swap(part, "row", rows, k) for k, part in enumerate(parts_of(tuple(range(1, rows))), 1)]
+        parts = parts_of((0,)) + far_parts
         return call(
             finish_kernel,
             (

time: 74.1 us -> 71.8 us (0.969)
  waiting for transfers between devices: 32.8 us -> 30.9 us
    ppermute x23, waiting for transfers between devices: 32.8 us -> 30.9 us  [swap(): return lax.ppermute(value, axes, [(i, i ^ mask) for i in range(size)])]
    pallas_call x2 -> x4, Pallas kernels: 1.92 us -> 1.91 us  [parts_of(): call(functools.partial(solve_parts_kernel, rows, masks, first), (jax.Shap...]
  transfers between devices with their start and end apart: 23 -> 23, of which waited for: 20 -> 19; matrix products, arithmetic and copies ran while one was open for 0% -> 0% of each run, Pallas kernels for 6% -> 8%
where the time goes in v4:
time: 71.8 us; the launch traced here: 71.6 us
  waiting for transfers between devices  30.9 us (43%)
  starting transfers between devices  24.6 us (34%)
  Pallas kernels  14.9 us (21%)
  between operations  0.86 us (1%)
    ppermute x23, waiting for transfers between devices, swap(): return lax.ppermute(value, axes, [(i, i ^ mask) for i in range(size)])  30.9 us
    ppermute x23, starting transfers between devices, swap(): return lax.ppermute(value, axes, [(i, i ^ mask) for i in range(size)])  24.6 us
    pallas_call x1, Pallas kernels, body(): call(leaf_kernel, (pltpu.VMEM(vec.shape, F32), pltpu.VMEM(vec.shape, F32)...  4.49 us
    pallas_call x1, Pallas kernels, body(): call(functools.partial(separator_kernel, shape, inside), (piece, piece) +...  2.57 us
    pallas_call x1, Pallas kernels, beside(): pl.pallas_call(load_kernel, out_shape=pltpu.VMEM(value.shape, value.dtype...  2.24 us
    pallas_call x4, Pallas kernels, parts_of(): call(functools.partial(solve_parts_kernel, rows, masks, first), (jax.Shap...  1.91 us
  transfers between devices with their start and end apart: 23, of which 19 were waited for; matrix products, arithmetic and copies ran while one was open for 0% of the time, Pallas kernels for 8%

profile of v4, /device:TPU:0, one launch (start us, length us, event | category | flops | bytes accessed | tf_op | source)
XLA Modules:
  0.0 71.6 jit_solution(13015153955345888077)
XLA Ops:
  0.6 4.5 %shard_map.77 = (f32[1,16,1024]{2,1,0:T(8,128)S(1)}, f32[1,16,1024]{2,1,0:T(8,128)S(1)}) custom-call(f32[2,16,1024]{2,1,0:T(8,128)} %rhs.2, f32[2,1024,1024]{2,1,0:T(8,128)} %inverse.9), custom_call_target="tpu_custom_call" | custom-call | flops 67108864 | bytes 8388608 | tf_op jit(solution)/shard_map/pallas_call | solution.py:309
  5.1 0.5 collective-permute-start
  5.6 0.9 %collective-permute-done = f32[1,16,1024]{2,1,0:T(8,128)S(1)} collective-permute-done((f32[1,16,1024]{2,1,0:T(8,128)S(1)}, f32[1,16,1024]{2,1,0:T(8,128)S(1)}, u32[]{:S(2)}, u32[]{:S(2)}) %collective-permute-start) | collective-permute-done | bytes 65568 | tf_op jit(solution)/shard_map/ppermute | solution.py:249
  6.6 2.7 %collective-permute-start.1 = (f32[1,16,1024]{2,1,0:T(8,128)S(1)}, f32[1,16,1024]{2,1,0:T(8,128)S(1)}, u32[]{:S(2)}, u32[]{:S(2)}) collective-permute-start(f32[1,16,1024]{2,1,0:T(8,128)S(1)} %add.44), channel_id=1, source_target_pairs={{0,3},{1,2},{2,1},{3,0},{4,7},{5,6},{6,5},{7,4},{8,11},{9,10},{10,... | collective-permute-start | bytes 196616 | tf_op jit(solution)/shard_map/ppermute | solution.py:249
  9.3 2.2 %shard_map.78.update = f32[2,512,1024]{2,1,0:T(8,128)S(1)} custom-call(f32[2,512,1024]{2,1,0:T(8,128)} %update.3), custom_call_target="tpu_custom_call" | custom-call | bytes 4194304 | tf_op jit(solution)/shard_map/pallas_call | solution.py:259
  11.6 0.4 collective-permute-start.2
  12.0 0.7 shard_map.79
  12.7 0.2 collective-permute-done.2.vectors
  12.9 0.7 shard_map.80
  13.6 2.2 %collective-permute-start.3 = (f32[16,1024]{1,0:T(8,128)S(1)}, f32[16,1024]{1,0:T(8,128)S(1)}, u32[]{:S(2)}, u32[]{:S(2)}) collective-permute-start(f32[16,1024]{1,0:T(8,128)S(1)} %pad_maximum_fusion.1), channel_id=1, source_target_pairs={{0,4},{4,0},{8,12},{12,8},{1,5},{5,1},{9,13},{13,9},{2,6},{6,2},{1... | collective-permute-start | bytes 196616 | tf_op jit(solution)/shard_map/ppermute | solution.py:249
  15.7 2.6 %collective-permute-start.4 = (f32[16,1024]{1,0:T(8,128)S(1)}, f32[16,1024]{1,0:T(8,128)S(1)}, u32[]{:S(2)}, u32[]{:S(2)}) collective-permute-start(f32[16,1024]{1,0:T(8,128)S(1)} %pad_maximum_fusion.1), channel_id=1, source_target_pairs={{0,8},{4,12},{8,0},{12,4},{1,9},{5,13},{9,1},{13,5},{2,10},{6,14},... | collective-permute-start | bytes 196616 | tf_op jit(solution)/shard_map/ppermute | solution.py:249
  18.3 4.9 %collective-permute-done.4 = f32[16,1024]{1,0:T(8,128)S(1)} collective-permute-done((f32[16,1024]{1,0:T(8,128)S(1)}, f32[16,1024]{1,0:T(8,128)S(1)}, u32[]{:S(2)}, u32[]{:S(2)}) %collective-permute-start.4) | collective-permute-done | bytes 65568 | tf_op jit(solution)/shard_map/ppermute | solution.py:249
  23.3 1.2 %collective-permute-done.5 = f32[16,1024]{1,0:T(8,128)S(1)} collective-permute-done((f32[16,1024]{1,0:T(8,128)S(1)}, f32[16,1024]{1,0:T(8,128)S(1)}, u32[]{:S(2)}, u32[]{:S(2)}) %collective-permute-start.5) | collective-permute-done | bytes 65568 | tf_op jit(solution)/shard_map/ppermute | solution.py:249
  24.6 2.7 %collective-permute-start.7 = (f32[16,1152]{1,0:T(8,128)S(1)}, f32[16,1152]{1,0:T(8,128)S(1)}, u32[]{:S(2)}, u32[]{:S(2)}) collective-permute-start(f32[16,1152]{1,0:T(8,128)S(1)} %get-tuple-element.30), channel_id=1, source_target_pairs={{0,17},{1,16},{2,19},{3,18},{16,1},{17,0},{18,3},{19,2},{4,21},{5,... | collective-permute-start | bytes 221192 | tf_op jit(solution)/shard_map/ppermute | solution.py:249
  27.4 1.7 %collective-permute-done.6 = f32[16,1152]{1,0:T(8,128)S(1)} collective-permute-done((f32[16,1152]{1,0:T(8,128)S(1)}, f32[16,1152]{1,0:T(8,128)S(1)}, u32[]{:S(2)}, u32[]{:S(2)}) %collective-permute-start.6) | collective-permute-done | bytes 73760 | tf_op jit(solution)/shard_map/ppermute | solution.py:249
  29.1 0.8 %collective-permute-done.7 = f32[16,1152]{1,0:T(8,128)S(1)} collective-permute-done((f32[16,1152]{1,0:T(8,128)S(1)}, f32[16,1152]{1,0:T(8,128)S(1)}, u32[]{:S(2)}, u32[]{:S(2)}) %collective-permute-start.7) | collective-permute-done | bytes 73760 | tf_op jit(solution)/shard_map/ppermute | solution.py:249
  29.9 2.1 %collective-permute-done.8 = f32[16,1152]{1,0:T(8,128)S(1)} collective-permute-done((f32[16,1152]{1,0:T(8,128)S(1)}, f32[16,1152]{1,0:T(8,128)S(1)}, u32[]{:S(2)}, u32[]{:S(2)}) %collective-permute-start.8) | collective-permute-done | bytes 73760 | tf_op jit(solution)/shard_map/ppermute | solution.py:249
  32.1 0.8 %shard_map.81.start = f32[32,16,128]{2,1,0:T(8,128)S(1)} custom-call(f32[4,16,1152]{2,1,0:T(8,128)S(1)} %pad_maximum_fusion.near, f32[16,4096]{1,0:T(8,128)S(1)} %copy-done.2), custom_call_target="tpu_custom_call" | custom-call | flops 131072 | bytes 786432 | tf_op jit(solution)/shard_map/pallas_call | solution.py:348
  32.9 0.7 %collective-permute-done.9.far = f32[4,16,1152]{2,1,0:T(8,128)S(1)} collective-permute-done((f32[4,16,1152]{2,1,0:T(8,128)S(1)}, f32[4,16,1152]{2,1,0:T(8,128)S(1)}, u32[]{:S(2)}, u32[]{:S(2)}) %collective-permute-start.9) | collective-permute-done | bytes 294944 | tf_op jit(solution)/shard_map/ppermute | solution.py:249
  33.7 2.6 %shard_map.82 = (f32[4,16,1536]{2,1,0:T(8,128)S(1)}, f32[4,16,1536]{2,1,0:T(8,128)S(1)}) custom-call(f32[4,16,1152]{2,1,0:T(8,128)S(1)} %pad_maximum_fusion.near, f32[4,16,1152]{2,1,0:T(8,128)S(1)} %collective-permute-done.9.far, f32[32,16,128]{2,1,0:T(8,128)S(1)} %shard_map.81.start, f32[128,4096]{1,0:T(8,128)S(1)} %copy-done.1), custom_call_target="tpu_custom_call" | custom-call | flops 33554432 | bytes 2097152 | tf_op jit(solution)/shard_map/pallas_call | solution.py:360
  36.3 0.2 collective-permute-start.10
  36.5 1.6 %collective-permute-done.10 = f32[4,16,1536]{2,1,0:T(8,128)S(1)} collective-permute-done((f32[4,16,1536]{2,1,0:T(8,128)S(1)}, f32[4,16,1536]{2,1,0:T(8,128)S(1)}, u32[]{:S(2)}, u32[]{:S(2)}) %collective-permute-start.10) | collective-permute-done | bytes 393248 | tf_op jit(solution)/shard_map/ppermute | solution.py:249
  38.1 1.0 %collective-permute-start.11 = (f32[16,1536]{1,0:T(8,128)S(1)}, f32[16,1536]{1,0:T(8,128)S(1)}, u32[]{:S(2)}, u32[]{:S(2)}) collective-permute-start(f32[16,1536]{1,0:T(8,128)S(1)} %get-tuple-element.28), channel_id=1, source_target_pairs={{0,3},{1,2},{2,1},{3,0},{16,19},{17,18},{18,17},{19,16},{4,7},{5,6... | collective-permute-start | bytes 294920 | tf_op jit(solution)/shard_map/ppermute | solution.py:249
  39.1 0.9 %collective-permute-start.12 = (f32[16,1536]{1,0:T(8,128)S(1)}, f32[16,1536]{1,0:T(8,128)S(1)}, u32[]{:S(2)}, u32[]{:S(2)}) collective-permute-start(f32[16,1536]{1,0:T(8,128)S(1)} %get-tuple-element.26), channel_id=1, source_target_pairs={{0,17},{1,16},{2,19},{3,18},{16,1},{17,0},{18,3},{19,2},{4,21},{5,... | collective-permute-start | bytes 294920 | tf_op jit(solution)/shard_map/ppermute | solution.py:249
  40.0 1.2 %collective-permute-start.13 = (f32[16,1536]{1,0:T(8,128)S(1)}, f32[16,1536]{1,0:T(8,128)S(1)}, u32[]{:S(2)}, u32[]{:S(2)}) collective-permute-start(f32[16,1536]{1,0:T(8,128)S(1)} %get-tuple-element.27), channel_id=1, source_target_pairs={{0,19},{1,18},{2,17},{3,16},{16,3},{17,2},{18,1},{19,0},{4,23},{5,... | collective-permute-start | bytes 294920 | tf_op jit(solution)/shard_map/ppermute | solution.py:249
  41.2 1.8 %collective-permute-done.11 = f32[16,1536]{1,0:T(8,128)S(1)} collective-permute-done((f32[16,1536]{1,0:T(8,128)S(1)}, f32[16,1536]{1,0:T(8,128)S(1)}, u32[]{:S(2)}, u32[]{:S(2)}) %collective-permute-start.11) | collective-permute-done | bytes 98336 | tf_op jit(solution)/shard_map/ppermute | solution.py:249
  43.0 0.8 %collective-permute-done.12 = f32[16,1536]{1,0:T(8,128)S(1)} collective-permute-done((f32[16,1536]{1,0:T(8,128)S(1)}, f32[16,1536]{1,0:T(8,128)S(1)}, u32[]{:S(2)}, u32[]{:S(2)}) %collective-permute-start.12) | collective-permute-done | bytes 98336 | tf_op jit(solution)/shard_map/ppermute | solution.py:249
  43.7 2.4 %collective-permute-done.13 = f32[16,1536]{1,0:T(8,128)S(1)} collective-permute-done((f32[16,1536]{1,0:T(8,128)S(1)}, f32[16,1536]{1,0:T(8,128)S(1)}, u32[]{:S(2)}, u32[]{:S(2)}) %collective-permute-start.13) | collective-permute-done | bytes 98336 | tf_op jit(solution)/shard_map/ppermute | solution.py:249
  46.2 0.9 %collective-permute-start.14 = (f32[16,1024]{1,0:T(8,128)S(1)}, f32[16,1024]{1,0:T(8,128)S(1)}, u32[]{:S(2)}, u32[]{:S(2)}) collective-permute-start(f32[16,1024]{1,0:T(8,128)S(1)} %slice.28), channel_id=1, source_target_pairs={{0,4},{4,0},{8,12},{12,8},{1,5},{5,1},{9,13},{13,9},{2,6},{6,2},{1... | collective-permute-start | bytes 196616 | tf_op jit(solution)/shard_map/ppermute | solution.py:249
  47.1 1.7 %collective-permute-start.15 = (f32[16,1024]{1,0:T(8,128)S(1)}, f32[16,1024]{1,0:T(8,128)S(1)}, u32[]{:S(2)}, u32[]{:S(2)}) collective-permute-start(f32[16,1024]{1,0:T(8,128)S(1)} %slice.28), channel_id=1, source_target_pairs={{0,8},{4,12},{8,0},{12,4},{1,9},{5,13},{9,1},{13,5},{2,10},{6,14},... | collective-permute-start | bytes 196616 | tf_op jit(solution)/shard_map/ppermute | solution.py:249
  48.8 1.8 %collective-permute-start.16 = (f32[16,1024]{1,0:T(8,128)S(1)}, f32[16,1024]{1,0:T(8,128)S(1)}, u32[]{:S(2)}, u32[]{:S(2)}) collective-permute-start(f32[16,1024]{1,0:T(8,128)S(1)} %slice.28), channel_id=1, source_target_pairs={{0,12},{4,8},{8,4},{12,0},{1,13},{5,9},{9,5},{13,1},{2,14},{6,10},... | collective-permute-start | bytes 196616 | tf_op jit(solution)/shard_map/ppermute | solution.py:249
  50.6 4.8 %collective-permute-done.15 = f32[16,1024]{1,0:T(8,128)S(1)} collective-permute-done((f32[16,1024]{1,0:T(8,128)S(1)}, f32[16,1024]{1,0:T(8,128)S(1)}, u32[]{:S(2)}, u32[]{:S(2)}) %collective-permute-start.15) | collective-permute-done | bytes 65568 | tf_op jit(solution)/shard_map/ppermute | solution.py:249
  55.5 0.5 shard_map.84
  56.0 0.5 shard_map.83
  56.4 0.8 %collective-permute-done.17 = f32[1,16,1024]{2,1,0:T(8,128)S(1)} collective-permute-done((f32[1,16,1024]{2,1,0:T(8,128)S(1)}, f32[1,16,1024]{2,1,0:T(8,128)S(1)}, u32[]{:S(2)}, u32[]{:S(2)}) %collective-permute-start.17) | collective-permute-done | bytes 65568 | tf_op jit(solution)/shard_map/ppermute | solution.py:249
  57.2 1.0 %collective-permute-start.18 = (f32[1,16,1024]{2,1,0:T(8,128)S(1)}, f32[1,16,1024]{2,1,0:T(8,128)S(1)}, u32[]{:S(2)}, u32[]{:S(2)}) collective-permute-start(f32[1,16,1024]{2,1,0:T(8,128)S(1)} %add.56), channel_id=1, source_target_pairs={{0,3},{1,2},{2,1},{3,0},{4,7},{5,6},{6,5},{7,4},{8,11},{9,10},{10,... | collective-permute-start | bytes 196616 | tf_op jit(solution)/shard_map/ppermute | solution.py:249
  58.2 3.1 %collective-permute-done.18 = f32[1,16,1024]{2,1,0:T(8,128)S(1)} collective-permute-done((f32[1,16,1024]{2,1,0:T(8,128)S(1)}, f32[1,16,1024]{2,1,0:T(8,128)S(1)}, u32[]{:S(2)}, u32[]{:S(2)}) %collective-permute-start.18) | collective-permute-done | bytes 65568 | tf_op jit(solution)/shard_map/ppermute | solution.py:249
  61.4 0.2 collective-permute-start.19
  61.6 0.3 shard_map.85
  61.9 0.7 shard_map.87
  62.7 0.7 shard_map.88
  63.4 2.1 %collective-permute-start.22 = (f32[16,640]{1,0:T(8,128)S(1)}, f32[16,640]{1,0:T(8,128)S(1)}, u32[]{:S(2)}, u32[]{:S(2)}) collective-permute-start(f32[16,640]{1,0:T(8,128)S(1)} %pad_maximum_fusion.5), channel_id=1, source_target_pairs={{0,12},{4,8},{8,4},{12,0},{1,13},{5,9},{9,5},{13,1},{2,14},{6,10},... | collective-permute-start | bytes 122888 | tf_op jit(solution)/shard_map/ppermute | solution.py:249
  65.5 0.8 %collective-permute-start.21 = (f32[16,640]{1,0:T(8,128)S(1)}, f32[16,640]{1,0:T(8,128)S(1)}, u32[]{:S(2)}, u32[]{:S(2)}) collective-permute-start(f32[16,640]{1,0:T(8,128)S(1)} %pad_maximum_fusion.4), channel_id=1, source_target_pairs={{0,8},{4,12},{8,0},{12,4},{1,9},{5,13},{9,1},{13,5},{2,10},{6,14},... | collective-permute-start | bytes 122888 | tf_op jit(solution)/shard_map/ppermute | solution.py:249
  66.3 1.5 %collective-permute-start.20 = (f32[16,640]{1,0:T(8,128)S(1)}, f32[16,640]{1,0:T(8,128)S(1)}, u32[]{:S(2)}, u32[]{:S(2)}) collective-permute-start(f32[16,640]{1,0:T(8,128)S(1)} %pad_maximum_fusion.3), channel_id=1, source_target_pairs={{0,4},{4,0},{8,12},{12,8},{1,5},{5,1},{9,13},{13,9},{2,6},{6,2},{1... | collective-permute-start | bytes 122888 | tf_op jit(solution)/shard_map/ppermute | solution.py:249
  67.8 0.3 shard_map.86
  68.1 1.3 %collective-permute-done.22.refs_3_ = f32[16,640]{1,0:T(8,128)S(1)} collective-permute-done((f32[16,640]{1,0:T(8,128)S(1)}, f32[16,640]{1,0:T(8,128)S(1)}, u32[]{:S(2)}, u32[]{:S(2)}) %collective-permute-start.22) | collective-permute-done | bytes 40992 | tf_op jit(solution)/shard_map/ppermute | solution.py:249
  69.4 1.5 %collective-permute-done.21.refs_2_ = f32[16,640]{1,0:T(8,128)S(1)} collective-permute-done((f32[16,640]{1,0:T(8,128)S(1)}, f32[16,640]{1,0:T(8,128)S(1)}, u32[]{:S(2)}, u32[]{:S(2)}) %collective-permute-start.21) | collective-permute-done | bytes 40992 | tf_op jit(solution)/shard_map/ppermute | solution.py:249
  71.0 0.6 shard_map.89
  (43 shorter events, 0.6 us)
Async XLA Ops:
  5.1 1.4 %collective-permute-start = (f32[1,16,1024]{2,1,0:T(8,128)S(1)}, f32[1,16,1024]{2,1,0:T(8,128)S(1)}, u32[]{:S(2)}, u32[]{:S(2)}) collective-permute-start(f32[1,16,1024]{2,1,0:T(8,128)S(1)} %get-tuple-element.15), channel_id=1, source_target_pairs={{0,1},{1,0},{2,3},{3,2},{4,5},{5,4},{6,7},{7,6},{8,9},{9,8},{10,11... | collective-permute-start | bytes 196616 | tf_op jit(solution)/shard_map/ppermute | solution.py:249
  6.6 4.9 %collective-permute-start.1 = (f32[1,16,1024]{2,1,0:T(8,128)S(1)}, f32[1,16,1024]{2,1,0:T(8,128)S(1)}, u32[]{:S(2)}, u32[]{:S(2)}) collective-permute-start(f32[1,16,1024]{2,1,0:T(8,128)S(1)} %add.44), channel_id=1, source_target_pairs={{0,3},{1,2},{2,1},{3,0},{4,7},{5,6},{6,5},{7,4},{8,11},{9,10},{10,... | collective-permute-start | bytes 196616 | tf_op jit(solution)/shard_map/ppermute | solution.py:249
  11.5 6.8 %copy-start.3 = (s32[2,16]{1,0:T(2,128)S(1)}, s32[2,16]{1,0:T(2,128)}, u32[]{:S(2)}) copy-start(s32[2,16]{1,0:T(2,128)} %param.9) | copy-start | bytes 388
  11.5 20.6 %copy-start.2 = (f32[16,4096]{1,0:T(8,128)S(1)}, f32[16,4096]{1,0:T(8,128)}, u32[]{:S(2)}) copy-start(f32[16,4096]{1,0:T(8,128)} %rhs.3) | copy-start | bytes 786436
  11.6 1.3 %collective-permute-start.2 = (f32[1,16,1024]{2,1,0:T(8,128)S(1)}, f32[1,16,1024]{2,1,0:T(8,128)S(1)}, u32[]{:S(2)}, u32[]{:S(2)}) collective-permute-start(f32[1,16,1024]{2,1,0:T(8,128)S(1)} %add.45.vectors), channel_id=1, source_target_pairs={{0,1},{1,0},{2,3},{3,2},{4,5},{5,4},{6,7},{7,6},{8,9},{9,8},{10,11... | collective-permute-start | bytes 196616 | tf_op jit(solution)/shard_map/ppermute | solution.py:249
  12.7 21.0 %copy-start.1 = (f32[128,4096]{1,0:T(8,128)S(1)}, f32[128,4096]{1,0:T(8,128)}, u32[]{:S(2)}) copy-start(f32[128,4096]{1,0:T(8,128)} %sep.1) | copy-start | bytes 6291460
  13.6 41.9 %copy-start = (f32[2,512,1024]{2,1,0:T(8,128)S(1)}, f32[2,512,1024]{2,1,0:T(8,128)}, u32[]{:S(2)}) copy-start(f32[2,512,1024]{2,1,0:T(8,128)} %update.3) | copy-start | bytes 12582916
  13.6 4.8 %collective-permute-start.3 = (f32[16,1024]{1,0:T(8,128)S(1)}, f32[16,1024]{1,0:T(8,128)S(1)}, u32[]{:S(2)}, u32[]{:S(2)}) collective-permute-start(f32[16,1024]{1,0:T(8,128)S(1)} %pad_maximum_fusion.1), channel_id=1, source_target_pairs={{0,4},{4,0},{8,12},{12,8},{1,5},{5,1},{9,13},{13,9},{2,6},{6,2},{1... | collective-permute-start | bytes 196616 | tf_op jit(solution)/shard_map/ppermute | solution.py:249
  15.7 7.6 %collective-permute-start.4 = (f32[16,1024]{1,0:T(8,128)S(1)}, f32[16,1024]{1,0:T(8,128)S(1)}, u32[]{:S(2)}, u32[]{:S(2)}) collective-permute-start(f32[16,1024]{1,0:T(8,128)S(1)} %pad_maximum_fusion.1), channel_id=1, source_target_pairs={{0,8},{4,12},{8,0},{12,4},{1,9},{5,13},{9,1},{13,5},{2,10},{6,14},... | collective-permute-start | bytes 196616 | tf_op jit(solution)/shard_map/ppermute | solution.py:249
  18.3 6.2 %collective-permute-start.5 = (f32[16,1024]{1,0:T(8,128)S(1)}, f32[16,1024]{1,0:T(8,128)S(1)}, u32[]{:S(2)}, u32[]{:S(2)}) collective-permute-start(f32[16,1024]{1,0:T(8,128)S(1)} %pad_maximum_fusion.1), channel_id=1, source_target_pairs={{0,12},{4,8},{8,4},{12,0},{1,13},{5,9},{9,5},{13,1},{2,14},{6,10},... | collective-permute-start | bytes 196616 | tf_op jit(solution)/shard_map/ppermute | solution.py:249
  24.5 4.6 %collective-permute-start.6 = (f32[16,1152]{1,0:T(8,128)S(1)}, f32[16,1152]{1,0:T(8,128)S(1)}, u32[]{:S(2)}, u32[]{:S(2)}) collective-permute-start(f32[16,1152]{1,0:T(8,128)S(1)} %get-tuple-element.30), channel_id=1, source_target_pairs={{0,3},{1,2},{2,1},{3,0},{16,19},{17,18},{18,17},{19,16},{4,7},{5,6... | collective-permute-start | bytes 221192 | tf_op jit(solution)/shard_map/ppermute | solution.py:249
  24.6 5.3 %collective-permute-start.7 = (f32[16,1152]{1,0:T(8,128)S(1)}, f32[16,1152]{1,0:T(8,128)S(1)}, u32[]{:S(2)}, u32[]{:S(2)}) collective-permute-start(f32[16,1152]{1,0:T(8,128)S(1)} %get-tuple-element.30), channel_id=1, source_target_pairs={{0,17},{1,16},{2,19},{3,18},{16,1},{17,0},{18,3},{19,2},{4,21},{5,... | collective-permute-start | bytes 221192 | tf_op jit(solution)/shard_map/ppermute | solution.py:249
  27.3 4.7 %collective-permute-start.8 = (f32[16,1152]{1,0:T(8,128)S(1)}, f32[16,1152]{1,0:T(8,128)S(1)}, u32[]{:S(2)}, u32[]{:S(2)}) collective-permute-start(f32[16,1152]{1,0:T(8,128)S(1)} %get-tuple-element.30), channel_id=1, source_target_pairs={{0,19},{1,18},{2,17},{3,16},{16,3},{17,2},{18,1},{19,0},{4,23},{5,... | collective-permute-start | bytes 221192 | tf_op jit(solution)/shard_map/ppermute | solution.py:249
  32.0 1.6 %collective-permute-start.9 = (f32[4,16,1152]{2,1,0:T(8,128)S(1)}, f32[4,16,1152]{2,1,0:T(8,128)S(1)}, u32[]{:S(2)}, u32[]{:S(2)}) collective-permute-start(f32[4,16,1152]{2,1,0:T(8,128)S(1)} %pad_maximum_fusion.near), channel_id=1, source_target_pairs={{0,1},{1,0},{2,3},{3,2},{4,5},{5,4},{6,7},{7,6},{8,9},{9,8},{10,11... | collective-permute-start | bytes 884744 | tf_op jit(solution)/shard_map/ppermute | solution.py:249
  32.1 29.5 %slice-start = ((s8[8388608]{0:T(1024)(128)(4,1)}), s8[4194304]{0:T(1024)(128)(4,1)S(1)}, s32[]{:S(2)}) async-start(s8[8388608]{0:T(1024)(128)(4,1)} %bitcast.15), calls=%async_computation | async-start | bytes 8388608
  36.3 1.8 %collective-permute-start.10 = (f32[4,16,1536]{2,1,0:T(8,128)S(1)}, f32[4,16,1536]{2,1,0:T(8,128)S(1)}, u32[]{:S(2)}, u32[]{:S(2)}) collective-permute-start(f32[4,16,1536]{2,1,0:T(8,128)S(1)} %get-tuple-element.19), channel_id=1, source_target_pairs={{0,1},{1,0},{2,3},{3,2},{4,5},{5,4},{6,7},{7,6},{8,9},{9,8},{10,11... | collective-permute-start | bytes 1179656 | tf_op jit(solution)/shard_map/ppermute | solution.py:249
  38.1 4.8 %collective-permute-start.11 = (f32[16,1536]{1,0:T(8,128)S(1)}, f32[16,1536]{1,0:T(8,128)S(1)}, u32[]{:S(2)}, u32[]{:S(2)}) collective-permute-start(f32[16,1536]{1,0:T(8,128)S(1)} %get-tuple-element.28), channel_id=1, source_target_pairs={{0,3},{1,2},{2,1},{3,0},{16,19},{17,18},{18,17},{19,16},{4,7},{5,6... | collective-permute-start | bytes 294920 | tf_op jit(solution)/shard_map/ppermute | solution.py:249
  39.1 4.6 %collective-permute-start.12 = (f32[16,1536]{1,0:T(8,128)S(1)}, f32[16,1536]{1,0:T(8,128)S(1)}, u32[]{:S(2)}, u32[]{:S(2)}) collective-permute-start(f32[16,1536]{1,0:T(8,128)S(1)} %get-tuple-element.26), channel_id=1, source_target_pairs={{0,17},{1,16},{2,19},{3,18},{16,1},{17,0},{18,3},{19,2},{4,21},{5,... | collective-permute-start | bytes 294920 | tf_op jit(solution)/shard_map/ppermute | solution.py:249
  40.0 6.1 %collective-permute-start.13 = (f32[16,1536]{1,0:T(8,128)S(1)}, f32[16,1536]{1,0:T(8,128)S(1)}, u32[]{:S(2)}, u32[]{:S(2)}) collective-permute-start(f32[16,1536]{1,0:T(8,128)S(1)} %get-tuple-element.27), channel_id=1, source_target_pairs={{0,19},{1,18},{2,17},{3,16},{16,3},{17,2},{18,1},{19,0},{4,23},{5,... | collective-permute-start | bytes 294920 | tf_op jit(solution)/shard_map/ppermute | solution.py:249
  46.2 4.5 %collective-permute-start.14 = (f32[16,1024]{1,0:T(8,128)S(1)}, f32[16,1024]{1,0:T(8,128)S(1)}, u32[]{:S(2)}, u32[]{:S(2)}) collective-permute-start(f32[16,1024]{1,0:T(8,128)S(1)} %slice.28), channel_id=1, source_target_pairs={{0,4},{4,0},{8,12},{12,8},{1,5},{5,1},{9,13},{13,9},{2,6},{6,2},{1... | collective-permute-start | bytes 196616 | tf_op jit(solution)/shard_map/ppermute | solution.py:249
  47.1 8.4 %collective-permute-start.15 = (f32[16,1024]{1,0:T(8,128)S(1)}, f32[16,1024]{1,0:T(8,128)S(1)}, u32[]{:S(2)}, u32[]{:S(2)}) collective-permute-start(f32[16,1024]{1,0:T(8,128)S(1)} %slice.28), channel_id=1, source_target_pairs={{0,8},{4,12},{8,0},{12,4},{1,9},{5,13},{9,1},{13,5},{2,10},{6,14},... | collective-permute-start | bytes 196616 | tf_op jit(solution)/shard_map/ppermute | solution.py:249
  48.8 6.7 %collective-permute-start.16 = (f32[16,1024]{1,0:T(8,128)S(1)}, f32[16,1024]{1,0:T(8,128)S(1)}, u32[]{:S(2)}, u32[]{:S(2)}) collective-permute-start(f32[16,1024]{1,0:T(8,128)S(1)} %slice.28), channel_id=1, source_target_pairs={{0,12},{4,8},{8,4},{12,0},{1,13},{5,9},{9,5},{13,1},{2,14},{6,10},... | collective-permute-start | bytes 196616 | tf_op jit(solution)/shard_map/ppermute | solution.py:249
  55.5 6.1 %slice-start.1 = ((s8[8388608]{0:T(1024)(128)(4,1)}), s8[4194304]{0:T(1024)(128)(4,1)S(1)}, s32[]{:S(2)}) async-start(s8[8388608]{0:T(1024)(128)(4,1)} %bitcast.15), calls=%async_computation.1 | async-start | bytes 8388608
  56.0 1.3 %collective-permute-start.17 = (f32[1,16,1024]{2,1,0:T(8,128)S(1)}, f32[1,16,1024]{2,1,0:T(8,128)S(1)}, u32[]{:S(2)}, u32[]{:S(2)}) collective-permute-start(f32[1,16,1024]{2,1,0:T(8,128)S(1)} %shard_map.84), channel_id=1, source_target_pairs={{0,1},{1,0},{2,3},{3,2},{4,5},{5,4},{6,7},{7,6},{8,9},{9,8},{10,11... | collective-permute-start | bytes 196616 | tf_op jit(solution)/shard_map/ppermute | solution.py:249
  57.2 4.1 %collective-permute-start.18 = (f32[1,16,1024]{2,1,0:T(8,128)S(1)}, f32[1,16,1024]{2,1,0:T(8,128)S(1)}, u32[]{:S(2)}, u32[]{:S(2)}) collective-permute-start(f32[1,16,1024]{2,1,0:T(8,128)S(1)} %add.56), channel_id=1, source_target_pairs={{0,3},{1,2},{2,1},{3,0},{4,7},{5,6},{6,5},{7,4},{8,11},{9,10},{10,... | collective-permute-start | bytes 196616 | tf_op jit(solution)/shard_map/ppermute | solution.py:249
  61.4 1.3 %collective-permute-start.19 = (f32[1,16,1024]{2,1,0:T(8,128)S(1)}, f32[1,16,1024]{2,1,0:T(8,128)S(1)}, u32[]{:S(2)}, u32[]{:S(2)}) collective-permute-start(f32[1,16,1024]{2,1,0:T(8,128)S(1)} %add.57.pull), channel_id=1, source_target_pairs={{0,1},{1,0},{2,3},{3,2},{4,5},{5,4},{6,7},{7,6},{8,9},{9,8},{10,11... | collective-permute-start | bytes 196616 | tf_op jit(solution)/shard_map/ppermute | solution.py:249
  63.4 6.0 %collective-permute-start.22 = (f32[16,640]{1,0:T(8,128)S(1)}, f32[16,640]{1,0:T(8,128)S(1)}, u32[]{:S(2)}, u32[]{:S(2)}) collective-permute-start(f32[16,640]{1,0:T(8,128)S(1)} %pad_maximum_fusion.5), channel_id=1, source_target_pairs={{0,12},{4,8},{8,4},{12,0},{1,13},{5,9},{9,5},{13,1},{2,14},{6,10},... | collective-permute-start | bytes 122888 | tf_op jit(solution)/shard_map/ppermute | solution.py:249
  65.5 5.4 %collective-permute-start.21 = (f32[16,640]{1,0:T(8,128)S(1)}, f32[16,640]{1,0:T(8,128)S(1)}, u32[]{:S(2)}, u32[]{:S(2)}) collective-permute-start(f32[16,640]{1,0:T(8,128)S(1)} %pad_maximum_fusion.4), channel_id=1, source_target_pairs={{0,8},{4,12},{8,0},{12,4},{1,9},{5,13},{9,1},{13,5},{2,10},{6,14},... | collective-permute-start | bytes 122888 | tf_op jit(solution)/shard_map/ppermute | solution.py:249
  66.3 4.7 %collective-permute-start.20 = (f32[16,640]{1,0:T(8,128)S(1)}, f32[16,640]{1,0:T(8,128)S(1)}, u32[]{:S(2)}, u32[]{:S(2)}) collective-permute-start(f32[16,640]{1,0:T(8,128)S(1)} %pad_maximum_fusion.3), channel_id=1, source_target_pairs={{0,4},{4,0},{8,12},{12,8},{1,5},{5,1},{9,13},{13,9},{2,6},{6,2},{1... | collective-permute-start | bytes 122888 | tf_op jit(solution)/shard_map/ppermute | solution.py:249

commit v5 on v4

--- a/solution.py
+++ b/solution.py
@@ -13,6 +13,7 @@
 
 F32, BF16 = jnp.float32, jnp.bfloat16
 HBM = pl.BlockSpec(memory_space=pltpu.HBM)
+SCALARS = pl.BlockSpec(memory_space=pltpu.SMEM)
 WHOLE = pl.BlockSpec(memory_space=pltpu.VMEM)
 
 
@@ -123,22 +124,19 @@
     return (col + side + (chip > 0)) % CORES
 
 
-def spots(lines, side, numbers, length):
-    chips, subs, _ = numbers.shape
+def spots(table, side, chips, length):
+    count = length // BLOCK
+    for chip in range(chips):
+        for k in range(count):
+            yield chip, slice(k * BLOCK, (k + 1) * BLOCK), table[side, chip * count + k]
+
+
+def scatter_kernel(lines, near, rhs, out, table, numbers, sems):
+    chips, _, length = near.shape
+    length -= BLOCK
+    subs = numbers.shape[1]
     here = length // (subs * BLOCK)
     me = lax.axis_index("col")
-    for chip in range(chips):
-        col = (me // CORES ^ (chip % lines)) * CORES + core_of(me, side, chip)
-        role = role_of(col)
-        for slot in range(subs):
-            sub = sub_of(slot, subs // CORES, role)
-            for k in range(here):
-                at = (slot * here + k) * BLOCK
-                block = numbers[chip, sub, col * here + k].astype(jnp.int32)
-                yield chip, slice(at, at + BLOCK), block
-
-
-def scatter_kernel(lines, near, rhs, out, numbers, sems):
     copies = numbers_of(near, numbers, sems)
     for copy in copies:
         copy.start()
@@ -146,49 +144,76 @@
         out[b] = rhs[:, b * BLOCK : (b + 1) * BLOCK]
     for copy in copies:
         copy.wait()
-    for chip, lanes, block in spots(lines, 0, numbers, near.shape[2] - BLOCK):
+    for side in range(CORES):
+        for chip in range(chips):
+            col = (me // CORES ^ (chip % lines)) * CORES + core_of(me, side, chip)
+            role = role_of(col)
+            for slot in range(subs):
+                sub = sub_of(slot, subs // CORES, role)
+                for k in range(here):
+                    block = numbers[chip, sub, col * here + k].astype(jnp.int32)
+                    table[side, (chip * subs + slot) * here + k] = block
+    for chip, lanes, block in spots(table, 0, chips, length):
         out[block] -= near[chip, :, lanes]
 
 
-def separator_kernel(sizes, inside, near, far, start, sep, keep, send, *rest):
-    leaves, rows, cols, lines = sizes
-    *back, held, high, low, ours, theirs, our_sems, their_sems = rest
-    chips = far.shape[0]
+def prepare_kernel(inside, sep, both, *rest):
+    *tall, land, sem = rest
+    rows = sep.shape[0]
+    copy = pltpu.make_async_copy(sep, land, sem)
+    copy.start()
+    copy.wait()
+    both[:rows], both[rows:] = split(land[...])
+    if inside:
+        tall[0][:, :rows], tall[0][:, rows:] = split(land[...].T)
+
+
+def separator_kernel(sizes, inside, table, far, start, both, *rest):
+    *tall, send, held = rest
+    chips, nrhs, length = far.shape
+    length -= BLOCK
     total = held.shape[0]
-    length = far.shape[2] - BLOCK
-
-    copies = numbers_of(far, theirs, their_sems) + numbers_of(near, ours, our_sems)
-    for copy in copies:
-        copy.start()
+    sep_rows = both.shape[0] // 2
+
     held[...] = start[...]
-    high[...], low[...] = split(sep[...])
-    for copy in copies:
-        copy.wait()
-    for chip, lanes, block in spots(lines, 1, theirs, length):
+    for chip, lanes, block in spots(table, 1, chips, length):
         held[block] -= far[chip, :, lanes]
-    updated = jnp.concatenate([held[b] for b in range(total)], 1)
-    forward = dot3(updated, (high[...], low[...]), ROWS_OF)
-    terms = dot3(forward, (high[...], low[...]), COLUMNS_OF)
+    updated = jnp.concatenate(split(jnp.concatenate([held[b] for b in range(total)], 1)))
+    matrix, dims = (tall[0], COLUMNS_OF) if inside else (both, ROWS_OF)
+    forward = lax.dot_general(updated, matrix[...], dims, preferred_element_type=F32)
+    forward = forward[:nrhs, :sep_rows] + (forward[nrhs:, :sep_rows] + forward[:nrhs, sep_rows:])
+    high, low = split(forward)
+    parts = jnp.concatenate(
+        [jnp.concatenate([high, high], 1), jnp.concatenate([low, jnp.zeros_like(low)], 1)]
+    )
+    terms = lax.dot_general(parts, both[...], COLUMNS_OF, preferred_element_type=F32)
+    terms = terms[:nrhs] + terms[nrhs:]
     for b in range(total):
         held[b] = terms[:, b * BLOCK : (b + 1) * BLOCK]
-    for side, numbers, out in ((1, theirs, send), (0, ours, keep)):
-        for chip, lanes, block in spots(lines, side, numbers, length):
-            out[chip, :, lanes] = held[block]
+    pick(sizes, 1, inside, sep_rows, table, held, length, send)
+
+
+def keep_kernel(sizes, inside, sep_rows, length, table, held, keep):
+    pick(sizes, 0, inside, sep_rows, table, held, length, keep)
+
+
+def pick(sizes, side, inside, sep_rows, table, held, length, out):
+    _, rows, cols, lines = sizes
+    for chip, lanes, block in spots(table, side, out.shape[0], length):
+        out[chip, :, lanes] = held[block]
     if not inside:
-        back[0][...] = terms
         return
-    wide = sep.shape[0] // BLOCK
+    wide = sep_rows // BLOCK
     me = lax.axis_index("col")
     plane = lax.axis_index("leaf") * lines + me // CORES
-    for side, out in ((1, send), (0, keep)):
-        for chip in range(chips):
-            other = plane ^ chip
-            col = (other % lines) * CORES + core_of(me, side, chip)
-            for row in range(rows):
-                for w in range(wide):
-                    block = ((other // lines * rows + row) * cols + col) * wide + w
-                    at = length + (row * wide + w) * BLOCK
-                    out[chip, :, at : at + BLOCK] = held[block]
+    for chip in range(out.shape[0]):
+        other = plane ^ chip
+        col = (other % lines) * CORES + core_of(me, side, chip)
+        for row in range(rows):
+            for w in range(wide):
+                block = ((other // lines * rows + row) * cols + col) * wide + w
+                at = length + (row * wide + w) * BLOCK
+                out[chip, :, at : at + BLOCK] = held[block]
 
 
 def pull_kernel(first, pulled, update, out):
@@ -334,7 +359,21 @@
         for first, vectors in ((0, mine), (half, other))
     ]
     coupled = jnp.concatenate(coupled, 1)
-    coupled = coupled + sum(swap(coupled, "row", rows, k) for k in range(1, rows))
+    arrived = [swap(coupled, "row", rows, k) for k in range(1, rows)]
+    inside = sep_rows % BLOCK == 0
+    prepared = pl.pallas_call(
+        functools.partial(prepare_kernel, inside),
+        out_shape=[pltpu.VMEM((2 * sep_rows, width), BF16)]
+        + ([pltpu.VMEM((width, 2 * sep_rows), BF16)] if inside else []),
+        in_specs=[HBM],
+        scratch_shapes=[pltpu.VMEM(sep_inverse.shape, F32), pltpu.SemaphoreType.DMA],
+        compiler_params=pltpu.CompilerParams(vmem_limit_bytes=12 * MIB),
+        cost_estimate=pl.CostEstimate(
+            flops=0, bytes_accessed=8 * sep_inverse.size, transcendentals=0
+        ),
+    )(in_hbm(sep_inverse))
+    arrived, prepared = lax.optimization_barrier((arrived, prepared))
+    coupled = coupled + sum(arrived)
     numbers = jnp.pad(
         update_map.astype(F32), ((0, nrhs - subs), (0, BLOCK - update_map.shape[1]))
     )
@@ -345,36 +384,41 @@
     far = swap(near, "col", cols, 1)
 
     shape = (leaves, rows, cols, lines)
-    start = call(
+    size = subs * up
+    start, table = pl.pallas_call(
         functools.partial(scatter_kernel, lines),
-        jax.ShapeDtypeStruct((width // BLOCK, nrhs, BLOCK), F32),
-        [WHOLE, WHOLE],
-        4,
-        (2 * nrhs * width, 12 * nrhs * width),
-        (pltpu.SMEM((chips, subs, BLOCK), F32), pltpu.SemaphoreType.DMA((chips,))),
+        out_shape=[
+            jax.ShapeDtypeStruct((width // BLOCK, nrhs, BLOCK), F32),
+            pltpu.SMEM((CORES, chips * size // BLOCK), jnp.int32),
+        ],
+        in_specs=[WHOLE, WHOLE],
+        out_specs=[WHOLE, SCALARS],
+        scratch_shapes=[pltpu.SMEM((chips, subs, BLOCK), F32), pltpu.SemaphoreType.DMA((chips,))],
+        compiler_params=pltpu.CompilerParams(vmem_limit_bytes=4 * MIB),
+        cost_estimate=pl.CostEstimate(
+            flops=2 * nrhs * width, bytes_accessed=12 * nrhs * width, transcendentals=0
+        ),
     )(near, sep_rhs)
-    inside = sep_rows % BLOCK == 0
+    table = pltpu.with_memory_space_constraint(table, pltpu.SMEM)
     own_width = rows * sep_rows
-    length = subs * up + (own_width if inside else 0)
+    length = size + (own_width if inside else 0)
     piece = jax.ShapeDtypeStruct((chips, nrhs, length), F32)
-    keep, send, *back = call(
+    send, held = call(
         functools.partial(separator_kernel, shape, inside),
-        (piece, piece) + (() if inside else (jax.ShapeDtypeStruct((nrhs, width), F32),)),
-        [WHOLE] * 4,
+        (piece, jax.ShapeDtypeStruct((width // BLOCK, nrhs, BLOCK), F32)),
+        [SCALARS] + [WHOLE] * (2 + len(prepared)),
         12,
         (4 * nrhs * sep_inverse.size, 4 * sep_inverse.size),
-        (
-            pltpu.VMEM((width // BLOCK, nrhs, BLOCK), F32),
-            pltpu.VMEM(sep_inverse.shape, BF16),
-            pltpu.VMEM(sep_inverse.shape, BF16),
-            pltpu.SMEM((chips, subs, BLOCK), F32),
-            pltpu.SMEM((chips, subs, BLOCK), F32),
-            pltpu.SemaphoreType.DMA((chips,)),
-            pltpu.SemaphoreType.DMA((chips,)),
-        ),
-    )(near, far, start, sep_inverse)
+    )(table, far, start, *map(in_vmem, prepared))
+    keep = call(
+        functools.partial(keep_kernel, shape, inside, sep_rows, size),
+        piece,
+        [SCALARS, WHOLE],
+        4,
+        (0, 8 * piece.size),
+    )(table, held)
     if not inside:
-        own = back[0].reshape(nrhs, leaves, rows, lines, CORES, sep_rows)
+        own = held.transpose(1, 0, 2).reshape(nrhs, leaves, rows, lines, CORES, sep_rows)
         own = own.transpose(4, 1, 3, 0, 2, 5).reshape(CORES, chips, nrhs, own_width)
         own = picked(picked(own, 0, core, CORES), 1, plane, chips)
         own = [jnp.concatenate([own[i][:1], own[1 - i][1:]]) for i in range(CORES)]

time: 71.8 us -> 70.8 us (0.986)
  waiting for transfers between devices: 30.9 us -> 28.1 us
  Pallas kernels: 14.9 us -> 16.7 us
    ppermute x23, waiting for transfers between devices: 30.9 us -> 28.1 us  [swap(): return lax.ppermute(value, axes, [(i, i ^ mask) for i in range(size)])]
    pallas_call x2 -> x4, Pallas kernels: 3.37 us -> 5.15 us  [the longest x1 2.62 us: body(): pl.pallas_call(functools.partial(prepare_kernel, inside), out_shape=[pltp...]
  transfers between devices with their start and end apart: 23 -> 23, of which waited for: 19 -> 18; matrix products, arithmetic and copies ran while one was open for 0% -> 0% of each run, Pallas kernels for 8% -> 12%
where the time goes in v5:
time: 70.8 us; the launch traced here: 70.6 us
  waiting for transfers between devices  28.1 us (40%)
  starting transfers between devices  24.7 us (35%)
  Pallas kernels  16.7 us (24%)
  between operations  0.86 us (1%)
    ppermute x23, waiting for transfers between devices, swap(): return lax.ppermute(value, axes, [(i, i ^ mask) for i in range(size)])  28.1 us
    ppermute x23, starting transfers between devices, swap(): return lax.ppermute(value, axes, [(i, i ^ mask) for i in range(size)])  24.7 us
    pallas_call x1, Pallas kernels, body(): call(leaf_kernel, (pltpu.VMEM(vec.shape, F32), pltpu.VMEM(vec.shape, F32)...  4.49 us
    pallas_call x1, Pallas kernels, body(): pl.pallas_call(functools.partial(prepare_kernel, inside), out_shape=[pltp...  2.62 us
    pallas_call x1, Pallas kernels, beside(): pl.pallas_call(load_kernel, out_shape=pltpu.VMEM(value.shape, value.dtype...  2.24 us
    pallas_call x4, Pallas kernels, parts_of(): call(functools.partial(solve_parts_kernel, rows, masks, first), (jax.Shap...  1.91 us
    pallas_call x1, Pallas kernels, body(): call(functools.partial(separator_kernel, shape, inside), (piece, jax.Shap...  1.44 us
  transfers between devices with their start and end apart: 23, of which 18 were waited for; matrix products, arithmetic and copies ran while one was open for 0% of the time, Pallas kernels for 12%

profile of v5, /device:TPU:0, one launch (start us, length us, event | category | flops | bytes accessed | tf_op | source)
XLA Modules:
  0.0 70.6 jit_solution(14982951827183921425)
XLA Ops:
  0.6 4.5 %shard_map.77 = (f32[1,16,1024]{2,1,0:T(8,128)S(1)}, f32[1,16,1024]{2,1,0:T(8,128)S(1)}) custom-call(f32[2,16,1024]{2,1,0:T(8,128)} %rhs.2, f32[2,1024,1024]{2,1,0:T(8,128)} %inverse.9), custom_call_target="tpu_custom_call" | custom-call | flops 67108864 | bytes 8388608 | tf_op jit(solution)/shard_map/pallas_call | solution.py:334
  5.1 0.5 collective-permute-start
  5.6 0.9 %collective-permute-done = f32[1,16,1024]{2,1,0:T(8,128)S(1)} collective-permute-done((f32[1,16,1024]{2,1,0:T(8,128)S(1)}, f32[1,16,1024]{2,1,0:T(8,128)S(1)}, u32[]{:S(2)}, u32[]{:S(2)}) %collective-permute-start) | collective-permute-done | bytes 65568 | tf_op jit(solution)/shard_map/ppermute | solution.py:274
  6.6 2.7 %collective-permute-start.1 = (f32[1,16,1024]{2,1,0:T(8,128)S(1)}, f32[1,16,1024]{2,1,0:T(8,128)S(1)}, u32[]{:S(2)}, u32[]{:S(2)}) collective-permute-start(f32[1,16,1024]{2,1,0:T(8,128)S(1)} %add.44), channel_id=1, source_target_pairs={{0,3},{1,2},{2,1},{3,0},{4,7},{5,6},{6,5},{7,4},{8,11},{9,10},{10,... | collective-permute-start | bytes 196616 | tf_op jit(solution)/shard_map/ppermute | solution.py:274
  9.3 2.2 %shard_map.78.update = f32[2,512,1024]{2,1,0:T(8,128)S(1)} custom-call(f32[2,512,1024]{2,1,0:T(8,128)} %update.3), custom_call_target="tpu_custom_call" | custom-call | bytes 4194304 | tf_op jit(solution)/shard_map/pallas_call | solution.py:284
  11.5 0.4 collective-permute-start.2
  12.0 0.7 shard_map.79
  12.6 0.2 collective-permute-done.2.vectors
  12.9 0.7 shard_map.80
  13.6 4.2 %collective-permute-start.5 = (f32[16,1024]{1,0:T(8,128)S(1)}, f32[16,1024]{1,0:T(8,128)S(1)}, u32[]{:S(2)}, u32[]{:S(2)}) collective-permute-start(f32[16,1024]{1,0:T(8,128)S(1)} %pad_maximum_fusion.1), channel_id=1, source_target_pairs={{0,12},{4,8},{8,4},{12,0},{1,13},{5,9},{9,5},{13,1},{2,14},{6,10},... | collective-permute-start | bytes 196616 | tf_op jit(solution)/shard_map/ppermute | solution.py:274
  17.7 0.6 collective-permute-start.3
  18.4 2.6 %shard_map.81 = (bf16[256,4096]{1,0:T(8,128)(2,1)S(1)}, bf16[4096,256]{1,0:T(8,128)(2,1)S(1)}) custom-call(f32[128,4096]{1,0:T(8,128)} %sep.1), custom_call_target="tpu_custom_call" | custom-call | bytes 4194304 | tf_op jit(solution)/shard_map/pallas_call | solution.py:364
  21.0 2.6 %collective-permute-done.4 = f32[16,1024]{1,0:T(8,128)S(1)} collective-permute-done((f32[16,1024]{1,0:T(8,128)S(1)}, f32[16,1024]{1,0:T(8,128)S(1)}, u32[]{:S(2)}, u32[]{:S(2)}) %collective-permute-start.4) | collective-permute-done | bytes 65568 | tf_op jit(solution)/shard_map/ppermute | solution.py:274
  23.7 0.9 %collective-permute-start.7 = (f32[16,1152]{1,0:T(8,128)S(1)}, f32[16,1152]{1,0:T(8,128)S(1)}, u32[]{:S(2)}, u32[]{:S(2)}) collective-permute-start(f32[16,1152]{1,0:T(8,128)S(1)} %get-tuple-element.48), channel_id=1, source_target_pairs={{0,17},{1,16},{2,19},{3,18},{16,1},{17,0},{18,3},{19,2},{4,21},{5,... | collective-permute-start | bytes 221192 | tf_op jit(solution)/shard_map/ppermute | solution.py:274
  24.5 1.9 %collective-permute-start.6 = (f32[16,1152]{1,0:T(8,128)S(1)}, f32[16,1152]{1,0:T(8,128)S(1)}, u32[]{:S(2)}, u32[]{:S(2)}) collective-permute-start(f32[16,1152]{1,0:T(8,128)S(1)} %get-tuple-element.48), channel_id=1, source_target_pairs={{0,3},{1,2},{2,1},{3,0},{16,19},{17,18},{18,17},{19,16},{4,7},{5,6... | collective-permute-start | bytes 221192 | tf_op jit(solution)/shard_map/ppermute | solution.py:274
  26.5 1.8 %collective-permute-done.7 = f32[16,1152]{1,0:T(8,128)S(1)} collective-permute-done((f32[16,1152]{1,0:T(8,128)S(1)}, f32[16,1152]{1,0:T(8,128)S(1)}, u32[]{:S(2)}, u32[]{:S(2)}) %collective-permute-start.7) | collective-permute-done | bytes 73760 | tf_op jit(solution)/shard_map/ppermute | solution.py:274
  28.2 0.2 collective-permute-done.6
  28.5 3.3 %collective-permute-done.8 = f32[16,1152]{1,0:T(8,128)S(1)} collective-permute-done((f32[16,1152]{1,0:T(8,128)S(1)}, f32[16,1152]{1,0:T(8,128)S(1)}, u32[]{:S(2)}, u32[]{:S(2)}) %collective-permute-start.8) | collective-permute-done | bytes 73760 | tf_op jit(solution)/shard_map/ppermute | solution.py:274
  31.9 1.0 %shard_map.82 = (f32[32,16,128]{2,1,0:T(8,128)S(1)}, s32[2,32]{1,0:T(2,128)S(4)}) custom-call(f32[4,16,1152]{2,1,0:T(8,128)S(1)} %pad_maximum_fusion.near, f32[16,4096]{1,0:T(8,128)S(1)} %copy-done.1), custom_call_target="tpu_custom_call" | custom-call | flops 131072 | bytes 786432 | tf_op jit(solution)/shard_map/pallas_call | solution.py:388
  33.0 0.5 collective-permute-done.9.far
  33.5 1.4 %shard_map.83 = (f32[4,16,1536]{2,1,0:T(8,128)S(1)}, f32[32,16,128]{2,1,0:T(8,128)S(1)}) custom-call(s32[2,32]{1,0:T(2,128)S(4)} %get-tuple-element.32.table, f32[4,16,1152]{2,1,0:T(8,128)S(1)} %collective-permute-done.9.far, f32[32,16,128]{2,1,0:T(8,128)S(1)} %get-tuple-element.33.start, bf16[256,4096]{1,0:T(8,128)(2,1)S(1)} %get-tuple-element.34.both, ...), custom_call_target="tpu_custom_call" | custom-call | flops 33554432 | bytes 2097152 | tf_op jit(solution)/shard_map/pallas_call | solution.py:406
  34.9 0.2 collective-permute-start.10
  35.2 1.5 %collective-permute-done.10 = f32[4,16,1536]{2,1,0:T(8,128)S(1)} collective-permute-done((f32[4,16,1536]{2,1,0:T(8,128)S(1)}, f32[4,16,1536]{2,1,0:T(8,128)S(1)}, u32[]{:S(2)}, u32[]{:S(2)}) %collective-permute-start.10) | collective-permute-done | bytes 393248 | tf_op jit(solution)/shard_map/ppermute | solution.py:274
  36.8 0.3 collective-permute-start.12
  37.1 1.4 %collective-permute-start.13 = (f32[16,1536]{1,0:T(8,128)S(1)}, f32[16,1536]{1,0:T(8,128)S(1)}, u32[]{:S(2)}, u32[]{:S(2)}) collective-permute-start(f32[16,1536]{1,0:T(8,128)S(1)} %get-tuple-element.45), channel_id=1, source_target_pairs={{0,19},{1,18},{2,17},{3,16},{16,3},{17,2},{18,1},{19,0},{4,23},{5,... | collective-permute-start | bytes 294920 | tf_op jit(solution)/shard_map/ppermute | solution.py:274
  38.6 1.2 %collective-permute-start.11 = (f32[16,1536]{1,0:T(8,128)S(1)}, f32[16,1536]{1,0:T(8,128)S(1)}, u32[]{:S(2)}, u32[]{:S(2)}) collective-permute-start(f32[16,1536]{1,0:T(8,128)S(1)} %get-tuple-element.46), channel_id=1, source_target_pairs={{0,3},{1,2},{2,1},{3,0},{16,19},{17,18},{18,17},{19,16},{4,7},{5,6... | collective-permute-start | bytes 294920 | tf_op jit(solution)/shard_map/ppermute | solution.py:274
  39.8 1.8 %collective-permute-done.12 = f32[16,1536]{1,0:T(8,128)S(1)} collective-permute-done((f32[16,1536]{1,0:T(8,128)S(1)}, f32[16,1536]{1,0:T(8,128)S(1)}, u32[]{:S(2)}, u32[]{:S(2)}) %collective-permute-start.12) | collective-permute-done | bytes 98336 | tf_op jit(solution)/shard_map/ppermute | solution.py:274
  41.6 2.2 %collective-permute-done.13 = f32[16,1536]{1,0:T(8,128)S(1)} collective-permute-done((f32[16,1536]{1,0:T(8,128)S(1)}, f32[16,1536]{1,0:T(8,128)S(1)}, u32[]{:S(2)}, u32[]{:S(2)}) %collective-permute-start.13) | collective-permute-done | bytes 98336 | tf_op jit(solution)/shard_map/ppermute | solution.py:274
  43.8 1.8 %collective-permute-done.11 = f32[16,1536]{1,0:T(8,128)S(1)} collective-permute-done((f32[16,1536]{1,0:T(8,128)S(1)}, f32[16,1536]{1,0:T(8,128)S(1)}, u32[]{:S(2)}, u32[]{:S(2)}) %collective-permute-start.11) | collective-permute-done | bytes 98336 | tf_op jit(solution)/shard_map/ppermute | solution.py:274
  45.6 2.5 %collective-permute-start.16 = (f32[16,1024]{1,0:T(8,128)S(1)}, f32[16,1024]{1,0:T(8,128)S(1)}, u32[]{:S(2)}, u32[]{:S(2)}) collective-permute-start(f32[16,1024]{1,0:T(8,128)S(1)} %slice.28), channel_id=1, source_target_pairs={{0,12},{4,8},{8,4},{12,0},{1,13},{5,9},{9,5},{13,1},{2,14},{6,10},... | collective-permute-start | bytes 196616 | tf_op jit(solution)/shard_map/ppermute | solution.py:274
  48.3 1.8 %collective-permute-start.14 = (f32[16,1024]{1,0:T(8,128)S(1)}, f32[16,1024]{1,0:T(8,128)S(1)}, u32[]{:S(2)}, u32[]{:S(2)}) collective-permute-start(f32[16,1024]{1,0:T(8,128)S(1)} %slice.28), channel_id=1, source_target_pairs={{0,4},{4,0},{8,12},{12,8},{1,5},{5,1},{9,13},{13,9},{2,6},{6,2},{1... | collective-permute-start | bytes 196616 | tf_op jit(solution)/shard_map/ppermute | solution.py:274
  50.1 2.3 %collective-permute-done.16 = f32[16,1024]{1,0:T(8,128)S(1)} collective-permute-done((f32[16,1024]{1,0:T(8,128)S(1)}, f32[16,1024]{1,0:T(8,128)S(1)}, u32[]{:S(2)}, u32[]{:S(2)}) %collective-permute-start.16) | collective-permute-done | bytes 65568 | tf_op jit(solution)/shard_map/ppermute | solution.py:274
  52.4 2.3 %collective-permute-done.15 = f32[16,1024]{1,0:T(8,128)S(1)} collective-permute-done((f32[16,1024]{1,0:T(8,128)S(1)}, f32[16,1024]{1,0:T(8,128)S(1)}, u32[]{:S(2)}, u32[]{:S(2)}) %collective-permute-start.15) | collective-permute-done | bytes 65568 | tf_op jit(solution)/shard_map/ppermute | solution.py:274
  54.8 0.5 shard_map.86
  55.3 0.5 shard_map.85
  55.7 0.8 %collective-permute-done.17 = f32[1,16,1024]{2,1,0:T(8,128)S(1)} collective-permute-done((f32[1,16,1024]{2,1,0:T(8,128)S(1)}, f32[1,16,1024]{2,1,0:T(8,128)S(1)}, u32[]{:S(2)}, u32[]{:S(2)}) %collective-permute-start.17) | collective-permute-done | bytes 65568 | tf_op jit(solution)/shard_map/ppermute | solution.py:274
  56.5 1.0 %collective-permute-start.18 = (f32[1,16,1024]{2,1,0:T(8,128)S(1)}, f32[1,16,1024]{2,1,0:T(8,128)S(1)}, u32[]{:S(2)}, u32[]{:S(2)}) collective-permute-start(f32[1,16,1024]{2,1,0:T(8,128)S(1)} %add.56), channel_id=1, source_target_pairs={{0,3},{1,2},{2,1},{3,0},{4,7},{5,6},{6,5},{7,4},{8,11},{9,10},{10,... | collective-permute-start | bytes 196616 | tf_op jit(solution)/shard_map/ppermute | solution.py:274
  57.5 3.1 %collective-permute-done.18 = f32[1,16,1024]{2,1,0:T(8,128)S(1)} collective-permute-done((f32[1,16,1024]{2,1,0:T(8,128)S(1)}, f32[1,16,1024]{2,1,0:T(8,128)S(1)}, u32[]{:S(2)}, u32[]{:S(2)}) %collective-permute-start.18) | collective-permute-done | bytes 65568 | tf_op jit(solution)/shard_map/ppermute | solution.py:274
  60.7 0.2 collective-permute-start.19
  60.9 0.3 shard_map.87
  61.2 0.7 shard_map.89
  62.0 0.7 shard_map.90
  62.7 2.2 %collective-permute-start.22 = (f32[16,640]{1,0:T(8,128)S(1)}, f32[16,640]{1,0:T(8,128)S(1)}, u32[]{:S(2)}, u32[]{:S(2)}) collective-permute-start(f32[16,640]{1,0:T(8,128)S(1)} %pad_maximum_fusion.5), channel_id=1, source_target_pairs={{0,12},{4,8},{8,4},{12,0},{1,13},{5,9},{9,5},{13,1},{2,14},{6,10},... | collective-permute-start | bytes 122888 | tf_op jit(solution)/shard_map/ppermute | solution.py:274
  64.9 2.2 %collective-permute-start.20 = (f32[16,640]{1,0:T(8,128)S(1)}, f32[16,640]{1,0:T(8,128)S(1)}, u32[]{:S(2)}, u32[]{:S(2)}) collective-permute-start(f32[16,640]{1,0:T(8,128)S(1)} %pad_maximum_fusion.3), channel_id=1, source_target_pairs={{0,4},{4,0},{8,12},{12,8},{1,5},{5,1},{9,13},{13,9},{2,6},{6,2},{1... | collective-permute-start | bytes 122888 | tf_op jit(solution)/shard_map/ppermute | solution.py:274
  67.1 0.3 shard_map.88
  67.4 1.3 %collective-permute-done.22.refs_3_ = f32[16,640]{1,0:T(8,128)S(1)} collective-permute-done((f32[16,640]{1,0:T(8,128)S(1)}, f32[16,640]{1,0:T(8,128)S(1)}, u32[]{:S(2)}, u32[]{:S(2)}) %collective-permute-start.22) | collective-permute-done | bytes 40992 | tf_op jit(solution)/shard_map/ppermute | solution.py:274
  68.7 1.3 %collective-permute-done.21.refs_2_ = f32[16,640]{1,0:T(8,128)S(1)} collective-permute-done((f32[16,640]{1,0:T(8,128)S(1)}, f32[16,640]{1,0:T(8,128)S(1)}, u32[]{:S(2)}, u32[]{:S(2)}) %collective-permute-start.21) | collective-permute-done | bytes 40992 | tf_op jit(solution)/shard_map/ppermute | solution.py:274
  70.0 0.6 shard_map.91
  (43 shorter events, 0.6 us)
Async XLA Ops:
  5.1 1.4 %collective-permute-start = (f32[1,16,1024]{2,1,0:T(8,128)S(1)}, f32[1,16,1024]{2,1,0:T(8,128)S(1)}, u32[]{:S(2)}, u32[]{:S(2)}) collective-permute-start(f32[1,16,1024]{2,1,0:T(8,128)S(1)} %get-tuple-element.24), channel_id=1, source_target_pairs={{0,1},{1,0},{2,3},{3,2},{4,5},{5,4},{6,7},{7,6},{8,9},{9,8},{10,11... | collective-permute-start | bytes 196616 | tf_op jit(solution)/shard_map/ppermute | solution.py:274
  6.6 4.9 %collective-permute-start.1 = (f32[1,16,1024]{2,1,0:T(8,128)S(1)}, f32[1,16,1024]{2,1,0:T(8,128)S(1)}, u32[]{:S(2)}, u32[]{:S(2)}) collective-permute-start(f32[1,16,1024]{2,1,0:T(8,128)S(1)} %add.44), channel_id=1, source_target_pairs={{0,3},{1,2},{2,1},{3,0},{4,7},{5,6},{6,5},{7,4},{8,11},{9,10},{10,... | collective-permute-start | bytes 196616 | tf_op jit(solution)/shard_map/ppermute | solution.py:274
  11.5 6.8 %copy-start.2 = (s32[2,16]{1,0:T(2,128)S(1)}, s32[2,16]{1,0:T(2,128)}, u32[]{:S(2)}) copy-start(s32[2,16]{1,0:T(2,128)} %param.9) | copy-start | bytes 388
  11.5 1.3 %collective-permute-start.2 = (f32[1,16,1024]{2,1,0:T(8,128)S(1)}, f32[1,16,1024]{2,1,0:T(8,128)S(1)}, u32[]{:S(2)}, u32[]{:S(2)}) collective-permute-start(f32[1,16,1024]{2,1,0:T(8,128)S(1)} %add.45.vectors), channel_id=1, source_target_pairs={{0,1},{1,0},{2,3},{3,2},{4,5},{5,4},{6,7},{7,6},{8,9},{9,8},{10,11... | collective-permute-start | bytes 196616 | tf_op jit(solution)/shard_map/ppermute | solution.py:274
  12.6 19.3 %copy-start.1 = (f32[16,4096]{1,0:T(8,128)S(1)}, f32[16,4096]{1,0:T(8,128)}, u32[]{:S(2)}) copy-start(f32[16,4096]{1,0:T(8,128)} %rhs.3) | copy-start | bytes 786436
  13.6 7.5 %collective-permute-start.5 = (f32[16,1024]{1,0:T(8,128)S(1)}, f32[16,1024]{1,0:T(8,128)S(1)}, u32[]{:S(2)}, u32[]{:S(2)}) collective-permute-start(f32[16,1024]{1,0:T(8,128)S(1)} %pad_maximum_fusion.1), channel_id=1, source_target_pairs={{0,12},{4,8},{8,4},{12,0},{1,13},{5,9},{9,5},{13,1},{2,14},{6,10},... | collective-permute-start | bytes 196616 | tf_op jit(solution)/shard_map/ppermute | solution.py:274
  17.7 5.9 %collective-permute-start.4 = (f32[16,1024]{1,0:T(8,128)S(1)}, f32[16,1024]{1,0:T(8,128)S(1)}, u32[]{:S(2)}, u32[]{:S(2)}) collective-permute-start(f32[16,1024]{1,0:T(8,128)S(1)} %pad_maximum_fusion.1), channel_id=1, source_target_pairs={{0,8},{4,12},{8,0},{12,4},{1,9},{5,13},{9,1},{13,5},{2,10},{6,14},... | collective-permute-start | bytes 196616 | tf_op jit(solution)/shard_map/ppermute | solution.py:274
  17.7 5.9 %collective-permute-start.3 = (f32[16,1024]{1,0:T(8,128)S(1)}, f32[16,1024]{1,0:T(8,128)S(1)}, u32[]{:S(2)}, u32[]{:S(2)}) collective-permute-start(f32[16,1024]{1,0:T(8,128)S(1)} %pad_maximum_fusion.1), channel_id=1, source_target_pairs={{0,4},{4,0},{8,12},{12,8},{1,5},{5,1},{9,13},{13,9},{2,6},{6,2},{1... | collective-permute-start | bytes 196616 | tf_op jit(solution)/shard_map/ppermute | solution.py:274
  23.7 4.6 %collective-permute-start.7 = (f32[16,1152]{1,0:T(8,128)S(1)}, f32[16,1152]{1,0:T(8,128)S(1)}, u32[]{:S(2)}, u32[]{:S(2)}) collective-permute-start(f32[16,1152]{1,0:T(8,128)S(1)} %get-tuple-element.48), channel_id=1, source_target_pairs={{0,17},{1,16},{2,19},{3,18},{16,1},{17,0},{18,3},{19,2},{4,21},{5,... | collective-permute-start | bytes 221192 | tf_op jit(solution)/shard_map/ppermute | solution.py:274
  24.5 4.0 %collective-permute-start.6 = (f32[16,1152]{1,0:T(8,128)S(1)}, f32[16,1152]{1,0:T(8,128)S(1)}, u32[]{:S(2)}, u32[]{:S(2)}) collective-permute-start(f32[16,1152]{1,0:T(8,128)S(1)} %get-tuple-element.48), channel_id=1, source_target_pairs={{0,3},{1,2},{2,1},{3,0},{16,19},{17,18},{18,17},{19,16},{4,7},{5,6... | collective-permute-start | bytes 221192 | tf_op jit(solution)/shard_map/ppermute | solution.py:274
  26.5 5.4 %collective-permute-start.8 = (f32[16,1152]{1,0:T(8,128)S(1)}, f32[16,1152]{1,0:T(8,128)S(1)}, u32[]{:S(2)}, u32[]{:S(2)}) collective-permute-start(f32[16,1152]{1,0:T(8,128)S(1)} %get-tuple-element.48), channel_id=1, source_target_pairs={{0,19},{1,18},{2,17},{3,16},{16,3},{17,2},{18,1},{19,0},{4,23},{5,... | collective-permute-start | bytes 221192 | tf_op jit(solution)/shard_map/ppermute | solution.py:274
  31.8 1.6 %collective-permute-start.9 = (f32[4,16,1152]{2,1,0:T(8,128)S(1)}, f32[4,16,1152]{2,1,0:T(8,128)S(1)}, u32[]{:S(2)}, u32[]{:S(2)}) collective-permute-start(f32[4,16,1152]{2,1,0:T(8,128)S(1)} %pad_maximum_fusion.near), channel_id=1, source_target_pairs={{0,1},{1,0},{2,3},{3,2},{4,5},{5,4},{6,7},{7,6},{8,9},{9,8},{10,11... | collective-permute-start | bytes 884744 | tf_op jit(solution)/shard_map/ppermute | solution.py:274
  32.9 21.8 %copy-start = (f32[2,512,1024]{2,1,0:T(8,128)S(1)}, f32[2,512,1024]{2,1,0:T(8,128)}, u32[]{:S(2)}) copy-start(f32[2,512,1024]{2,1,0:T(8,128)} %update.3) | copy-start | bytes 12582916
  33.5 27.4 %slice-start = ((s8[8388608]{0:T(1024)(128)(4,1)}), s8[4194304]{0:T(1024)(128)(4,1)S(1)}, s32[]{:S(2)}) async-start(s8[8388608]{0:T(1024)(128)(4,1)} %bitcast.15), calls=%async_computation | async-start | bytes 8388608
  34.9 1.8 %collective-permute-start.10 = (f32[4,16,1536]{2,1,0:T(8,128)S(1)}, f32[4,16,1536]{2,1,0:T(8,128)S(1)}, u32[]{:S(2)}, u32[]{:S(2)}) collective-permute-start(f32[4,16,1536]{2,1,0:T(8,128)S(1)} %get-tuple-element.37), channel_id=1, source_target_pairs={{0,1},{1,0},{2,3},{3,2},{4,5},{5,4},{6,7},{7,6},{8,9},{9,8},{10,11... | collective-permute-start | bytes 1179656 | tf_op jit(solution)/shard_map/ppermute | solution.py:274
  36.8 4.8 %collective-permute-start.12 = (f32[16,1536]{1,0:T(8,128)S(1)}, f32[16,1536]{1,0:T(8,128)S(1)}, u32[]{:S(2)}, u32[]{:S(2)}) collective-permute-start(f32[16,1536]{1,0:T(8,128)S(1)} %get-tuple-element.44), channel_id=1, source_target_pairs={{0,17},{1,16},{2,19},{3,18},{16,1},{17,0},{18,3},{19,2},{4,21},{5,... | collective-permute-start | bytes 294920 | tf_op jit(solution)/shard_map/ppermute | solution.py:274
  37.1 6.7 %collective-permute-start.13 = (f32[16,1536]{1,0:T(8,128)S(1)}, f32[16,1536]{1,0:T(8,128)S(1)}, u32[]{:S(2)}, u32[]{:S(2)}) collective-permute-start(f32[16,1536]{1,0:T(8,128)S(1)} %get-tuple-element.45), channel_id=1, source_target_pairs={{0,19},{1,18},{2,17},{3,16},{16,3},{17,2},{18,1},{19,0},{4,23},{5,... | collective-permute-start | bytes 294920 | tf_op jit(solution)/shard_map/ppermute | solution.py:274
  38.6 7.0 %collective-permute-start.11 = (f32[16,1536]{1,0:T(8,128)S(1)}, f32[16,1536]{1,0:T(8,128)S(1)}, u32[]{:S(2)}, u32[]{:S(2)}) collective-permute-start(f32[16,1536]{1,0:T(8,128)S(1)} %get-tuple-element.46), channel_id=1, source_target_pairs={{0,3},{1,2},{2,1},{3,0},{16,19},{17,18},{18,17},{19,16},{4,7},{5,6... | collective-permute-start | bytes 294920 | tf_op jit(solution)/shard_map/ppermute | solution.py:274
  45.6 6.8 %collective-permute-start.16 = (f32[16,1024]{1,0:T(8,128)S(1)}, f32[16,1024]{1,0:T(8,128)S(1)}, u32[]{:S(2)}, u32[]{:S(2)}) collective-permute-start(f32[16,1024]{1,0:T(8,128)S(1)} %slice.28), channel_id=1, source_target_pairs={{0,12},{4,8},{8,4},{12,0},{1,13},{5,9},{9,5},{13,1},{2,14},{6,10},... | collective-permute-start | bytes 196616 | tf_op jit(solution)/shard_map/ppermute | solution.py:274
  48.2 6.6 %collective-permute-start.15 = (f32[16,1024]{1,0:T(8,128)S(1)}, f32[16,1024]{1,0:T(8,128)S(1)}, u32[]{:S(2)}, u32[]{:S(2)}) collective-permute-start(f32[16,1024]{1,0:T(8,128)S(1)} %slice.28), channel_id=1, source_target_pairs={{0,8},{4,12},{8,0},{12,4},{1,9},{5,13},{9,1},{13,5},{2,10},{6,14},... | collective-permute-start | bytes 196616 | tf_op jit(solution)/shard_map/ppermute | solution.py:274
  48.3 6.5 %collective-permute-start.14 = (f32[16,1024]{1,0:T(8,128)S(1)}, f32[16,1024]{1,0:T(8,128)S(1)}, u32[]{:S(2)}, u32[]{:S(2)}) collective-permute-start(f32[16,1024]{1,0:T(8,128)S(1)} %slice.28), channel_id=1, source_target_pairs={{0,4},{4,0},{8,12},{12,8},{1,5},{5,1},{9,13},{13,9},{2,6},{6,2},{1... | collective-permute-start | bytes 196616 | tf_op jit(solution)/shard_map/ppermute | solution.py:274
  54.8 6.1 %slice-start.1 = ((s8[8388608]{0:T(1024)(128)(4,1)}), s8[4194304]{0:T(1024)(128)(4,1)S(1)}, s32[]{:S(2)}) async-start(s8[8388608]{0:T(1024)(128)(4,1)} %bitcast.15), calls=%async_computation.1 | async-start | bytes 8388608
  55.3 1.3 %collective-permute-start.17 = (f32[1,16,1024]{2,1,0:T(8,128)S(1)}, f32[1,16,1024]{2,1,0:T(8,128)S(1)}, u32[]{:S(2)}, u32[]{:S(2)}) collective-permute-start(f32[1,16,1024]{2,1,0:T(8,128)S(1)} %shard_map.86), channel_id=1, source_target_pairs={{0,1},{1,0},{2,3},{3,2},{4,5},{5,4},{6,7},{7,6},{8,9},{9,8},{10,11... | collective-permute-start | bytes 196616 | tf_op jit(solution)/shard_map/ppermute | solution.py:274
  56.5 4.1 %collective-permute-start.18 = (f32[1,16,1024]{2,1,0:T(8,128)S(1)}, f32[1,16,1024]{2,1,0:T(8,128)S(1)}, u32[]{:S(2)}, u32[]{:S(2)}) collective-permute-start(f32[1,16,1024]{2,1,0:T(8,128)S(1)} %add.56), channel_id=1, source_target_pairs={{0,3},{1,2},{2,1},{3,0},{4,7},{5,6},{6,5},{7,4},{8,11},{9,10},{10,... | collective-permute-start | bytes 196616 | tf_op jit(solution)/shard_map/ppermute | solution.py:274
  60.7 1.3 %collective-permute-start.19 = (f32[1,16,1024]{2,1,0:T(8,128)S(1)}, f32[1,16,1024]{2,1,0:T(8,128)S(1)}, u32[]{:S(2)}, u32[]{:S(2)}) collective-permute-start(f32[1,16,1024]{2,1,0:T(8,128)S(1)} %add.57.pull), channel_id=1, source_target_pairs={{0,1},{1,0},{2,3},{3,2},{4,5},{5,4},{6,7},{7,6},{8,9},{9,8},{10,11... | collective-permute-start | bytes 196616 | tf_op jit(solution)/shard_map/ppermute | solution.py:274
  62.7 6.1 %collective-permute-start.22 = (f32[16,640]{1,0:T(8,128)S(1)}, f32[16,640]{1,0:T(8,128)S(1)}, u32[]{:S(2)}, u32[]{:S(2)}) collective-permute-start(f32[16,640]{1,0:T(8,128)S(1)} %pad_maximum_fusion.5), channel_id=1, source_target_pairs={{0,12},{4,8},{8,4},{12,0},{1,13},{5,9},{9,5},{13,1},{2,14},{6,10},... | collective-permute-start | bytes 122888 | tf_op jit(solution)/shard_map/ppermute | solution.py:274
  64.9 5.1 %collective-permute-start.21 = (f32[16,640]{1,0:T(8,128)S(1)}, f32[16,640]{1,0:T(8,128)S(1)}, u32[]{:S(2)}, u32[]{:S(2)}) collective-permute-start(f32[16,640]{1,0:T(8,128)S(1)} %pad_maximum_fusion.4), channel_id=1, source_target_pairs={{0,8},{4,12},{8,0},{12,4},{1,9},{5,13},{9,1},{13,5},{2,10},{6,14},... | collective-permute-start | bytes 122888 | tf_op jit(solution)/shard_map/ppermute | solution.py:274
  64.9 5.1 %collective-permute-start.20 = (f32[16,640]{1,0:T(8,128)S(1)}, f32[16,640]{1,0:T(8,128)S(1)}, u32[]{:S(2)}, u32[]{:S(2)}) collective-permute-start(f32[16,640]{1,0:T(8,128)S(1)} %pad_maximum_fusion.3), channel_id=1, source_target_pairs={{0,4},{4,0},{8,12},{12,8},{1,5},{5,1},{9,13},{13,9},{2,6},{6,2},{1... | collective-permute-start | bytes 122888 | tf_op jit(solution)/shard_map/ppermute | solution.py:274

commit v6 on v5

--- a/solution.py
+++ b/solution.py
@@ -10,6 +10,7 @@
 BLOCK = 128
 CORES = 2
 MIB = 1 << 20
+LIMIT = 56
 
 F32, BF16 = jnp.float32, jnp.bfloat16
 HBM = pl.BlockSpec(memory_space=pltpu.HBM)
@@ -57,33 +58,41 @@
     return min(rows, 512)
 
 
-def leaf_kernel(rhs, inverse, mine, other, held, land, sems, rhs_sem):
-    subs, rows, _ = inverse.shape
-    half = subs // CORES
+def leaf_kernel(rhs, inverse, other, kept, held, land, sems, rhs_sem):
+    half, rows, _ = land.shape
     role = role_of(lax.axis_index("col"))
     chunk = chunk_of(rows)
     steps = rows // chunk
-    order = [*range(half, subs), *range(half)]
 
     def fetch(slot, step):
         part = pl.ds(step * chunk, chunk)
+        into = kept.at[slot] if slot < half else land.at[slot - half]
         return pltpu.make_async_copy(
-            inverse.at[sub_of(slot, half, role), part], land.at[slot, part], sems.at[slot * steps + step]
+            inverse.at[sub_of(slot, half, role), part], into.at[part], sems.at[slot * steps + step]
         )
 
     first = pltpu.make_async_copy(rhs, held, rhs_sem)
     first.start()
-    for slot in order:
+    for slot in [*range(half, 2 * half), *range(half)]:
         for step in range(steps):
             fetch(slot, step).start()
     first.wait()
-    for slot in order:
-        out, at = (mine, slot) if slot < half else (other, slot - half)
+    for slot in range(half, 2 * half):
         value = held[sub_of(slot, half, role)]
         for step in range(steps):
             part = pl.ds(step * chunk, chunk)
             fetch(slot, step).wait()
-            out[at, :, part] = dot3(value, split(land[slot, part]), ROWS_OF)
+            other[slot - half, :, part] = dot3(value, split(land[slot - half, part]), ROWS_OF)
+    for slot in range(half):
+        for step in range(steps):
+            fetch(slot, step).wait()
+
+
+def rest_kernel(rhs, kept, mine):
+    half = kept.shape[0]
+    role = role_of(lax.axis_index("col"))
+    for slot in range(half):
+        mine[slot] = dot3(rhs[sub_of(slot, half, role)], split(kept[slot]), ROWS_OF)
 
 
 def couple_kernel(first, vectors, update, out):
@@ -331,21 +340,28 @@
 
     vec = jax.ShapeDtypeStruct((half, nrhs, leaf_rows), F32)
     leaf_flops = 2 * nrhs * leaf_inverse.size
-    mine, other = call(
+    half_shape = (half, leaf_rows, leaf_cols)
+    other, kept = pl.pallas_call(
         leaf_kernel,
-        (pltpu.VMEM(vec.shape, F32), pltpu.VMEM(vec.shape, F32)),
-        [HBM, HBM],
-        61,
-        (leaf_flops, 4 * leaf_inverse.size),
-        (
+        out_shape=[pltpu.VMEM(vec.shape, F32), pltpu.VMEM(half_shape, F32)],
+        in_specs=[HBM, HBM],
+        out_specs=[WHOLE, pl.BlockSpec(memory_space=pl.ANY)],
+        scratch_shapes=[
             pltpu.VMEM(leaf_rhs.shape, F32),
-            pltpu.VMEM(leaf_inverse.shape, F32),
+            pltpu.VMEM(half_shape, F32),
             pltpu.SemaphoreType.DMA((subs * (leaf_rows // chunk_of(leaf_rows)),)),
             pltpu.SemaphoreType.DMA,
+        ],
+        compiler_params=pltpu.CompilerParams(vmem_limit_bytes=LIMIT * MIB),
+        cost_estimate=pl.CostEstimate(
+            flops=leaf_flops, bytes_accessed=4 * leaf_inverse.size, transcendentals=0
         ),
     )(in_hbm(leaf_rhs), in_hbm(leaf_inverse))
-
-    mine = mine + swap(other, "col", cols, 1)
+    arrived = swap(other, "col", cols, 1)
+    mine = call(rest_kernel, vec, [WHOLE, WHOLE], 12, (leaf_flops // 2, 2 * leaf_inverse.size))(
+        leaf_rhs, in_vmem(kept)
+    )
+    mine = mine + arrived
     arrived, update = beside(swap(mine, "col", cols, CORES + 1), update_rows)
     mine, other = sum_over_lines(mine, cols, arrived)
     coupled = [

time: 70.8 us -> 70.4 us (level)
  starting transfers between devices: 24.7 us -> 23.7 us
    ppermute x23, starting transfers between devices: 24.7 us -> 23.7 us  [swap(): return lax.ppermute(value, axes, [(i, i ^ mask) for i in range(size)])]
    pallas_call x1 -> x2, Pallas kernels: 4.49 us -> 4.86 us  [the longest x1 3.61 us: body(): pl.pallas_call(leaf_kernel, out_shape=[pltpu.VMEM(vec.shape, F32), pltpu....]
  transfers between devices with their start and end apart: 23 -> 23, of which waited for: 18 -> 19; matrix products, arithmetic and copies ran while one was open for 0% -> 0% of each run, Pallas kernels for 12% -> 14%
where the time goes in v6:
time: 70.4 us; the launch traced here: 70.2 us
  waiting for transfers between devices  28.3 us (40%)
  starting transfers between devices  23.7 us (34%)
  Pallas kernels  17.1 us (24%)
  between operations  0.87 us (1%)
    ppermute x23, waiting for transfers between devices, swap(): return lax.ppermute(value, axes, [(i, i ^ mask) for i in range(size)])  28.3 us
    ppermute x23, starting transfers between devices, swap(): return lax.ppermute(value, axes, [(i, i ^ mask) for i in range(size)])  23.7 us
    pallas_call x1, Pallas kernels, body(): pl.pallas_call(leaf_kernel, out_shape=[pltpu.VMEM(vec.shape, F32), pltpu....  3.61 us
    pallas_call x1, Pallas kernels, body(): pl.pallas_call(functools.partial(prepare_kernel, inside), out_shape=[pltp...  2.62 us
    pallas_call x1, Pallas kernels, beside(): pl.pallas_call(load_kernel, out_shape=pltpu.VMEM(value.shape, value.dtype...  2.24 us
    pallas_call x4, Pallas kernels, parts_of(): call(functools.partial(solve_parts_kernel, rows, masks, first), (jax.Shap...  1.91 us
    pallas_call x1, Pallas kernels, body(): call(functools.partial(separator_kernel, shape, inside), (piece, jax.Shap...  1.44 us
  transfers between devices with their start and end apart: 23, of which 19 were waited for; matrix products, arithmetic and copies ran while one was open for 0% of the time, Pallas kernels for 14%

profile of v6, /device:TPU:0, one launch (start us, length us, event | category | flops | bytes accessed | tf_op | source)
XLA Modules:
  0.0 70.2 jit_solution(7757385897559126316)
XLA Ops:
  0.6 3.6 %shard_map.77 = (f32[1,16,1024]{2,1,0:T(8,128)S(1)}, f32[1,1024,1024]{2,1,0:T(8,128)S(1)}) custom-call(f32[2,16,1024]{2,1,0:T(8,128)} %rhs.4, f32[2,1024,1024]{2,1,0:T(8,128)} %inverse.9), custom_call_target="tpu_custom_call" | custom-call | flops 67108864 | bytes 8388608 | tf_op jit(solution)/shard_map/pallas_call | solution.py:344
  4.3 0.5 collective-permute-start
  4.8 1.2 %shard_map.78 = f32[1,16,1024]{2,1,0:T(8,128)S(1)} custom-call(f32[2,16,1024]{2,1,0:T(8,128)S(1)} %copy-done.1, f32[1,1024,1024]{2,1,0:T(8,128)S(1)} %get-tuple-element.23.kept), custom_call_target="tpu_custom_call" | custom-call | flops 33554432 | bytes 4194304 | tf_op jit(solution)/shard_map/pallas_call | solution.py:361
  6.1 2.7 %collective-permute-start.1 = (f32[1,16,1024]{2,1,0:T(8,128)S(1)}, f32[1,16,1024]{2,1,0:T(8,128)S(1)}, u32[]{:S(2)}, u32[]{:S(2)}) collective-permute-start(f32[1,16,1024]{2,1,0:T(8,128)S(1)} %add.44), channel_id=1, source_target_pairs={{0,3},{1,2},{2,1},{3,0},{4,7},{5,6},{6,5},{7,4},{8,11},{9,10},{10,... | collective-permute-start | bytes 196616 | tf_op jit(solution)/shard_map/ppermute | solution.py:283
  8.8 2.2 %shard_map.79.update = f32[2,512,1024]{2,1,0:T(8,128)S(1)} custom-call(f32[2,512,1024]{2,1,0:T(8,128)} %update.3), custom_call_target="tpu_custom_call" | custom-call | bytes 4194304 | tf_op jit(solution)/shard_map/pallas_call | solution.py:293
  11.4 0.7 shard_map.80
  12.1 0.5 collective-permute-done.2.vectors
  12.5 0.7 shard_map.81
  13.2 1.5 %collective-permute-start.3 = (f32[16,1024]{1,0:T(8,128)S(1)}, f32[16,1024]{1,0:T(8,128)S(1)}, u32[]{:S(2)}, u32[]{:S(2)}) collective-permute-start(f32[16,1024]{1,0:T(8,128)S(1)} %pad_maximum_fusion.1), channel_id=1, source_target_pairs={{0,4},{4,0},{8,12},{12,8},{1,5},{5,1},{9,13},{13,9},{2,6},{6,2},{1... | collective-permute-start | bytes 196616 | tf_op jit(solution)/shard_map/ppermute | solution.py:283
  14.7 2.6 %collective-permute-start.4 = (f32[16,1024]{1,0:T(8,128)S(1)}, f32[16,1024]{1,0:T(8,128)S(1)}, u32[]{:S(2)}, u32[]{:S(2)}) collective-permute-start(f32[16,1024]{1,0:T(8,128)S(1)} %pad_maximum_fusion.1), channel_id=1, source_target_pairs={{0,8},{4,12},{8,0},{12,4},{1,9},{5,13},{9,1},{13,5},{2,10},{6,14},... | collective-permute-start | bytes 196616 | tf_op jit(solution)/shard_map/ppermute | solution.py:283
  17.3 0.4 collective-permute-start.5
  17.7 2.6 %shard_map.82 = (bf16[256,4096]{1,0:T(8,128)(2,1)S(1)}, bf16[4096,256]{1,0:T(8,128)(2,1)S(1)}) custom-call(f32[128,4096]{1,0:T(8,128)} %sep.1), custom_call_target="tpu_custom_call" | custom-call | bytes 4194304 | tf_op jit(solution)/shard_map/pallas_call | solution.py:380
  20.3 2.0 %collective-permute-done.4 = f32[16,1024]{1,0:T(8,128)S(1)} collective-permute-done((f32[16,1024]{1,0:T(8,128)S(1)}, f32[16,1024]{1,0:T(8,128)S(1)}, u32[]{:S(2)}, u32[]{:S(2)}) %collective-permute-start.4) | collective-permute-done | bytes 65568 | tf_op jit(solution)/shard_map/ppermute | solution.py:283
  22.3 1.1 %collective-permute-done.5 = f32[16,1024]{1,0:T(8,128)S(1)} collective-permute-done((f32[16,1024]{1,0:T(8,128)S(1)}, f32[16,1024]{1,0:T(8,128)S(1)}, u32[]{:S(2)}, u32[]{:S(2)}) %collective-permute-start.5) | collective-permute-done | bytes 65568 | tf_op jit(solution)/shard_map/ppermute | solution.py:283
  23.5 2.7 %collective-permute-start.7 = (f32[16,1152]{1,0:T(8,128)S(1)}, f32[16,1152]{1,0:T(8,128)S(1)}, u32[]{:S(2)}, u32[]{:S(2)}) collective-permute-start(f32[16,1152]{1,0:T(8,128)S(1)} %get-tuple-element.48), channel_id=1, source_target_pairs={{0,17},{1,16},{2,19},{3,18},{16,1},{17,0},{18,3},{19,2},{4,21},{5,... | collective-permute-start | bytes 221192 | tf_op jit(solution)/shard_map/ppermute | solution.py:283
  26.3 1.7 %collective-permute-done.6 = f32[16,1152]{1,0:T(8,128)S(1)} collective-permute-done((f32[16,1152]{1,0:T(8,128)S(1)}, f32[16,1152]{1,0:T(8,128)S(1)}, u32[]{:S(2)}, u32[]{:S(2)}) %collective-permute-start.6) | collective-permute-done | bytes 73760 | tf_op jit(solution)/shard_map/ppermute | solution.py:283
  28.0 0.8 %collective-permute-done.7 = f32[16,1152]{1,0:T(8,128)S(1)} collective-permute-done((f32[16,1152]{1,0:T(8,128)S(1)}, f32[16,1152]{1,0:T(8,128)S(1)}, u32[]{:S(2)}, u32[]{:S(2)}) %collective-permute-start.7) | collective-permute-done | bytes 73760 | tf_op jit(solution)/shard_map/ppermute | solution.py:283
  28.8 2.1 %collective-permute-done.8 = f32[16,1152]{1,0:T(8,128)S(1)} collective-permute-done((f32[16,1152]{1,0:T(8,128)S(1)}, f32[16,1152]{1,0:T(8,128)S(1)}, u32[]{:S(2)}, u32[]{:S(2)}) %collective-permute-start.8) | collective-permute-done | bytes 73760 | tf_op jit(solution)/shard_map/ppermute | solution.py:283
  31.0 1.0 %shard_map.83 = (f32[32,16,128]{2,1,0:T(8,128)S(1)}, s32[2,32]{1,0:T(2,128)S(4)}) custom-call(f32[4,16,1152]{2,1,0:T(8,128)S(1)} %pad_maximum_fusion.near, f32[16,4096]{1,0:T(8,128)S(1)} %copy-done.2), custom_call_target="tpu_custom_call" | custom-call | flops 131072 | bytes 786432 | tf_op jit(solution)/shard_map/pallas_call | solution.py:404
  32.0 0.5 collective-permute-done.9.far
  32.6 1.4 %shard_map.84 = (f32[4,16,1536]{2,1,0:T(8,128)S(1)}, f32[32,16,128]{2,1,0:T(8,128)S(1)}) custom-call(s32[2,32]{1,0:T(2,128)S(4)} %get-tuple-element.32.table, f32[4,16,1152]{2,1,0:T(8,128)S(1)} %collective-permute-done.9.far, f32[32,16,128]{2,1,0:T(8,128)S(1)} %get-tuple-element.33.start, bf16[256,4096]{1,0:T(8,128)(2,1)S(1)} %get-tuple-element.34.both, ...), custom_call_target="tpu_custom_call" | custom-call | flops 33554432 | bytes 2097152 | tf_op jit(solution)/shard_map/pallas_call | solution.py:422
  34.3 1.5 %collective-permute-done.10 = f32[4,16,1536]{2,1,0:T(8,128)S(1)} collective-permute-done((f32[4,16,1536]{2,1,0:T(8,128)S(1)}, f32[4,16,1536]{2,1,0:T(8,128)S(1)}, u32[]{:S(2)}, u32[]{:S(2)}) %collective-permute-start.10) | collective-permute-done | bytes 393248 | tf_op jit(solution)/shard_map/ppermute | solution.py:283
  35.9 1.0 %collective-permute-start.11 = (f32[16,1536]{1,0:T(8,128)S(1)}, f32[16,1536]{1,0:T(8,128)S(1)}, u32[]{:S(2)}, u32[]{:S(2)}) collective-permute-start(f32[16,1536]{1,0:T(8,128)S(1)} %get-tuple-element.46), channel_id=1, source_target_pairs={{0,3},{1,2},{2,1},{3,0},{16,19},{17,18},{18,17},{19,16},{4,7},{5,6... | collective-permute-start | bytes 294920 | tf_op jit(solution)/shard_map/ppermute | solution.py:283
  36.9 0.9 %collective-permute-start.12 = (f32[16,1536]{1,0:T(8,128)S(1)}, f32[16,1536]{1,0:T(8,128)S(1)}, u32[]{:S(2)}, u32[]{:S(2)}) collective-permute-start(f32[16,1536]{1,0:T(8,128)S(1)} %get-tuple-element.44), channel_id=1, source_target_pairs={{0,17},{1,16},{2,19},{3,18},{16,1},{17,0},{18,3},{19,2},{4,21},{5,... | collective-permute-start | bytes 294920 | tf_op jit(solution)/shard_map/ppermute | solution.py:283
  37.8 1.1 %collective-permute-start.13 = (f32[16,1536]{1,0:T(8,128)S(1)}, f32[16,1536]{1,0:T(8,128)S(1)}, u32[]{:S(2)}, u32[]{:S(2)}) collective-permute-start(f32[16,1536]{1,0:T(8,128)S(1)} %get-tuple-element.45), channel_id=1, source_target_pairs={{0,19},{1,18},{2,17},{3,16},{16,3},{17,2},{18,1},{19,0},{4,23},{5,... | collective-permute-start | bytes 294920 | tf_op jit(solution)/shard_map/ppermute | solution.py:283
  38.9 1.8 %collective-permute-done.11 = f32[16,1536]{1,0:T(8,128)S(1)} collective-permute-done((f32[16,1536]{1,0:T(8,128)S(1)}, f32[16,1536]{1,0:T(8,128)S(1)}, u32[]{:S(2)}, u32[]{:S(2)}) %collective-permute-start.11) | collective-permute-done | bytes 98336 | tf_op jit(solution)/shard_map/ppermute | solution.py:283
  40.7 0.8 %collective-permute-done.12 = f32[16,1536]{1,0:T(8,128)S(1)} collective-permute-done((f32[16,1536]{1,0:T(8,128)S(1)}, f32[16,1536]{1,0:T(8,128)S(1)}, u32[]{:S(2)}, u32[]{:S(2)}) %collective-permute-start.12) | collective-permute-done | bytes 98336 | tf_op jit(solution)/shard_map/ppermute | solution.py:283
  41.5 2.4 %collective-permute-done.13 = f32[16,1536]{1,0:T(8,128)S(1)} collective-permute-done((f32[16,1536]{1,0:T(8,128)S(1)}, f32[16,1536]{1,0:T(8,128)S(1)}, u32[]{:S(2)}, u32[]{:S(2)}) %collective-permute-start.13) | collective-permute-done | bytes 98336 | tf_op jit(solution)/shard_map/ppermute | solution.py:283
  43.9 1.8 %collective-permute-start.14 = (f32[16,1024]{1,0:T(8,128)S(1)}, f32[16,1024]{1,0:T(8,128)S(1)}, u32[]{:S(2)}, u32[]{:S(2)}) collective-permute-start(f32[16,1024]{1,0:T(8,128)S(1)} %slice.28), channel_id=1, source_target_pairs={{0,4},{4,0},{8,12},{12,8},{1,5},{5,1},{9,13},{13,9},{2,6},{6,2},{1... | collective-permute-start | bytes 196616 | tf_op jit(solution)/shard_map/ppermute | solution.py:283
  45.7 1.1 %collective-permute-start.15 = (f32[16,1024]{1,0:T(8,128)S(1)}, f32[16,1024]{1,0:T(8,128)S(1)}, u32[]{:S(2)}, u32[]{:S(2)}) collective-permute-start(f32[16,1024]{1,0:T(8,128)S(1)} %slice.28), channel_id=1, source_target_pairs={{0,8},{4,12},{8,0},{12,4},{1,9},{5,13},{9,1},{13,5},{2,10},{6,14},... | collective-permute-start | bytes 196616 | tf_op jit(solution)/shard_map/ppermute | solution.py:283
  46.8 1.6 %collective-permute-start.16 = (f32[16,1024]{1,0:T(8,128)S(1)}, f32[16,1024]{1,0:T(8,128)S(1)}, u32[]{:S(2)}, u32[]{:S(2)}) collective-permute-start(f32[16,1024]{1,0:T(8,128)S(1)} %slice.28), channel_id=1, source_target_pairs={{0,12},{4,8},{8,4},{12,0},{1,13},{5,9},{9,5},{13,1},{2,14},{6,10},... | collective-permute-start | bytes 196616 | tf_op jit(solution)/shard_map/ppermute | solution.py:283
  48.4 5.5 %collective-permute-done.15 = f32[16,1024]{1,0:T(8,128)S(1)} collective-permute-done((f32[16,1024]{1,0:T(8,128)S(1)}, f32[16,1024]{1,0:T(8,128)S(1)}, u32[]{:S(2)}, u32[]{:S(2)}) %collective-permute-start.15) | collective-permute-done | bytes 65568 | tf_op jit(solution)/shard_map/ppermute | solution.py:283
  53.9 0.5 shard_map.87
  54.4 0.5 shard_map.86
  54.8 0.8 %collective-permute-done.17 = f32[1,16,1024]{2,1,0:T(8,128)S(1)} collective-permute-done((f32[1,16,1024]{2,1,0:T(8,128)S(1)}, f32[1,16,1024]{2,1,0:T(8,128)S(1)}, u32[]{:S(2)}, u32[]{:S(2)}) %collective-permute-start.17) | collective-permute-done | bytes 65568 | tf_op jit(solution)/shard_map/ppermute | solution.py:283
  55.6 0.6 collective-permute-start.18
  56.2 3.5 %collective-permute-done.18 = f32[1,16,1024]{2,1,0:T(8,128)S(1)} collective-permute-done((f32[1,16,1024]{2,1,0:T(8,128)S(1)}, f32[1,16,1024]{2,1,0:T(8,128)S(1)}, u32[]{:S(2)}, u32[]{:S(2)}) %collective-permute-start.18) | collective-permute-done | bytes 65568 | tf_op jit(solution)/shard_map/ppermute | solution.py:283
  59.8 0.2 collective-permute-start.19
  60.0 0.3 shard_map.88
  60.3 0.7 shard_map.90
  61.1 0.7 shard_map.91
  61.8 2.0 %collective-permute-start.22 = (f32[16,640]{1,0:T(8,128)S(1)}, f32[16,640]{1,0:T(8,128)S(1)}, u32[]{:S(2)}, u32[]{:S(2)}) collective-permute-start(f32[16,640]{1,0:T(8,128)S(1)} %pad_maximum_fusion.5), channel_id=1, source_target_pairs={{0,12},{4,8},{8,4},{12,0},{1,13},{5,9},{9,5},{13,1},{2,14},{6,10},... | collective-permute-start | bytes 122888 | tf_op jit(solution)/shard_map/ppermute | solution.py:283
  63.8 1.0 %collective-permute-start.21 = (f32[16,640]{1,0:T(8,128)S(1)}, f32[16,640]{1,0:T(8,128)S(1)}, u32[]{:S(2)}, u32[]{:S(2)}) collective-permute-start(f32[16,640]{1,0:T(8,128)S(1)} %pad_maximum_fusion.4), channel_id=1, source_target_pairs={{0,8},{4,12},{8,0},{12,4},{1,9},{5,13},{9,1},{13,5},{2,10},{6,14},... | collective-permute-start | bytes 122888 | tf_op jit(solution)/shard_map/ppermute | solution.py:283
  64.8 1.4 %collective-permute-start.20 = (f32[16,640]{1,0:T(8,128)S(1)}, f32[16,640]{1,0:T(8,128)S(1)}, u32[]{:S(2)}, u32[]{:S(2)}) collective-permute-start(f32[16,640]{1,0:T(8,128)S(1)} %pad_maximum_fusion.3), channel_id=1, source_target_pairs={{0,4},{4,0},{8,12},{12,8},{1,5},{5,1},{9,13},{13,9},{2,6},{6,2},{1... | collective-permute-start | bytes 122888 | tf_op jit(solution)/shard_map/ppermute | solution.py:283
  66.2 0.3 shard_map.89
  66.5 1.5 %collective-permute-done.22.refs_3_ = f32[16,640]{1,0:T(8,128)S(1)} collective-permute-done((f32[16,640]{1,0:T(8,128)S(1)}, f32[16,640]{1,0:T(8,128)S(1)}, u32[]{:S(2)}, u32[]{:S(2)}) %collective-permute-start.22) | collective-permute-done | bytes 40992 | tf_op jit(solution)/shard_map/ppermute | solution.py:283
  68.1 1.4 %collective-permute-done.21.refs_2_ = f32[16,640]{1,0:T(8,128)S(1)} collective-permute-done((f32[16,640]{1,0:T(8,128)S(1)}, f32[16,640]{1,0:T(8,128)S(1)}, u32[]{:S(2)}, u32[]{:S(2)}) %collective-permute-start.21) | collective-permute-done | bytes 40992 | tf_op jit(solution)/shard_map/ppermute | solution.py:283
  69.6 0.6 shard_map.92
  (46 shorter events, 1.3 us)
Async XLA Ops:
  0.6 4.2 %copy-start.1 = (f32[2,16,1024]{2,1,0:T(8,128)S(1)}, f32[2,16,1024]{2,1,0:T(8,128)}, u32[]{:S(2)}) copy-start(f32[2,16,1024]{2,1,0:T(8,128)} %rhs.4) | copy-start | bytes 393220
  4.3 1.8 %collective-permute-start = (f32[1,16,1024]{2,1,0:T(8,128)S(1)}, f32[1,16,1024]{2,1,0:T(8,128)S(1)}, u32[]{:S(2)}, u32[]{:S(2)}) collective-permute-start(f32[1,16,1024]{2,1,0:T(8,128)S(1)} %get-tuple-element.24), channel_id=1, source_target_pairs={{0,1},{1,0},{2,3},{3,2},{4,5},{5,4},{6,7},{7,6},{8,9},{9,8},{10,11... | collective-permute-start | bytes 196616 | tf_op jit(solution)/shard_map/ppermute | solution.py:283
  6.1 5.1 %collective-permute-start.1 = (f32[1,16,1024]{2,1,0:T(8,128)S(1)}, f32[1,16,1024]{2,1,0:T(8,128)S(1)}, u32[]{:S(2)}, u32[]{:S(2)}) collective-permute-start(f32[1,16,1024]{2,1,0:T(8,128)S(1)} %add.44), channel_id=1, source_target_pairs={{0,3},{1,2},{2,1},{3,0},{4,7},{5,6},{6,5},{7,4},{8,11},{9,10},{10,... | collective-permute-start | bytes 196616 | tf_op jit(solution)/shard_map/ppermute | solution.py:283
  11.2 1.3 %collective-permute-start.2 = (f32[1,16,1024]{2,1,0:T(8,128)S(1)}, f32[1,16,1024]{2,1,0:T(8,128)S(1)}, u32[]{:S(2)}, u32[]{:S(2)}) collective-permute-start(f32[1,16,1024]{2,1,0:T(8,128)S(1)} %add.45.vectors), channel_id=1, source_target_pairs={{0,1},{1,0},{2,3},{3,2},{4,5},{5,4},{6,7},{7,6},{8,9},{9,8},{10,11... | collective-permute-start | bytes 196616 | tf_op jit(solution)/shard_map/ppermute | solution.py:283
  12.1 8.2 %copy-start.3 = (s32[2,16]{1,0:T(2,128)S(1)}, s32[2,16]{1,0:T(2,128)}, u32[]{:S(2)}) copy-start(s32[2,16]{1,0:T(2,128)} %param.9) | copy-start | bytes 388
  12.1 18.9 %copy-start.2 = (f32[16,4096]{1,0:T(8,128)S(1)}, f32[16,4096]{1,0:T(8,128)}, u32[]{:S(2)}) copy-start(f32[16,4096]{1,0:T(8,128)} %rhs.5) | copy-start | bytes 786436
  13.2 7.1 %collective-permute-start.3 = (f32[16,1024]{1,0:T(8,128)S(1)}, f32[16,1024]{1,0:T(8,128)S(1)}, u32[]{:S(2)}, u32[]{:S(2)}) collective-permute-start(f32[16,1024]{1,0:T(8,128)S(1)} %pad_maximum_fusion.1), channel_id=1, source_target_pairs={{0,4},{4,0},{8,12},{12,8},{1,5},{5,1},{9,13},{13,9},{2,6},{6,2},{1... | collective-permute-start | bytes 196616 | tf_op jit(solution)/shard_map/ppermute | solution.py:283
  14.7 7.7 %collective-permute-start.4 = (f32[16,1024]{1,0:T(8,128)S(1)}, f32[16,1024]{1,0:T(8,128)S(1)}, u32[]{:S(2)}, u32[]{:S(2)}) collective-permute-start(f32[16,1024]{1,0:T(8,128)S(1)} %pad_maximum_fusion.1), channel_id=1, source_target_pairs={{0,8},{4,12},{8,0},{12,4},{1,9},{5,13},{9,1},{13,5},{2,10},{6,14},... | collective-permute-start | bytes 196616 | tf_op jit(solution)/shard_map/ppermute | solution.py:283
  17.3 6.1 %collective-permute-start.5 = (f32[16,1024]{1,0:T(8,128)S(1)}, f32[16,1024]{1,0:T(8,128)S(1)}, u32[]{:S(2)}, u32[]{:S(2)}) collective-permute-start(f32[16,1024]{1,0:T(8,128)S(1)} %pad_maximum_fusion.1), channel_id=1, source_target_pairs={{0,12},{4,8},{8,4},{12,0},{1,13},{5,9},{9,5},{13,1},{2,14},{6,10},... | collective-permute-start | bytes 196616 | tf_op jit(solution)/shard_map/ppermute | solution.py:283
  23.4 4.6 %collective-permute-start.6 = (f32[16,1152]{1,0:T(8,128)S(1)}, f32[16,1152]{1,0:T(8,128)S(1)}, u32[]{:S(2)}, u32[]{:S(2)}) collective-permute-start(f32[16,1152]{1,0:T(8,128)S(1)} %get-tuple-element.48), channel_id=1, source_target_pairs={{0,3},{1,2},{2,1},{3,0},{16,19},{17,18},{18,17},{19,16},{4,7},{5,6... | collective-permute-start | bytes 221192 | tf_op jit(solution)/shard_map/ppermute | solution.py:283
  23.5 5.3 %collective-permute-start.7 = (f32[16,1152]{1,0:T(8,128)S(1)}, f32[16,1152]{1,0:T(8,128)S(1)}, u32[]{:S(2)}, u32[]{:S(2)}) collective-permute-start(f32[16,1152]{1,0:T(8,128)S(1)} %get-tuple-element.48), channel_id=1, source_target_pairs={{0,17},{1,16},{2,19},{3,18},{16,1},{17,0},{18,3},{19,2},{4,21},{5,... | collective-permute-start | bytes 221192 | tf_op jit(solution)/shard_map/ppermute | solution.py:283
  26.2 4.7 %collective-permute-start.8 = (f32[16,1152]{1,0:T(8,128)S(1)}, f32[16,1152]{1,0:T(8,128)S(1)}, u32[]{:S(2)}, u32[]{:S(2)}) collective-permute-start(f32[16,1152]{1,0:T(8,128)S(1)} %get-tuple-element.48), channel_id=1, source_target_pairs={{0,19},{1,18},{2,17},{3,16},{16,3},{17,2},{18,1},{19,0},{4,23},{5,... | collective-permute-start | bytes 221192 | tf_op jit(solution)/shard_map/ppermute | solution.py:283
  30.9 1.6 %collective-permute-start.9 = (f32[4,16,1152]{2,1,0:T(8,128)S(1)}, f32[4,16,1152]{2,1,0:T(8,128)S(1)}, u32[]{:S(2)}, u32[]{:S(2)}) collective-permute-start(f32[4,16,1152]{2,1,0:T(8,128)S(1)} %pad_maximum_fusion.near), channel_id=1, source_target_pairs={{0,1},{1,0},{2,3},{3,2},{4,5},{5,4},{6,7},{7,6},{8,9},{9,8},{10,11... | collective-permute-start | bytes 884744 | tf_op jit(solution)/shard_map/ppermute | solution.py:283
  32.0 21.9 %copy-start = (f32[2,512,1024]{2,1,0:T(8,128)S(1)}, f32[2,512,1024]{2,1,0:T(8,128)}, u32[]{:S(2)}) copy-start(f32[2,512,1024]{2,1,0:T(8,128)} %update.3) | copy-start | bytes 12582916
  32.6 27.4 %slice-start = ((s8[8388608]{0:T(1024)(128)(4,1)}), s8[4194304]{0:T(1024)(128)(4,1)S(1)}, s32[]{:S(2)}) async-start(s8[8388608]{0:T(1024)(128)(4,1)} %bitcast.15), calls=%async_computation | async-start | bytes 8388608
  34.0 1.8 %collective-permute-start.10 = (f32[4,16,1536]{2,1,0:T(8,128)S(1)}, f32[4,16,1536]{2,1,0:T(8,128)S(1)}, u32[]{:S(2)}, u32[]{:S(2)}) collective-permute-start(f32[4,16,1536]{2,1,0:T(8,128)S(1)} %get-tuple-element.37), channel_id=1, source_target_pairs={{0,1},{1,0},{2,3},{3,2},{4,5},{5,4},{6,7},{7,6},{8,9},{9,8},{10,11... | collective-permute-start | bytes 1179656 | tf_op jit(solution)/shard_map/ppermute | solution.py:283
  35.9 4.8 %collective-permute-start.11 = (f32[16,1536]{1,0:T(8,128)S(1)}, f32[16,1536]{1,0:T(8,128)S(1)}, u32[]{:S(2)}, u32[]{:S(2)}) collective-permute-start(f32[16,1536]{1,0:T(8,128)S(1)} %get-tuple-element.46), channel_id=1, source_target_pairs={{0,3},{1,2},{2,1},{3,0},{16,19},{17,18},{18,17},{19,16},{4,7},{5,6... | collective-permute-start | bytes 294920 | tf_op jit(solution)/shard_map/ppermute | solution.py:283
  36.9 4.6 %collective-permute-start.12 = (f32[16,1536]{1,0:T(8,128)S(1)}, f32[16,1536]{1,0:T(8,128)S(1)}, u32[]{:S(2)}, u32[]{:S(2)}) collective-permute-start(f32[16,1536]{1,0:T(8,128)S(1)} %get-tuple-element.44), channel_id=1, source_target_pairs={{0,17},{1,16},{2,19},{3,18},{16,1},{17,0},{18,3},{19,2},{4,21},{5,... | collective-permute-start | bytes 294920 | tf_op jit(solution)/shard_map/ppermute | solution.py:283
  37.8 6.1 %collective-permute-start.13 = (f32[16,1536]{1,0:T(8,128)S(1)}, f32[16,1536]{1,0:T(8,128)S(1)}, u32[]{:S(2)}, u32[]{:S(2)}) collective-permute-start(f32[16,1536]{1,0:T(8,128)S(1)} %get-tuple-element.45), channel_id=1, source_target_pairs={{0,19},{1,18},{2,17},{3,16},{16,3},{17,2},{18,1},{19,0},{4,23},{5,... | collective-permute-start | bytes 294920 | tf_op jit(solution)/shard_map/ppermute | solution.py:283
  43.9 4.5 %collective-permute-start.14 = (f32[16,1024]{1,0:T(8,128)S(1)}, f32[16,1024]{1,0:T(8,128)S(1)}, u32[]{:S(2)}, u32[]{:S(2)}) collective-permute-start(f32[16,1024]{1,0:T(8,128)S(1)} %slice.28), channel_id=1, source_target_pairs={{0,4},{4,0},{8,12},{12,8},{1,5},{5,1},{9,13},{13,9},{2,6},{6,2},{1... | collective-permute-start | bytes 196616 | tf_op jit(solution)/shard_map/ppermute | solution.py:283
  45.7 8.2 %collective-permute-start.15 = (f32[16,1024]{1,0:T(8,128)S(1)}, f32[16,1024]{1,0:T(8,128)S(1)}, u32[]{:S(2)}, u32[]{:S(2)}) collective-permute-start(f32[16,1024]{1,0:T(8,128)S(1)} %slice.28), channel_id=1, source_target_pairs={{0,8},{4,12},{8,0},{12,4},{1,9},{5,13},{9,1},{13,5},{2,10},{6,14},... | collective-permute-start | bytes 196616 | tf_op jit(solution)/shard_map/ppermute | solution.py:283
  46.8 7.0 %collective-permute-start.16 = (f32[16,1024]{1,0:T(8,128)S(1)}, f32[16,1024]{1,0:T(8,128)S(1)}, u32[]{:S(2)}, u32[]{:S(2)}) collective-permute-start(f32[16,1024]{1,0:T(8,128)S(1)} %slice.28), channel_id=1, source_target_pairs={{0,12},{4,8},{8,4},{12,0},{1,13},{5,9},{9,5},{13,1},{2,14},{6,10},... | collective-permute-start | bytes 196616 | tf_op jit(solution)/shard_map/ppermute | solution.py:283
  53.9 6.1 %slice-start.1 = ((s8[8388608]{0:T(1024)(128)(4,1)}), s8[4194304]{0:T(1024)(128)(4,1)S(1)}, s32[]{:S(2)}) async-start(s8[8388608]{0:T(1024)(128)(4,1)} %bitcast.15), calls=%async_computation.1 | async-start | bytes 8388608
  54.4 1.3 %collective-permute-start.17 = (f32[1,16,1024]{2,1,0:T(8,128)S(1)}, f32[1,16,1024]{2,1,0:T(8,128)S(1)}, u32[]{:S(2)}, u32[]{:S(2)}) collective-permute-start(f32[1,16,1024]{2,1,0:T(8,128)S(1)} %shard_map.87), channel_id=1, source_target_pairs={{0,1},{1,0},{2,3},{3,2},{4,5},{5,4},{6,7},{7,6},{8,9},{9,8},{10,11... | collective-permute-start | bytes 196616 | tf_op jit(solution)/shard_map/ppermute | solution.py:283
  55.6 4.1 %collective-permute-start.18 = (f32[1,16,1024]{2,1,0:T(8,128)S(1)}, f32[1,16,1024]{2,1,0:T(8,128)S(1)}, u32[]{:S(2)}, u32[]{:S(2)}) collective-permute-start(f32[1,16,1024]{2,1,0:T(8,128)S(1)} %add.56), channel_id=1, source_target_pairs={{0,3},{1,2},{2,1},{3,0},{4,7},{5,6},{6,5},{7,4},{8,11},{9,10},{10,... | collective-permute-start | bytes 196616 | tf_op jit(solution)/shard_map/ppermute | solution.py:283
  59.8 1.3 %collective-permute-start.19 = (f32[1,16,1024]{2,1,0:T(8,128)S(1)}, f32[1,16,1024]{2,1,0:T(8,128)S(1)}, u32[]{:S(2)}, u32[]{:S(2)}) collective-permute-start(f32[1,16,1024]{2,1,0:T(8,128)S(1)} %add.57.pull), channel_id=1, source_target_pairs={{0,1},{1,0},{2,3},{3,2},{4,5},{5,4},{6,7},{7,6},{8,9},{9,8},{10,11... | collective-permute-start | bytes 196616 | tf_op jit(solution)/shard_map/ppermute | solution.py:283
  61.8 6.3 %collective-permute-start.22 = (f32[16,640]{1,0:T(8,128)S(1)}, f32[16,640]{1,0:T(8,128)S(1)}, u32[]{:S(2)}, u32[]{:S(2)}) collective-permute-start(f32[16,640]{1,0:T(8,128)S(1)} %pad_maximum_fusion.5), channel_id=1, source_target_pairs={{0,12},{4,8},{8,4},{12,0},{1,13},{5,9},{9,5},{13,1},{2,14},{6,10},... | collective-permute-start | bytes 122888 | tf_op jit(solution)/shard_map/ppermute | solution.py:283
  63.8 5.7 %collective-permute-start.21 = (f32[16,640]{1,0:T(8,128)S(1)}, f32[16,640]{1,0:T(8,128)S(1)}, u32[]{:S(2)}, u32[]{:S(2)}) collective-permute-start(f32[16,640]{1,0:T(8,128)S(1)} %pad_maximum_fusion.4), channel_id=1, source_target_pairs={{0,8},{4,12},{8,0},{12,4},{1,9},{5,13},{9,1},{13,5},{2,10},{6,14},... | collective-permute-start | bytes 122888 | tf_op jit(solution)/shard_map/ppermute | solution.py:283
  64.8 4.8 %collective-permute-start.20 = (f32[16,640]{1,0:T(8,128)S(1)}, f32[16,640]{1,0:T(8,128)S(1)}, u32[]{:S(2)}, u32[]{:S(2)}) collective-permute-start(f32[16,640]{1,0:T(8,128)S(1)} %pad_maximum_fusion.3), channel_id=1, source_target_pairs={{0,4},{4,0},{8,12},{12,8},{1,5},{5,1},{9,13},{13,9},{2,6},{6,2},{1... | collective-permute-start | bytes 122888 | tf_op jit(solution)/shard_map/ppermute | solution.py:283

commit v7 on v6

--- a/solution.py
+++ b/solution.py
@@ -55,44 +55,50 @@
 
 
 def chunk_of(rows):
-    return min(rows, 512)
-
-
-def leaf_kernel(rhs, inverse, other, kept, held, land, sems, rhs_sem):
-    half, rows, _ = land.shape
+    return min(rows // 2, 512)
+
+
+def leaf_kernel(rhs, inverse, other, begun, kept, held, land, sems, rhs_sem):
+    subs, rows, _ = land.shape
+    half = subs // CORES
     role = role_of(lax.axis_index("col"))
-    chunk = chunk_of(rows)
+    chunk = kept.shape[1]
     steps = rows // chunk
 
     def fetch(slot, step):
         part = pl.ds(step * chunk, chunk)
-        into = kept.at[slot] if slot < half else land.at[slot - half]
+        last = slot < half and step == steps - 1
         return pltpu.make_async_copy(
-            inverse.at[sub_of(slot, half, role), part], into.at[part], sems.at[slot * steps + step]
+            inverse.at[sub_of(slot, half, role), part],
+            kept.at[slot] if last else land.at[slot, part],
+            sems.at[slot * steps + step],
         )
 
+    order = [(slot, step) for slot in range(half, subs) for step in range(steps)]
+    order += [(slot, step) for step in range(steps) for slot in range(half)]
     first = pltpu.make_async_copy(rhs, held, rhs_sem)
     first.start()
-    for slot in [*range(half, 2 * half), *range(half)]:
-        for step in range(steps):
-            fetch(slot, step).start()
+    for slot, step in order:
+        fetch(slot, step).start()
     first.wait()
-    for slot in range(half, 2 * half):
+    for slot, step in order:
+        fetch(slot, step).wait()
+        if slot < half and step == steps - 1:
+            continue
+        part = pl.ds(step * chunk, chunk)
+        out, at = (begun, slot) if slot < half else (other, slot - half)
         value = held[sub_of(slot, half, role)]
-        for step in range(steps):
-            part = pl.ds(step * chunk, chunk)
-            fetch(slot, step).wait()
-            other[slot - half, :, part] = dot3(value, split(land[slot - half, part]), ROWS_OF)
-    for slot in range(half):
-        for step in range(steps):
-            fetch(slot, step).wait()
-
-
-def rest_kernel(rhs, kept, mine):
-    half = kept.shape[0]
+        out[at, :, part] = dot3(value, split(land[slot, part]), ROWS_OF)
+
+
+def rest_kernel(rhs, begun, kept, mine):
+    half, chunk, _ = kept.shape
+    done = begun.shape[2]
     role = role_of(lax.axis_index("col"))
     for slot in range(half):
-        mine[slot] = dot3(rhs[sub_of(slot, half, role)], split(kept[slot]), ROWS_OF)
+        value = rhs[sub_of(slot, half, role)]
+        mine[slot, :, :done] = begun[slot]
+        mine[slot, :, done:] = dot3(value, split(kept[slot]), ROWS_OF)
 
 
 def couple_kernel(first, vectors, update, out):
@@ -340,16 +346,20 @@
 
     vec = jax.ShapeDtypeStruct((half, nrhs, leaf_rows), F32)
     leaf_flops = 2 * nrhs * leaf_inverse.size
-    half_shape = (half, leaf_rows, leaf_cols)
-    other, kept = pl.pallas_call(
+    chunk = chunk_of(leaf_rows)
+    other, begun, kept = pl.pallas_call(
         leaf_kernel,
-        out_shape=[pltpu.VMEM(vec.shape, F32), pltpu.VMEM(half_shape, F32)],
+        out_shape=[
+            pltpu.VMEM(vec.shape, F32),
+            pltpu.VMEM((half, nrhs, leaf_rows - chunk), F32),
+            pltpu.VMEM((half, chunk, leaf_cols), F32),
+        ],
         in_specs=[HBM, HBM],
-        out_specs=[WHOLE, pl.BlockSpec(memory_space=pl.ANY)],
+        out_specs=[WHOLE, WHOLE, pl.BlockSpec(memory_space=pl.ANY)],
         scratch_shapes=[
             pltpu.VMEM(leaf_rhs.shape, F32),
-            pltpu.VMEM(half_shape, F32),
-            pltpu.SemaphoreType.DMA((subs * (leaf_rows // chunk_of(leaf_rows)),)),
+            pltpu.VMEM(leaf_inverse.shape, F32),
+            pltpu.SemaphoreType.DMA((subs * (leaf_rows // chunk),)),
             pltpu.SemaphoreType.DMA,
         ],
         compiler_params=pltpu.CompilerParams(vmem_limit_bytes=LIMIT * MIB),
@@ -358,8 +368,8 @@
         ),
     )(in_hbm(leaf_rhs), in_hbm(leaf_inverse))
     arrived = swap(other, "col", cols, 1)
-    mine = call(rest_kernel, vec, [WHOLE, WHOLE], 12, (leaf_flops // 2, 2 * leaf_inverse.size))(
-        leaf_rhs, in_vmem(kept)
+    mine = call(rest_kernel, vec, [WHOLE] * 3, 12, (leaf_flops // 4, leaf_inverse.size))(
+        leaf_rhs, begun, in_vmem(kept)
     )
     mine = mine + arrived
     arrived, update = beside(swap(mine, "col", cols, CORES + 1), update_rows)
@@ -375,7 +385,7 @@
         for first, vectors in ((0, mine), (half, other))
     ]
     coupled = jnp.concatenate(coupled, 1)
-    arrived = [swap(coupled, "row", rows, k) for k in range(1, rows)]
+    arrived = [swap(coupled, "row", rows, k) for k in reversed(range(1, rows))]
     inside = sep_rows % BLOCK == 0
     prepared = pl.pallas_call(
         functools.partial(prepare_kernel, inside),
@@ -441,10 +451,10 @@
         keep = jnp.concatenate([keep, own[0]], 2)
         send = jnp.concatenate([send, own[1]], 2)
     keep = keep + swap(send, "col", cols, 1)
-    pulled = keep[0] + sum(swap(keep[m], plane_axes, plane_size, CORES * m + 1) for m in range(1, chips))
+    pulled = keep[0] + sum(swap(keep[m], plane_axes, plane_size, CORES * m + 1) for m in reversed(range(1, chips)))
     own = pulled[:, subs * up :]
     pulled = pulled[:, : subs * up]
-    pulled = pulled + sum(swap(pulled, "row", rows, k) for k in range(1, rows))
+    pulled = pulled + sum(swap(pulled, "row", rows, k) for k in reversed(range(1, rows)))
 
     pull_other, pull_mine = (
         call(

time: 70.4 us -> 69.7 us (0.990)
  waiting for transfers between devices: 28.3 us -> 27.3 us
    ppermute x23, waiting for transfers between devices: 28.3 us -> 27.3 us  [swap(): return lax.ppermute(value, axes, [(i, i ^ mask) for i in range(size)])]
    ppermute x23, starting transfers between devices: 23.7 us -> 24.4 us  [swap(): return lax.ppermute(value, axes, [(i, i ^ mask) for i in range(size)])]
  transfers between devices with their start and end apart: 23 -> 23, of which waited for: 19 -> 19; matrix products, arithmetic and copies ran while one was open for 0% -> 0% of each run, Pallas kernels for 14% -> 13%
where the time goes in v7:
time: 69.7 us; the launch traced here: 69.5 us
  waiting for transfers between devices  27.3 us (39%)
  starting transfers between devices  24.4 us (35%)
  Pallas kernels  16.7 us (24%)
  between operations  0.86 us (1%)
    ppermute x23, waiting for transfers between devices, swap(): return lax.ppermute(value, axes, [(i, i ^ mask) for i in range(size)])  27.3 us
    ppermute x23, starting transfers between devices, swap(): return lax.ppermute(value, axes, [(i, i ^ mask) for i in range(size)])  24.4 us
    pallas_call x1, Pallas kernels, body(): pl.pallas_call(leaf_kernel, out_shape=[pltpu.VMEM(vec.shape, F32), pltpu....  3.82 us
    pallas_call x1, Pallas kernels, body(): pl.pallas_call(functools.partial(prepare_kernel, inside), out_shape=[pltp...  2.63 us
    pallas_call x1, Pallas kernels, beside(): pl.pallas_call(load_kernel, out_shape=pltpu.VMEM(value.shape, value.dtype...  2.24 us
    pallas_call x4, Pallas kernels, parts_of(): call(functools.partial(solve_parts_kernel, rows, masks, first), (jax.Shap...  1.91 us
    pallas_call x1, Pallas kernels, body(): call(functools.partial(separator_kernel, shape, inside), (piece, jax.Shap...  1.45 us
  transfers between devices with their start and end apart: 23, of which 19 were waited for; matrix products, arithmetic and copies ran while one was open for 0% of the time, Pallas kernels for 13%

profile of v7, /device:TPU:0, one launch (start us, length us, event | category | flops | bytes accessed | tf_op | source)
XLA Modules:
  0.0 69.5 jit_solution(5948581495494979367)
XLA Ops:
  0.6 3.8 %shard_map.77 = (f32[1,16,1024]{2,1,0:T(8,128)S(1)}, f32[1,16,512]{2,1,0:T(8,128)S(1)}, f32[1,512,1024]{2,1,0:T(8,128)S(1)}) custom-call(f32[2,16,1024]{2,1,0:T(8,128)} %rhs.4, f32[2,1024,1024]{2,1,0:T(8,128)} %inverse.9), custom_call_target="tpu_custom_call" | custom-call | flops 67108864 | bytes 8388608 | tf_op jit(solution)/shard_map/pallas_call | solution.py:350
  4.5 0.5 collective-permute-start
  5.0 0.7 shard_map.78
  5.7 0.2 collective-permute-done
  5.9 2.7 %collective-permute-start.1 = (f32[1,16,1024]{2,1,0:T(8,128)S(1)}, f32[1,16,1024]{2,1,0:T(8,128)S(1)}, u32[]{:S(2)}, u32[]{:S(2)}) collective-permute-start(f32[1,16,1024]{2,1,0:T(8,128)S(1)} %add.44), channel_id=1, source_target_pairs={{0,3},{1,2},{2,1},{3,0},{4,7},{5,6},{6,5},{7,4},{8,11},{9,10},{10,... | collective-permute-start | bytes 196616 | tf_op jit(solution)/shard_map/ppermute | solution.py:289
  8.6 2.2 %shard_map.79.update = f32[2,512,1024]{2,1,0:T(8,128)S(1)} custom-call(f32[2,512,1024]{2,1,0:T(8,128)} %update.3), custom_call_target="tpu_custom_call" | custom-call | bytes 4194304 | tf_op jit(solution)/shard_map/pallas_call | solution.py:299
  10.9 0.4 collective-permute-start.2
  11.3 0.7 shard_map.80
  12.2 0.7 shard_map.81
  12.9 2.2 %collective-permute-start.5 = (f32[16,1024]{1,0:T(8,128)S(1)}, f32[16,1024]{1,0:T(8,128)S(1)}, u32[]{:S(2)}, u32[]{:S(2)}) collective-permute-start(f32[16,1024]{1,0:T(8,128)S(1)} %pad_maximum_fusion.1), channel_id=1, source_target_pairs={{0,4},{4,0},{8,12},{12,8},{1,5},{5,1},{9,13},{13,9},{2,6},{6,2},{1... | collective-permute-start | bytes 196616 | tf_op jit(solution)/shard_map/ppermute | solution.py:289
  15.0 2.6 %collective-permute-start.4 = (f32[16,1024]{1,0:T(8,128)S(1)}, f32[16,1024]{1,0:T(8,128)S(1)}, u32[]{:S(2)}, u32[]{:S(2)}) collective-permute-start(f32[16,1024]{1,0:T(8,128)S(1)} %pad_maximum_fusion.1), channel_id=1, source_target_pairs={{0,8},{4,12},{8,0},{12,4},{1,9},{5,13},{9,1},{13,5},{2,10},{6,14},... | collective-permute-start | bytes 196616 | tf_op jit(solution)/shard_map/ppermute | solution.py:289
  17.6 2.6 %shard_map.82 = (bf16[256,4096]{1,0:T(8,128)(2,1)S(1)}, bf16[4096,256]{1,0:T(8,128)(2,1)S(1)}) custom-call(f32[128,4096]{1,0:T(8,128)} %sep.1), custom_call_target="tpu_custom_call" | custom-call | bytes 4194304 | tf_op jit(solution)/shard_map/pallas_call | solution.py:390
  20.3 2.3 %collective-permute-done.4 = f32[16,1024]{1,0:T(8,128)S(1)} collective-permute-done((f32[16,1024]{1,0:T(8,128)S(1)}, f32[16,1024]{1,0:T(8,128)S(1)}, u32[]{:S(2)}, u32[]{:S(2)}) %collective-permute-start.4) | collective-permute-done | bytes 65568 | tf_op jit(solution)/shard_map/ppermute | solution.py:289
  22.6 1.2 %collective-permute-done.3 = f32[16,1024]{1,0:T(8,128)S(1)} collective-permute-done((f32[16,1024]{1,0:T(8,128)S(1)}, f32[16,1024]{1,0:T(8,128)S(1)}, u32[]{:S(2)}, u32[]{:S(2)}) %collective-permute-start.3) | collective-permute-done | bytes 65568 | tf_op jit(solution)/shard_map/ppermute | solution.py:289
  23.9 2.7 %collective-permute-start.6 = (f32[16,1152]{1,0:T(8,128)S(1)}, f32[16,1152]{1,0:T(8,128)S(1)}, u32[]{:S(2)}, u32[]{:S(2)}) collective-permute-start(f32[16,1152]{1,0:T(8,128)S(1)} %get-tuple-element.50), channel_id=1, source_target_pairs={{0,3},{1,2},{2,1},{3,0},{16,19},{17,18},{18,17},{19,16},{4,7},{5,6... | collective-permute-start | bytes 221192 | tf_op jit(solution)/shard_map/ppermute | solution.py:289
  26.7 1.8 %collective-permute-done.7 = f32[16,1152]{1,0:T(8,128)S(1)} collective-permute-done((f32[16,1152]{1,0:T(8,128)S(1)}, f32[16,1152]{1,0:T(8,128)S(1)}, u32[]{:S(2)}, u32[]{:S(2)}) %collective-permute-start.7) | collective-permute-done | bytes 73760 | tf_op jit(solution)/shard_map/ppermute | solution.py:289
  28.4 0.2 collective-permute-done.6
  28.7 2.6 %collective-permute-done.8 = f32[16,1152]{1,0:T(8,128)S(1)} collective-permute-done((f32[16,1152]{1,0:T(8,128)S(1)}, f32[16,1152]{1,0:T(8,128)S(1)}, u32[]{:S(2)}, u32[]{:S(2)}) %collective-permute-start.8) | collective-permute-done | bytes 73760 | tf_op jit(solution)/shard_map/ppermute | solution.py:289
  31.4 1.0 %shard_map.83 = (f32[32,16,128]{2,1,0:T(8,128)S(1)}, s32[2,32]{1,0:T(2,128)S(4)}) custom-call(f32[4,16,1152]{2,1,0:T(8,128)S(1)} %pad_maximum_fusion.near, f32[16,4096]{1,0:T(8,128)S(1)} %copy-done.2), custom_call_target="tpu_custom_call" | custom-call | flops 131072 | bytes 786432 | tf_op jit(solution)/shard_map/pallas_call | solution.py:414
  32.5 0.5 collective-permute-done.9.far
  33.0 1.4 %shard_map.84 = (f32[4,16,1536]{2,1,0:T(8,128)S(1)}, f32[32,16,128]{2,1,0:T(8,128)S(1)}) custom-call(s32[2,32]{1,0:T(2,128)S(4)} %get-tuple-element.34.table, f32[4,16,1152]{2,1,0:T(8,128)S(1)} %collective-permute-done.9.far, f32[32,16,128]{2,1,0:T(8,128)S(1)} %get-tuple-element.35.start, bf16[256,4096]{1,0:T(8,128)(2,1)S(1)} %get-tuple-element.36.both, ...), custom_call_target="tpu_custom_call" | custom-call | flops 33554432 | bytes 2097152 | tf_op jit(solution)/shard_map/pallas_call | solution.py:432
  34.7 1.5 %collective-permute-done.10 = f32[4,16,1536]{2,1,0:T(8,128)S(1)} collective-permute-done((f32[4,16,1536]{2,1,0:T(8,128)S(1)}, f32[4,16,1536]{2,1,0:T(8,128)S(1)}, u32[]{:S(2)}, u32[]{:S(2)}) %collective-permute-start.10) | collective-permute-done | bytes 393248 | tf_op jit(solution)/shard_map/ppermute | solution.py:289
  36.3 1.0 %collective-permute-start.12 = (f32[16,1536]{1,0:T(8,128)S(1)}, f32[16,1536]{1,0:T(8,128)S(1)}, u32[]{:S(2)}, u32[]{:S(2)}) collective-permute-start(f32[16,1536]{1,0:T(8,128)S(1)} %get-tuple-element.46), channel_id=1, source_target_pairs={{0,17},{1,16},{2,19},{3,18},{16,1},{17,0},{18,3},{19,2},{4,21},{5,... | collective-permute-start | bytes 294920 | tf_op jit(solution)/shard_map/ppermute | solution.py:289
  37.3 0.5 collective-permute-start.13
  37.8 1.5 %collective-permute-start.11 = (f32[16,1536]{1,0:T(8,128)S(1)}, f32[16,1536]{1,0:T(8,128)S(1)}, u32[]{:S(2)}, u32[]{:S(2)}) collective-permute-start(f32[16,1536]{1,0:T(8,128)S(1)} %get-tuple-element.48), channel_id=1, source_target_pairs={{0,19},{1,18},{2,17},{3,16},{16,3},{17,2},{18,1},{19,0},{4,23},{5,... | collective-permute-start | bytes 294920 | tf_op jit(solution)/shard_map/ppermute | solution.py:289
  39.3 1.8 %collective-permute-done.12 = f32[16,1536]{1,0:T(8,128)S(1)} collective-permute-done((f32[16,1536]{1,0:T(8,128)S(1)}, f32[16,1536]{1,0:T(8,128)S(1)}, u32[]{:S(2)}, u32[]{:S(2)}) %collective-permute-start.12) | collective-permute-done | bytes 98336 | tf_op jit(solution)/shard_map/ppermute | solution.py:289
  41.2 0.9 %collective-permute-done.13 = f32[16,1536]{1,0:T(8,128)S(1)} collective-permute-done((f32[16,1536]{1,0:T(8,128)S(1)}, f32[16,1536]{1,0:T(8,128)S(1)}, u32[]{:S(2)}, u32[]{:S(2)}) %collective-permute-start.13) | collective-permute-done | bytes 98336 | tf_op jit(solution)/shard_map/ppermute | solution.py:289
  42.1 1.9 %collective-permute-done.11 = f32[16,1536]{1,0:T(8,128)S(1)} collective-permute-done((f32[16,1536]{1,0:T(8,128)S(1)}, f32[16,1536]{1,0:T(8,128)S(1)}, u32[]{:S(2)}, u32[]{:S(2)}) %collective-permute-start.11) | collective-permute-done | bytes 98336 | tf_op jit(solution)/shard_map/ppermute | solution.py:289
  44.1 0.9 %collective-permute-start.16 = (f32[16,1024]{1,0:T(8,128)S(1)}, f32[16,1024]{1,0:T(8,128)S(1)}, u32[]{:S(2)}, u32[]{:S(2)}) collective-permute-start(f32[16,1024]{1,0:T(8,128)S(1)} %slice.28), channel_id=1, source_target_pairs={{0,4},{4,0},{8,12},{12,8},{1,5},{5,1},{9,13},{13,9},{2,6},{6,2},{1... | collective-permute-start | bytes 196616 | tf_op jit(solution)/shard_map/ppermute | solution.py:289
  45.0 1.7 %collective-permute-start.15 = (f32[16,1024]{1,0:T(8,128)S(1)}, f32[16,1024]{1,0:T(8,128)S(1)}, u32[]{:S(2)}, u32[]{:S(2)}) collective-permute-start(f32[16,1024]{1,0:T(8,128)S(1)} %slice.28), channel_id=1, source_target_pairs={{0,8},{4,12},{8,0},{12,4},{1,9},{5,13},{9,1},{13,5},{2,10},{6,14},... | collective-permute-start | bytes 196616 | tf_op jit(solution)/shard_map/ppermute | solution.py:289
  46.7 1.8 %collective-permute-start.14 = (f32[16,1024]{1,0:T(8,128)S(1)}, f32[16,1024]{1,0:T(8,128)S(1)}, u32[]{:S(2)}, u32[]{:S(2)}) collective-permute-start(f32[16,1024]{1,0:T(8,128)S(1)} %slice.28), channel_id=1, source_target_pairs={{0,12},{4,8},{8,4},{12,0},{1,13},{5,9},{9,5},{13,1},{2,14},{6,10},... | collective-permute-start | bytes 196616 | tf_op jit(solution)/shard_map/ppermute | solution.py:289
  48.5 4.8 %collective-permute-done.15 = f32[16,1024]{1,0:T(8,128)S(1)} collective-permute-done((f32[16,1024]{1,0:T(8,128)S(1)}, f32[16,1024]{1,0:T(8,128)S(1)}, u32[]{:S(2)}, u32[]{:S(2)}) %collective-permute-start.15) | collective-permute-done | bytes 65568 | tf_op jit(solution)/shard_map/ppermute | solution.py:289
  53.4 0.5 shard_map.87
  53.9 0.5 shard_map.86
  54.3 0.8 %collective-permute-done.17 = f32[1,16,1024]{2,1,0:T(8,128)S(1)} collective-permute-done((f32[1,16,1024]{2,1,0:T(8,128)S(1)}, f32[1,16,1024]{2,1,0:T(8,128)S(1)}, u32[]{:S(2)}, u32[]{:S(2)}) %collective-permute-start.17) | collective-permute-done | bytes 65568 | tf_op jit(solution)/shard_map/ppermute | solution.py:289
  55.1 0.8 %collective-permute-start.18 = (f32[1,16,1024]{2,1,0:T(8,128)S(1)}, f32[1,16,1024]{2,1,0:T(8,128)S(1)}, u32[]{:S(2)}, u32[]{:S(2)}) collective-permute-start(f32[1,16,1024]{2,1,0:T(8,128)S(1)} %add.56), channel_id=1, source_target_pairs={{0,3},{1,2},{2,1},{3,0},{4,7},{5,6},{6,5},{7,4},{8,11},{9,10},{10,... | collective-permute-start | bytes 196616 | tf_op jit(solution)/shard_map/ppermute | solution.py:289
  55.9 3.3 %collective-permute-done.18 = f32[1,16,1024]{2,1,0:T(8,128)S(1)} collective-permute-done((f32[1,16,1024]{2,1,0:T(8,128)S(1)}, f32[1,16,1024]{2,1,0:T(8,128)S(1)}, u32[]{:S(2)}, u32[]{:S(2)}) %collective-permute-start.18) | collective-permute-done | bytes 65568 | tf_op jit(solution)/shard_map/ppermute | solution.py:289
  59.3 0.2 collective-permute-start.19
  59.5 0.3 shard_map.88
  59.8 0.7 shard_map.90
  60.6 0.7 shard_map.91
  61.3 2.2 %collective-permute-start.22 = (f32[16,640]{1,0:T(8,128)S(1)}, f32[16,640]{1,0:T(8,128)S(1)}, u32[]{:S(2)}, u32[]{:S(2)}) collective-permute-start(f32[16,640]{1,0:T(8,128)S(1)} %pad_maximum_fusion.5), channel_id=1, source_target_pairs={{0,12},{4,8},{8,4},{12,0},{1,13},{5,9},{9,5},{13,1},{2,14},{6,10},... | collective-permute-start | bytes 122888 | tf_op jit(solution)/shard_map/ppermute | solution.py:289
  63.4 0.8 %collective-permute-start.21 = (f32[16,640]{1,0:T(8,128)S(1)}, f32[16,640]{1,0:T(8,128)S(1)}, u32[]{:S(2)}, u32[]{:S(2)}) collective-permute-start(f32[16,640]{1,0:T(8,128)S(1)} %pad_maximum_fusion.4), channel_id=1, source_target_pairs={{0,8},{4,12},{8,0},{12,4},{1,9},{5,13},{9,1},{13,5},{2,10},{6,14},... | collective-permute-start | bytes 122888 | tf_op jit(solution)/shard_map/ppermute | solution.py:289
  64.2 1.5 %collective-permute-start.20 = (f32[16,640]{1,0:T(8,128)S(1)}, f32[16,640]{1,0:T(8,128)S(1)}, u32[]{:S(2)}, u32[]{:S(2)}) collective-permute-start(f32[16,640]{1,0:T(8,128)S(1)} %pad_maximum_fusion.3), channel_id=1, source_target_pairs={{0,4},{4,0},{8,12},{12,8},{1,5},{5,1},{9,13},{13,9},{2,6},{6,2},{1... | collective-permute-start | bytes 122888 | tf_op jit(solution)/shard_map/ppermute | solution.py:289
  65.7 0.3 shard_map.89
  66.0 1.2 %collective-permute-done.22.refs_3_ = f32[16,640]{1,0:T(8,128)S(1)} collective-permute-done((f32[16,640]{1,0:T(8,128)S(1)}, f32[16,640]{1,0:T(8,128)S(1)}, u32[]{:S(2)}, u32[]{:S(2)}) %collective-permute-start.22) | collective-permute-done | bytes 40992 | tf_op jit(solution)/shard_map/ppermute | solution.py:289
  67.2 1.6 %collective-permute-done.21.refs_2_ = f32[16,640]{1,0:T(8,128)S(1)} collective-permute-done((f32[16,640]{1,0:T(8,128)S(1)}, f32[16,640]{1,0:T(8,128)S(1)}, u32[]{:S(2)}, u32[]{:S(2)}) %collective-permute-start.21) | collective-permute-done | bytes 40992 | tf_op jit(solution)/shard_map/ppermute | solution.py:289
  68.9 0.6 shard_map.92
  (46 shorter events, 1.1 us)
Async XLA Ops:
  0.6 4.4 %copy-start.1 = (f32[2,16,1024]{2,1,0:T(8,128)S(1)}, f32[2,16,1024]{2,1,0:T(8,128)}, u32[]{:S(2)}) copy-start(f32[2,16,1024]{2,1,0:T(8,128)} %rhs.4) | copy-start | bytes 393220
  4.5 1.4 %collective-permute-start = (f32[1,16,1024]{2,1,0:T(8,128)S(1)}, f32[1,16,1024]{2,1,0:T(8,128)S(1)}, u32[]{:S(2)}, u32[]{:S(2)}) collective-permute-start(f32[1,16,1024]{2,1,0:T(8,128)S(1)} %get-tuple-element.26), channel_id=1, source_target_pairs={{0,1},{1,0},{2,3},{3,2},{4,5},{5,4},{6,7},{7,6},{8,9},{9,8},{10,11... | collective-permute-start | bytes 196616 | tf_op jit(solution)/shard_map/ppermute | solution.py:289
  5.9 4.9 %collective-permute-start.1 = (f32[1,16,1024]{2,1,0:T(8,128)S(1)}, f32[1,16,1024]{2,1,0:T(8,128)S(1)}, u32[]{:S(2)}, u32[]{:S(2)}) collective-permute-start(f32[1,16,1024]{2,1,0:T(8,128)S(1)} %add.44), channel_id=1, source_target_pairs={{0,3},{1,2},{2,1},{3,0},{4,7},{5,6},{6,5},{7,4},{8,11},{9,10},{10,... | collective-permute-start | bytes 196616 | tf_op jit(solution)/shard_map/ppermute | solution.py:289
  10.9 1.3 %collective-permute-start.2 = (f32[1,16,1024]{2,1,0:T(8,128)S(1)}, f32[1,16,1024]{2,1,0:T(8,128)S(1)}, u32[]{:S(2)}, u32[]{:S(2)}) collective-permute-start(f32[1,16,1024]{2,1,0:T(8,128)S(1)} %add.45.vectors), channel_id=1, source_target_pairs={{0,1},{1,0},{2,3},{3,2},{4,5},{5,4},{6,7},{7,6},{8,9},{9,8},{10,11... | collective-permute-start | bytes 196616 | tf_op jit(solution)/shard_map/ppermute | solution.py:289
  12.0 5.7 %copy-start.3 = (s32[2,16]{1,0:T(2,128)S(1)}, s32[2,16]{1,0:T(2,128)}, u32[]{:S(2)}) copy-start(s32[2,16]{1,0:T(2,128)} %param.9) | copy-start | bytes 388
  12.9 18.6 %copy-start.2 = (f32[16,4096]{1,0:T(8,128)S(1)}, f32[16,4096]{1,0:T(8,128)}, u32[]{:S(2)}) copy-start(f32[16,4096]{1,0:T(8,128)} %rhs.5) | copy-start | bytes 786436
  12.9 7.4 %collective-permute-start.5 = (f32[16,1024]{1,0:T(8,128)S(1)}, f32[16,1024]{1,0:T(8,128)S(1)}, u32[]{:S(2)}, u32[]{:S(2)}) collective-permute-start(f32[16,1024]{1,0:T(8,128)S(1)} %pad_maximum_fusion.1), channel_id=1, source_target_pairs={{0,4},{4,0},{8,12},{12,8},{1,5},{5,1},{9,13},{13,9},{2,6},{6,2},{1... | collective-permute-start | bytes 196616 | tf_op jit(solution)/shard_map/ppermute | solution.py:289
  15.0 7.6 %collective-permute-start.4 = (f32[16,1024]{1,0:T(8,128)S(1)}, f32[16,1024]{1,0:T(8,128)S(1)}, u32[]{:S(2)}, u32[]{:S(2)}) collective-permute-start(f32[16,1024]{1,0:T(8,128)S(1)} %pad_maximum_fusion.1), channel_id=1, source_target_pairs={{0,8},{4,12},{8,0},{12,4},{1,9},{5,13},{9,1},{13,5},{2,10},{6,14},... | collective-permute-start | bytes 196616 | tf_op jit(solution)/shard_map/ppermute | solution.py:289
  17.6 6.2 %collective-permute-start.3 = (f32[16,1024]{1,0:T(8,128)S(1)}, f32[16,1024]{1,0:T(8,128)S(1)}, u32[]{:S(2)}, u32[]{:S(2)}) collective-permute-start(f32[16,1024]{1,0:T(8,128)S(1)} %pad_maximum_fusion.1), channel_id=1, source_target_pairs={{0,12},{4,8},{8,4},{12,0},{1,13},{5,9},{9,5},{13,1},{2,14},{6,10},... | collective-permute-start | bytes 196616 | tf_op jit(solution)/shard_map/ppermute | solution.py:289
  23.9 4.6 %collective-permute-start.7 = (f32[16,1152]{1,0:T(8,128)S(1)}, f32[16,1152]{1,0:T(8,128)S(1)}, u32[]{:S(2)}, u32[]{:S(2)}) collective-permute-start(f32[16,1152]{1,0:T(8,128)S(1)} %get-tuple-element.50), channel_id=1, source_target_pairs={{0,17},{1,16},{2,19},{3,18},{16,1},{17,0},{18,3},{19,2},{4,21},{5,... | collective-permute-start | bytes 221192 | tf_op jit(solution)/shard_map/ppermute | solution.py:289
  23.9 4.7 %collective-permute-start.6 = (f32[16,1152]{1,0:T(8,128)S(1)}, f32[16,1152]{1,0:T(8,128)S(1)}, u32[]{:S(2)}, u32[]{:S(2)}) collective-permute-start(f32[16,1152]{1,0:T(8,128)S(1)} %get-tuple-element.50), channel_id=1, source_target_pairs={{0,3},{1,2},{2,1},{3,0},{16,19},{17,18},{18,17},{19,16},{4,7},{5,6... | collective-permute-start | bytes 221192 | tf_op jit(solution)/shard_map/ppermute | solution.py:289
  26.6 4.7 %collective-permute-start.8 = (f32[16,1152]{1,0:T(8,128)S(1)}, f32[16,1152]{1,0:T(8,128)S(1)}, u32[]{:S(2)}, u32[]{:S(2)}) collective-permute-start(f32[16,1152]{1,0:T(8,128)S(1)} %get-tuple-element.50), channel_id=1, source_target_pairs={{0,19},{1,18},{2,17},{3,16},{16,3},{17,2},{18,1},{19,0},{4,23},{5,... | collective-permute-start | bytes 221192 | tf_op jit(solution)/shard_map/ppermute | solution.py:289
  31.3 1.6 %collective-permute-start.9 = (f32[4,16,1152]{2,1,0:T(8,128)S(1)}, f32[4,16,1152]{2,1,0:T(8,128)S(1)}, u32[]{:S(2)}, u32[]{:S(2)}) collective-permute-start(f32[4,16,1152]{2,1,0:T(8,128)S(1)} %pad_maximum_fusion.near), channel_id=1, source_target_pairs={{0,1},{1,0},{2,3},{3,2},{4,5},{5,4},{6,7},{7,6},{8,9},{9,8},{10,11... | collective-permute-start | bytes 884744 | tf_op jit(solution)/shard_map/ppermute | solution.py:289
  33.0 20.4 %copy-start = (f32[2,512,1024]{2,1,0:T(8,128)S(1)}, f32[2,512,1024]{2,1,0:T(8,128)}, u32[]{:S(2)}) copy-start(f32[2,512,1024]{2,1,0:T(8,128)} %update.3) | copy-start | bytes 12582916
  33.0 26.5 %slice-start = ((s8[8388608]{0:T(1024)(128)(4,1)}), s8[4194304]{0:T(1024)(128)(4,1)S(1)}, s32[]{:S(2)}) async-start(s8[8388608]{0:T(1024)(128)(4,1)} %bitcast.15), calls=%async_computation | async-start | bytes 8388608
  34.5 1.8 %collective-permute-start.10 = (f32[4,16,1536]{2,1,0:T(8,128)S(1)}, f32[4,16,1536]{2,1,0:T(8,128)S(1)}, u32[]{:S(2)}, u32[]{:S(2)}) collective-permute-start(f32[4,16,1536]{2,1,0:T(8,128)S(1)} %get-tuple-element.39), channel_id=1, source_target_pairs={{0,1},{1,0},{2,3},{3,2},{4,5},{5,4},{6,7},{7,6},{8,9},{9,8},{10,11... | collective-permute-start | bytes 1179656 | tf_op jit(solution)/shard_map/ppermute | solution.py:289
  36.3 4.8 %collective-permute-start.12 = (f32[16,1536]{1,0:T(8,128)S(1)}, f32[16,1536]{1,0:T(8,128)S(1)}, u32[]{:S(2)}, u32[]{:S(2)}) collective-permute-start(f32[16,1536]{1,0:T(8,128)S(1)} %get-tuple-element.46), channel_id=1, source_target_pairs={{0,17},{1,16},{2,19},{3,18},{16,1},{17,0},{18,3},{19,2},{4,21},{5,... | collective-permute-start | bytes 294920 | tf_op jit(solution)/shard_map/ppermute | solution.py:289
  37.3 4.8 %collective-permute-start.13 = (f32[16,1536]{1,0:T(8,128)S(1)}, f32[16,1536]{1,0:T(8,128)S(1)}, u32[]{:S(2)}, u32[]{:S(2)}) collective-permute-start(f32[16,1536]{1,0:T(8,128)S(1)} %get-tuple-element.47), channel_id=1, source_target_pairs={{0,3},{1,2},{2,1},{3,0},{16,19},{17,18},{18,17},{19,16},{4,7},{5,6... | collective-permute-start | bytes 294920 | tf_op jit(solution)/shard_map/ppermute | solution.py:289
  37.8 6.2 %collective-permute-start.11 = (f32[16,1536]{1,0:T(8,128)S(1)}, f32[16,1536]{1,0:T(8,128)S(1)}, u32[]{:S(2)}, u32[]{:S(2)}) collective-permute-start(f32[16,1536]{1,0:T(8,128)S(1)} %get-tuple-element.48), channel_id=1, source_target_pairs={{0,19},{1,18},{2,17},{3,16},{16,3},{17,2},{18,1},{19,0},{4,23},{5,... | collective-permute-start | bytes 294920 | tf_op jit(solution)/shard_map/ppermute | solution.py:289
  44.1 4.5 %collective-permute-start.16 = (f32[16,1024]{1,0:T(8,128)S(1)}, f32[16,1024]{1,0:T(8,128)S(1)}, u32[]{:S(2)}, u32[]{:S(2)}) collective-permute-start(f32[16,1024]{1,0:T(8,128)S(1)} %slice.28), channel_id=1, source_target_pairs={{0,4},{4,0},{8,12},{12,8},{1,5},{5,1},{9,13},{13,9},{2,6},{6,2},{1... | collective-permute-start | bytes 196616 | tf_op jit(solution)/shard_map/ppermute | solution.py:289
  45.0 8.4 %collective-permute-start.15 = (f32[16,1024]{1,0:T(8,128)S(1)}, f32[16,1024]{1,0:T(8,128)S(1)}, u32[]{:S(2)}, u32[]{:S(2)}) collective-permute-start(f32[16,1024]{1,0:T(8,128)S(1)} %slice.28), channel_id=1, source_target_pairs={{0,8},{4,12},{8,0},{12,4},{1,9},{5,13},{9,1},{13,5},{2,10},{6,14},... | collective-permute-start | bytes 196616 | tf_op jit(solution)/shard_map/ppermute | solution.py:289
  46.7 6.7 %collective-permute-start.14 = (f32[16,1024]{1,0:T(8,128)S(1)}, f32[16,1024]{1,0:T(8,128)S(1)}, u32[]{:S(2)}, u32[]{:S(2)}) collective-permute-start(f32[16,1024]{1,0:T(8,128)S(1)} %slice.28), channel_id=1, source_target_pairs={{0,12},{4,8},{8,4},{12,0},{1,13},{5,9},{9,5},{13,1},{2,14},{6,10},... | collective-permute-start | bytes 196616 | tf_op jit(solution)/shard_map/ppermute | solution.py:289
  53.4 6.1 %slice-start.1 = ((s8[8388608]{0:T(1024)(128)(4,1)}), s8[4194304]{0:T(1024)(128)(4,1)S(1)}, s32[]{:S(2)}) async-start(s8[8388608]{0:T(1024)(128)(4,1)} %bitcast.15), calls=%async_computation.1 | async-start | bytes 8388608
  53.9 1.3 %collective-permute-start.17 = (f32[1,16,1024]{2,1,0:T(8,128)S(1)}, f32[1,16,1024]{2,1,0:T(8,128)S(1)}, u32[]{:S(2)}, u32[]{:S(2)}) collective-permute-start(f32[1,16,1024]{2,1,0:T(8,128)S(1)} %shard_map.87), channel_id=1, source_target_pairs={{0,1},{1,0},{2,3},{3,2},{4,5},{5,4},{6,7},{7,6},{8,9},{9,8},{10,11... | collective-permute-start | bytes 196616 | tf_op jit(solution)/shard_map/ppermute | solution.py:289
  55.1 4.1 %collective-permute-start.18 = (f32[1,16,1024]{2,1,0:T(8,128)S(1)}, f32[1,16,1024]{2,1,0:T(8,128)S(1)}, u32[]{:S(2)}, u32[]{:S(2)}) collective-permute-start(f32[1,16,1024]{2,1,0:T(8,128)S(1)} %add.56), channel_id=1, source_target_pairs={{0,3},{1,2},{2,1},{3,0},{4,7},{5,6},{6,5},{7,4},{8,11},{9,10},{10,... | collective-permute-start | bytes 196616 | tf_op jit(solution)/shard_map/ppermute | solution.py:289
  59.3 1.3 %collective-permute-start.19 = (f32[1,16,1024]{2,1,0:T(8,128)S(1)}, f32[1,16,1024]{2,1,0:T(8,128)S(1)}, u32[]{:S(2)}, u32[]{:S(2)}) collective-permute-start(f32[1,16,1024]{2,1,0:T(8,128)S(1)} %add.57.pull), channel_id=1, source_target_pairs={{0,1},{1,0},{2,3},{3,2},{4,5},{5,4},{6,7},{7,6},{8,9},{9,8},{10,11... | collective-permute-start | bytes 196616 | tf_op jit(solution)/shard_map/ppermute | solution.py:289
  61.3 6.0 %collective-permute-start.22 = (f32[16,640]{1,0:T(8,128)S(1)}, f32[16,640]{1,0:T(8,128)S(1)}, u32[]{:S(2)}, u32[]{:S(2)}) collective-permute-start(f32[16,640]{1,0:T(8,128)S(1)} %pad_maximum_fusion.5), channel_id=1, source_target_pairs={{0,12},{4,8},{8,4},{12,0},{1,13},{5,9},{9,5},{13,1},{2,14},{6,10},... | collective-permute-start | bytes 122888 | tf_op jit(solution)/shard_map/ppermute | solution.py:289
  63.4 5.3 %collective-permute-start.21 = (f32[16,640]{1,0:T(8,128)S(1)}, f32[16,640]{1,0:T(8,128)S(1)}, u32[]{:S(2)}, u32[]{:S(2)}) collective-permute-start(f32[16,640]{1,0:T(8,128)S(1)} %pad_maximum_fusion.4), channel_id=1, source_target_pairs={{0,8},{4,12},{8,0},{12,4},{1,9},{5,13},{9,1},{13,5},{2,10},{6,14},... | collective-permute-start | bytes 122888 | tf_op jit(solution)/shard_map/ppermute | solution.py:289
  64.2 4.7 %collective-permute-start.20 = (f32[16,640]{1,0:T(8,128)S(1)}, f32[16,640]{1,0:T(8,128)S(1)}, u32[]{:S(2)}, u32[]{:S(2)}) collective-permute-start(f32[16,640]{1,0:T(8,128)S(1)} %pad_maximum_fusion.3), channel_id=1, source_target_pairs={{0,4},{4,0},{8,12},{12,8},{1,5},{5,1},{9,13},{13,9},{2,6},{6,2},{1... | collective-permute-start | bytes 122888 | tf_op jit(solution)/shard_map/ppermute | solution.py:289

commit v8 on v7

--- a/solution.py
+++ b/solution.py
@@ -405,7 +405,8 @@
     )
     coupled = jnp.concatenate([coupled, numbers], 1)
     near = jnp.stack(
-        [coupled] + [swap(coupled, plane_axes, plane_size, CORES * m + 1) for m in range(1, chips)]
+        [coupled]
+        + [swap(coupled, plane_axes, plane_size, CORES * m + 1) for m in reversed(range(1, chips))][::-1]
     )
     far = swap(near, "col", cols, 1)
 

time: 69.7 us -> 69.7 us (level)
  no operation moved by 1% of the time
where the time goes in v8:
time: 69.7 us; the launch traced here: 69.5 us
  waiting for transfers between devices  27.3 us (39%)
  starting transfers between devices  24.4 us (35%)
  Pallas kernels  16.7 us (24%)
  between operations  0.86 us (1%)
    ppermute x23, waiting for transfers between devices, swap(): return lax.ppermute(value, axes, [(i, i ^ mask) for i in range(size)])  27.3 us
    ppermute x23, starting transfers between devices, swap(): return lax.ppermute(value, axes, [(i, i ^ mask) for i in range(size)])  24.4 us
    pallas_call x1, Pallas kernels, body(): pl.pallas_call(leaf_kernel, out_shape=[pltpu.VMEM(vec.shape, F32), pltpu....  3.82 us
    pallas_call x1, Pallas kernels, body(): pl.pallas_call(functools.partial(prepare_kernel, inside), out_shape=[pltp...  2.63 us
    pallas_call x1, Pallas kernels, beside(): pl.pallas_call(load_kernel, out_shape=pltpu.VMEM(value.shape, value.dtype...  2.24 us
    pallas_call x4, Pallas kernels, parts_of(): call(functools.partial(solve_parts_kernel, rows, masks, first), (jax.Shap...  1.91 us
    pallas_call x1, Pallas kernels, body(): call(functools.partial(separator_kernel, shape, inside), (piece, jax.Shap...  1.45 us
  transfers between devices with their start and end apart: 23, of which 19 were waited for; matrix products, arithmetic and copies ran while one was open for 0% of the time, Pallas kernels for 13%

profile of v8, /device:TPU:0, one launch (start us, length us, event | category | flops | bytes accessed | tf_op | source)
XLA Modules:
  0.0 69.5 jit_solution(5948581495494979367)
XLA Ops:
  0.6 3.8 %shard_map.77 = (f32[1,16,1024]{2,1,0:T(8,128)S(1)}, f32[1,16,512]{2,1,0:T(8,128)S(1)}, f32[1,512,1024]{2,1,0:T(8,128)S(1)}) custom-call(f32[2,16,1024]{2,1,0:T(8,128)} %rhs.4, f32[2,1024,1024]{2,1,0:T(8,128)} %inverse.9), custom_call_target="tpu_custom_call" | custom-call | flops 67108864 | bytes 8388608 | tf_op jit(solution)/shard_map/pallas_call | solution.py:350
  4.5 0.5 collective-permute-start
  5.0 0.7 shard_map.78
  5.7 0.2 collective-permute-done
  5.9 2.7 %collective-permute-start.1 = (f32[1,16,1024]{2,1,0:T(8,128)S(1)}, f32[1,16,1024]{2,1,0:T(8,128)S(1)}, u32[]{:S(2)}, u32[]{:S(2)}) collective-permute-start(f32[1,16,1024]{2,1,0:T(8,128)S(1)} %add.44), channel_id=1, source_target_pairs={{0,3},{1,2},{2,1},{3,0},{4,7},{5,6},{6,5},{7,4},{8,11},{9,10},{10,... | collective-permute-start | bytes 196616 | tf_op jit(solution)/shard_map/ppermute | solution.py:289
  8.6 2.2 %shard_map.79.update = f32[2,512,1024]{2,1,0:T(8,128)S(1)} custom-call(f32[2,512,1024]{2,1,0:T(8,128)} %update.3), custom_call_target="tpu_custom_call" | custom-call | bytes 4194304 | tf_op jit(solution)/shard_map/pallas_call | solution.py:299
  10.9 0.4 collective-permute-start.2
  11.3 0.7 shard_map.80
  12.2 0.7 shard_map.81
  12.9 2.2 %collective-permute-start.5 = (f32[16,1024]{1,0:T(8,128)S(1)}, f32[16,1024]{1,0:T(8,128)S(1)}, u32[]{:S(2)}, u32[]{:S(2)}) collective-permute-start(f32[16,1024]{1,0:T(8,128)S(1)} %pad_maximum_fusion.1), channel_id=1, source_target_pairs={{0,4},{4,0},{8,12},{12,8},{1,5},{5,1},{9,13},{13,9},{2,6},{6,2},{1... | collective-permute-start | bytes 196616 | tf_op jit(solution)/shard_map/ppermute | solution.py:289
  15.0 2.6 %collective-permute-start.4 = (f32[16,1024]{1,0:T(8,128)S(1)}, f32[16,1024]{1,0:T(8,128)S(1)}, u32[]{:S(2)}, u32[]{:S(2)}) collective-permute-start(f32[16,1024]{1,0:T(8,128)S(1)} %pad_maximum_fusion.1), channel_id=1, source_target_pairs={{0,8},{4,12},{8,0},{12,4},{1,9},{5,13},{9,1},{13,5},{2,10},{6,14},... | collective-permute-start | bytes 196616 | tf_op jit(solution)/shard_map/ppermute | solution.py:289
  17.6 2.6 %shard_map.82 = (bf16[256,4096]{1,0:T(8,128)(2,1)S(1)}, bf16[4096,256]{1,0:T(8,128)(2,1)S(1)}) custom-call(f32[128,4096]{1,0:T(8,128)} %sep.1), custom_call_target="tpu_custom_call" | custom-call | bytes 4194304 | tf_op jit(solution)/shard_map/pallas_call | solution.py:390
  20.3 2.3 %collective-permute-done.4 = f32[16,1024]{1,0:T(8,128)S(1)} collective-permute-done((f32[16,1024]{1,0:T(8,128)S(1)}, f32[16,1024]{1,0:T(8,128)S(1)}, u32[]{:S(2)}, u32[]{:S(2)}) %collective-permute-start.4) | collective-permute-done | bytes 65568 | tf_op jit(solution)/shard_map/ppermute | solution.py:289
  22.6 1.2 %collective-permute-done.3 = f32[16,1024]{1,0:T(8,128)S(1)} collective-permute-done((f32[16,1024]{1,0:T(8,128)S(1)}, f32[16,1024]{1,0:T(8,128)S(1)}, u32[]{:S(2)}, u32[]{:S(2)}) %collective-permute-start.3) | collective-permute-done | bytes 65568 | tf_op jit(solution)/shard_map/ppermute | solution.py:289
  23.9 2.7 %collective-permute-start.6 = (f32[16,1152]{1,0:T(8,128)S(1)}, f32[16,1152]{1,0:T(8,128)S(1)}, u32[]{:S(2)}, u32[]{:S(2)}) collective-permute-start(f32[16,1152]{1,0:T(8,128)S(1)} %get-tuple-element.50), channel_id=1, source_target_pairs={{0,3},{1,2},{2,1},{3,0},{16,19},{17,18},{18,17},{19,16},{4,7},{5,6... | collective-permute-start | bytes 221192 | tf_op jit(solution)/shard_map/ppermute | solution.py:289
  26.7 1.8 %collective-permute-done.7 = f32[16,1152]{1,0:T(8,128)S(1)} collective-permute-done((f32[16,1152]{1,0:T(8,128)S(1)}, f32[16,1152]{1,0:T(8,128)S(1)}, u32[]{:S(2)}, u32[]{:S(2)}) %collective-permute-start.7) | collective-permute-done | bytes 73760 | tf_op jit(solution)/shard_map/ppermute | solution.py:289
  28.4 0.2 collective-permute-done.6
  28.7 2.6 %collective-permute-done.8 = f32[16,1152]{1,0:T(8,128)S(1)} collective-permute-done((f32[16,1152]{1,0:T(8,128)S(1)}, f32[16,1152]{1,0:T(8,128)S(1)}, u32[]{:S(2)}, u32[]{:S(2)}) %collective-permute-start.8) | collective-permute-done | bytes 73760 | tf_op jit(solution)/shard_map/ppermute | solution.py:289
  31.4 1.0 %shard_map.83 = (f32[32,16,128]{2,1,0:T(8,128)S(1)}, s32[2,32]{1,0:T(2,128)S(4)}) custom-call(f32[4,16,1152]{2,1,0:T(8,128)S(1)} %pad_maximum_fusion.near, f32[16,4096]{1,0:T(8,128)S(1)} %copy-done.2), custom_call_target="tpu_custom_call" | custom-call | flops 131072 | bytes 786432 | tf_op jit(solution)/shard_map/pallas_call | solution.py:415
  32.5 0.5 collective-permute-done.9.far
  33.0 1.4 %shard_map.84 = (f32[4,16,1536]{2,1,0:T(8,128)S(1)}, f32[32,16,128]{2,1,0:T(8,128)S(1)}) custom-call(s32[2,32]{1,0:T(2,128)S(4)} %get-tuple-element.34.table, f32[4,16,1152]{2,1,0:T(8,128)S(1)} %collective-permute-done.9.far, f32[32,16,128]{2,1,0:T(8,128)S(1)} %get-tuple-element.35.start, bf16[256,4096]{1,0:T(8,128)(2,1)S(1)} %get-tuple-element.36.both, ...), custom_call_target="tpu_custom_call" | custom-call | flops 33554432 | bytes 2097152 | tf_op jit(solution)/shard_map/pallas_call | solution.py:433
  34.7 1.5 %collective-permute-done.10 = f32[4,16,1536]{2,1,0:T(8,128)S(1)} collective-permute-done((f32[4,16,1536]{2,1,0:T(8,128)S(1)}, f32[4,16,1536]{2,1,0:T(8,128)S(1)}, u32[]{:S(2)}, u32[]{:S(2)}) %collective-permute-start.10) | collective-permute-done | bytes 393248 | tf_op jit(solution)/shard_map/ppermute | solution.py:289
  36.3 1.0 %collective-permute-start.12 = (f32[16,1536]{1,0:T(8,128)S(1)}, f32[16,1536]{1,0:T(8,128)S(1)}, u32[]{:S(2)}, u32[]{:S(2)}) collective-permute-start(f32[16,1536]{1,0:T(8,128)S(1)} %get-tuple-element.46), channel_id=1, source_target_pairs={{0,17},{1,16},{2,19},{3,18},{16,1},{17,0},{18,3},{19,2},{4,21},{5,... | collective-permute-start | bytes 294920 | tf_op jit(solution)/shard_map/ppermute | solution.py:289
  37.3 0.5 collective-permute-start.13
  37.8 1.5 %collective-permute-start.11 = (f32[16,1536]{1,0:T(8,128)S(1)}, f32[16,1536]{1,0:T(8,128)S(1)}, u32[]{:S(2)}, u32[]{:S(2)}) collective-permute-start(f32[16,1536]{1,0:T(8,128)S(1)} %get-tuple-element.48), channel_id=1, source_target_pairs={{0,19},{1,18},{2,17},{3,16},{16,3},{17,2},{18,1},{19,0},{4,23},{5,... | collective-permute-start | bytes 294920 | tf_op jit(solution)/shard_map/ppermute | solution.py:289
  39.3 1.8 %collective-permute-done.12 = f32[16,1536]{1,0:T(8,128)S(1)} collective-permute-done((f32[16,1536]{1,0:T(8,128)S(1)}, f32[16,1536]{1,0:T(8,128)S(1)}, u32[]{:S(2)}, u32[]{:S(2)}) %collective-permute-start.12) | collective-permute-done | bytes 98336 | tf_op jit(solution)/shard_map/ppermute | solution.py:289
  41.2 0.9 %collective-permute-done.13 = f32[16,1536]{1,0:T(8,128)S(1)} collective-permute-done((f32[16,1536]{1,0:T(8,128)S(1)}, f32[16,1536]{1,0:T(8,128)S(1)}, u32[]{:S(2)}, u32[]{:S(2)}) %collective-permute-start.13) | collective-permute-done | bytes 98336 | tf_op jit(solution)/shard_map/ppermute | solution.py:289
  42.1 1.9 %collective-permute-done.11 = f32[16,1536]{1,0:T(8,128)S(1)} collective-permute-done((f32[16,1536]{1,0:T(8,128)S(1)}, f32[16,1536]{1,0:T(8,128)S(1)}, u32[]{:S(2)}, u32[]{:S(2)}) %collective-permute-start.11) | collective-permute-done | bytes 98336 | tf_op jit(solution)/shard_map/ppermute | solution.py:289
  44.1 0.9 %collective-permute-start.16 = (f32[16,1024]{1,0:T(8,128)S(1)}, f32[16,1024]{1,0:T(8,128)S(1)}, u32[]{:S(2)}, u32[]{:S(2)}) collective-permute-start(f32[16,1024]{1,0:T(8,128)S(1)} %slice.28), channel_id=1, source_target_pairs={{0,4},{4,0},{8,12},{12,8},{1,5},{5,1},{9,13},{13,9},{2,6},{6,2},{1... | collective-permute-start | bytes 196616 | tf_op jit(solution)/shard_map/ppermute | solution.py:289
  45.0 1.7 %collective-permute-start.15 = (f32[16,1024]{1,0:T(8,128)S(1)}, f32[16,1024]{1,0:T(8,128)S(1)}, u32[]{:S(2)}, u32[]{:S(2)}) collective-permute-start(f32[16,1024]{1,0:T(8,128)S(1)} %slice.28), channel_id=1, source_target_pairs={{0,8},{4,12},{8,0},{12,4},{1,9},{5,13},{9,1},{13,5},{2,10},{6,14},... | collective-permute-start | bytes 196616 | tf_op jit(solution)/shard_map/ppermute | solution.py:289
  46.7 1.8 %collective-permute-start.14 = (f32[16,1024]{1,0:T(8,128)S(1)}, f32[16,1024]{1,0:T(8,128)S(1)}, u32[]{:S(2)}, u32[]{:S(2)}) collective-permute-start(f32[16,1024]{1,0:T(8,128)S(1)} %slice.28), channel_id=1, source_target_pairs={{0,12},{4,8},{8,4},{12,0},{1,13},{5,9},{9,5},{13,1},{2,14},{6,10},... | collective-permute-start | bytes 196616 | tf_op jit(solution)/shard_map/ppermute | solution.py:289
  48.5 4.8 %collective-permute-done.15 = f32[16,1024]{1,0:T(8,128)S(1)} collective-permute-done((f32[16,1024]{1,0:T(8,128)S(1)}, f32[16,1024]{1,0:T(8,128)S(1)}, u32[]{:S(2)}, u32[]{:S(2)}) %collective-permute-start.15) | collective-permute-done | bytes 65568 | tf_op jit(solution)/shard_map/ppermute | solution.py:289
  53.4 0.5 shard_map.87
  53.9 0.5 shard_map.86
  54.3 0.8 %collective-permute-done.17 = f32[1,16,1024]{2,1,0:T(8,128)S(1)} collective-permute-done((f32[1,16,1024]{2,1,0:T(8,128)S(1)}, f32[1,16,1024]{2,1,0:T(8,128)S(1)}, u32[]{:S(2)}, u32[]{:S(2)}) %collective-permute-start.17) | collective-permute-done | bytes 65568 | tf_op jit(solution)/shard_map/ppermute | solution.py:289
  55.1 0.8 %collective-permute-start.18 = (f32[1,16,1024]{2,1,0:T(8,128)S(1)}, f32[1,16,1024]{2,1,0:T(8,128)S(1)}, u32[]{:S(2)}, u32[]{:S(2)}) collective-permute-start(f32[1,16,1024]{2,1,0:T(8,128)S(1)} %add.56), channel_id=1, source_target_pairs={{0,3},{1,2},{2,1},{3,0},{4,7},{5,6},{6,5},{7,4},{8,11},{9,10},{10,... | collective-permute-start | bytes 196616 | tf_op jit(solution)/shard_map/ppermute | solution.py:289
  55.9 3.3 %collective-permute-done.18 = f32[1,16,1024]{2,1,0:T(8,128)S(1)} collective-permute-done((f32[1,16,1024]{2,1,0:T(8,128)S(1)}, f32[1,16,1024]{2,1,0:T(8,128)S(1)}, u32[]{:S(2)}, u32[]{:S(2)}) %collective-permute-start.18) | collective-permute-done | bytes 65568 | tf_op jit(solution)/shard_map/ppermute | solution.py:289
  59.3 0.2 collective-permute-start.19
  59.5 0.3 shard_map.88
  59.8 0.7 shard_map.90
  60.6 0.7 shard_map.91
  61.3 2.2 %collective-permute-start.22 = (f32[16,640]{1,0:T(8,128)S(1)}, f32[16,640]{1,0:T(8,128)S(1)}, u32[]{:S(2)}, u32[]{:S(2)}) collective-permute-start(f32[16,640]{1,0:T(8,128)S(1)} %pad_maximum_fusion.5), channel_id=1, source_target_pairs={{0,12},{4,8},{8,4},{12,0},{1,13},{5,9},{9,5},{13,1},{2,14},{6,10},... | collective-permute-start | bytes 122888 | tf_op jit(solution)/shard_map/ppermute | solution.py:289
  63.4 0.8 %collective-permute-start.21 = (f32[16,640]{1,0:T(8,128)S(1)}, f32[16,640]{1,0:T(8,128)S(1)}, u32[]{:S(2)}, u32[]{:S(2)}) collective-permute-start(f32[16,640]{1,0:T(8,128)S(1)} %pad_maximum_fusion.4), channel_id=1, source_target_pairs={{0,8},{4,12},{8,0},{12,4},{1,9},{5,13},{9,1},{13,5},{2,10},{6,14},... | collective-permute-start | bytes 122888 | tf_op jit(solution)/shard_map/ppermute | solution.py:289
  64.2 1.5 %collective-permute-start.20 = (f32[16,640]{1,0:T(8,128)S(1)}, f32[16,640]{1,0:T(8,128)S(1)}, u32[]{:S(2)}, u32[]{:S(2)}) collective-permute-start(f32[16,640]{1,0:T(8,128)S(1)} %pad_maximum_fusion.3), channel_id=1, source_target_pairs={{0,4},{4,0},{8,12},{12,8},{1,5},{5,1},{9,13},{13,9},{2,6},{6,2},{1... | collective-permute-start | bytes 122888 | tf_op jit(solution)/shard_map/ppermute | solution.py:289
  65.7 0.3 shard_map.89
  66.0 1.2 %collective-permute-done.22.refs_3_ = f32[16,640]{1,0:T(8,128)S(1)} collective-permute-done((f32[16,640]{1,0:T(8,128)S(1)}, f32[16,640]{1,0:T(8,128)S(1)}, u32[]{:S(2)}, u32[]{:S(2)}) %collective-permute-start.22) | collective-permute-done | bytes 40992 | tf_op jit(solution)/shard_map/ppermute | solution.py:289
  67.2 1.5 %collective-permute-done.21.refs_2_ = f32[16,640]{1,0:T(8,128)S(1)} collective-permute-done((f32[16,640]{1,0:T(8,128)S(1)}, f32[16,640]{1,0:T(8,128)S(1)}, u32[]{:S(2)}, u32[]{:S(2)}) %collective-permute-start.21) | collective-permute-done | bytes 40992 | tf_op jit(solution)/shard_map/ppermute | solution.py:289
  68.9 0.6 shard_map.92
  (46 shorter events, 1.1 us)
Async XLA Ops:
  0.6 4.4 %copy-start.1 = (f32[2,16,1024]{2,1,0:T(8,128)S(1)}, f32[2,16,1024]{2,1,0:T(8,128)}, u32[]{:S(2)}) copy-start(f32[2,16,1024]{2,1,0:T(8,128)} %rhs.4) | copy-start | bytes 393220
  4.5 1.4 %collective-permute-start = (f32[1,16,1024]{2,1,0:T(8,128)S(1)}, f32[1,16,1024]{2,1,0:T(8,128)S(1)}, u32[]{:S(2)}, u32[]{:S(2)}) collective-permute-start(f32[1,16,1024]{2,1,0:T(8,128)S(1)} %get-tuple-element.26), channel_id=1, source_target_pairs={{0,1},{1,0},{2,3},{3,2},{4,5},{5,4},{6,7},{7,6},{8,9},{9,8},{10,11... | collective-permute-start | bytes 196616 | tf_op jit(solution)/shard_map/ppermute | solution.py:289
  5.9 4.9 %collective-permute-start.1 = (f32[1,16,1024]{2,1,0:T(8,128)S(1)}, f32[1,16,1024]{2,1,0:T(8,128)S(1)}, u32[]{:S(2)}, u32[]{:S(2)}) collective-permute-start(f32[1,16,1024]{2,1,0:T(8,128)S(1)} %add.44), channel_id=1, source_target_pairs={{0,3},{1,2},{2,1},{3,0},{4,7},{5,6},{6,5},{7,4},{8,11},{9,10},{10,... | collective-permute-start | bytes 196616 | tf_op jit(solution)/shard_map/ppermute | solution.py:289
  10.9 1.3 %collective-permute-start.2 = (f32[1,16,1024]{2,1,0:T(8,128)S(1)}, f32[1,16,1024]{2,1,0:T(8,128)S(1)}, u32[]{:S(2)}, u32[]{:S(2)}) collective-permute-start(f32[1,16,1024]{2,1,0:T(8,128)S(1)} %add.45.vectors), channel_id=1, source_target_pairs={{0,1},{1,0},{2,3},{3,2},{4,5},{5,4},{6,7},{7,6},{8,9},{9,8},{10,11... | collective-permute-start | bytes 196616 | tf_op jit(solution)/shard_map/ppermute | solution.py:289
  12.0 5.7 %copy-start.3 = (s32[2,16]{1,0:T(2,128)S(1)}, s32[2,16]{1,0:T(2,128)}, u32[]{:S(2)}) copy-start(s32[2,16]{1,0:T(2,128)} %param.9) | copy-start | bytes 388
  12.9 18.6 %copy-start.2 = (f32[16,4096]{1,0:T(8,128)S(1)}, f32[16,4096]{1,0:T(8,128)}, u32[]{:S(2)}) copy-start(f32[16,4096]{1,0:T(8,128)} %rhs.5) | copy-start | bytes 786436
  12.9 7.4 %collective-permute-start.5 = (f32[16,1024]{1,0:T(8,128)S(1)}, f32[16,1024]{1,0:T(8,128)S(1)}, u32[]{:S(2)}, u32[]{:S(2)}) collective-permute-start(f32[16,1024]{1,0:T(8,128)S(1)} %pad_maximum_fusion.1), channel_id=1, source_target_pairs={{0,4},{4,0},{8,12},{12,8},{1,5},{5,1},{9,13},{13,9},{2,6},{6,2},{1... | collective-permute-start | bytes 196616 | tf_op jit(solution)/shard_map/ppermute | solution.py:289
  15.0 7.6 %collective-permute-start.4 = (f32[16,1024]{1,0:T(8,128)S(1)}, f32[16,1024]{1,0:T(8,128)S(1)}, u32[]{:S(2)}, u32[]{:S(2)}) collective-permute-start(f32[16,1024]{1,0:T(8,128)S(1)} %pad_maximum_fusion.1), channel_id=1, source_target_pairs={{0,8},{4,12},{8,0},{12,4},{1,9},{5,13},{9,1},{13,5},{2,10},{6,14},... | collective-permute-start | bytes 196616 | tf_op jit(solution)/shard_map/ppermute | solution.py:289
  17.6 6.2 %collective-permute-start.3 = (f32[16,1024]{1,0:T(8,128)S(1)}, f32[16,1024]{1,0:T(8,128)S(1)}, u32[]{:S(2)}, u32[]{:S(2)}) collective-permute-start(f32[16,1024]{1,0:T(8,128)S(1)} %pad_maximum_fusion.1), channel_id=1, source_target_pairs={{0,12},{4,8},{8,4},{12,0},{1,13},{5,9},{9,5},{13,1},{2,14},{6,10},... | collective-permute-start | bytes 196616 | tf_op jit(solution)/shard_map/ppermute | solution.py:289
  23.9 4.6 %collective-permute-start.7 = (f32[16,1152]{1,0:T(8,128)S(1)}, f32[16,1152]{1,0:T(8,128)S(1)}, u32[]{:S(2)}, u32[]{:S(2)}) collective-permute-start(f32[16,1152]{1,0:T(8,128)S(1)} %get-tuple-element.50), channel_id=1, source_target_pairs={{0,17},{1,16},{2,19},{3,18},{16,1},{17,0},{18,3},{19,2},{4,21},{5,... | collective-permute-start | bytes 221192 | tf_op jit(solution)/shard_map/ppermute | solution.py:289
  23.9 4.7 %collective-permute-start.6 = (f32[16,1152]{1,0:T(8,128)S(1)}, f32[16,1152]{1,0:T(8,128)S(1)}, u32[]{:S(2)}, u32[]{:S(2)}) collective-permute-start(f32[16,1152]{1,0:T(8,128)S(1)} %get-tuple-element.50), channel_id=1, source_target_pairs={{0,3},{1,2},{2,1},{3,0},{16,19},{17,18},{18,17},{19,16},{4,7},{5,6... | collective-permute-start | bytes 221192 | tf_op jit(solution)/shard_map/ppermute | solution.py:289
  26.6 4.7 %collective-permute-start.8 = (f32[16,1152]{1,0:T(8,128)S(1)}, f32[16,1152]{1,0:T(8,128)S(1)}, u32[]{:S(2)}, u32[]{:S(2)}) collective-permute-start(f32[16,1152]{1,0:T(8,128)S(1)} %get-tuple-element.50), channel_id=1, source_target_pairs={{0,19},{1,18},{2,17},{3,16},{16,3},{17,2},{18,1},{19,0},{4,23},{5,... | collective-permute-start | bytes 221192 | tf_op jit(solution)/shard_map/ppermute | solution.py:289
  31.3 1.6 %collective-permute-start.9 = (f32[4,16,1152]{2,1,0:T(8,128)S(1)}, f32[4,16,1152]{2,1,0:T(8,128)S(1)}, u32[]{:S(2)}, u32[]{:S(2)}) collective-permute-start(f32[4,16,1152]{2,1,0:T(8,128)S(1)} %pad_maximum_fusion.near), channel_id=1, source_target_pairs={{0,1},{1,0},{2,3},{3,2},{4,5},{5,4},{6,7},{7,6},{8,9},{9,8},{10,11... | collective-permute-start | bytes 884744 | tf_op jit(solution)/shard_map/ppermute | solution.py:289
  33.0 20.4 %copy-start = (f32[2,512,1024]{2,1,0:T(8,128)S(1)}, f32[2,512,1024]{2,1,0:T(8,128)}, u32[]{:S(2)}) copy-start(f32[2,512,1024]{2,1,0:T(8,128)} %update.3) | copy-start | bytes 12582916
  33.0 26.5 %slice-start = ((s8[8388608]{0:T(1024)(128)(4,1)}), s8[4194304]{0:T(1024)(128)(4,1)S(1)}, s32[]{:S(2)}) async-start(s8[8388608]{0:T(1024)(128)(4,1)} %bitcast.15), calls=%async_computation | async-start | bytes 8388608
  34.5 1.8 %collective-permute-start.10 = (f32[4,16,1536]{2,1,0:T(8,128)S(1)}, f32[4,16,1536]{2,1,0:T(8,128)S(1)}, u32[]{:S(2)}, u32[]{:S(2)}) collective-permute-start(f32[4,16,1536]{2,1,0:T(8,128)S(1)} %get-tuple-element.39), channel_id=1, source_target_pairs={{0,1},{1,0},{2,3},{3,2},{4,5},{5,4},{6,7},{7,6},{8,9},{9,8},{10,11... | collective-permute-start | bytes 1179656 | tf_op jit(solution)/shard_map/ppermute | solution.py:289
  36.3 4.8 %collective-permute-start.12 = (f32[16,1536]{1,0:T(8,128)S(1)}, f32[16,1536]{1,0:T(8,128)S(1)}, u32[]{:S(2)}, u32[]{:S(2)}) collective-permute-start(f32[16,1536]{1,0:T(8,128)S(1)} %get-tuple-element.46), channel_id=1, source_target_pairs={{0,17},{1,16},{2,19},{3,18},{16,1},{17,0},{18,3},{19,2},{4,21},{5,... | collective-permute-start | bytes 294920 | tf_op jit(solution)/shard_map/ppermute | solution.py:289
  37.3 4.8 %collective-permute-start.13 = (f32[16,1536]{1,0:T(8,128)S(1)}, f32[16,1536]{1,0:T(8,128)S(1)}, u32[]{:S(2)}, u32[]{:S(2)}) collective-permute-start(f32[16,1536]{1,0:T(8,128)S(1)} %get-tuple-element.47), channel_id=1, source_target_pairs={{0,3},{1,2},{2,1},{3,0},{16,19},{17,18},{18,17},{19,16},{4,7},{5,6... | collective-permute-start | bytes 294920 | tf_op jit(solution)/shard_map/ppermute | solution.py:289
  37.8 6.2 %collective-permute-start.11 = (f32[16,1536]{1,0:T(8,128)S(1)}, f32[16,1536]{1,0:T(8,128)S(1)}, u32[]{:S(2)}, u32[]{:S(2)}) collective-permute-start(f32[16,1536]{1,0:T(8,128)S(1)} %get-tuple-element.48), channel_id=1, source_target_pairs={{0,19},{1,18},{2,17},{3,16},{16,3},{17,2},{18,1},{19,0},{4,23},{5,... | collective-permute-start | bytes 294920 | tf_op jit(solution)/shard_map/ppermute | solution.py:289
  44.1 4.5 %collective-permute-start.16 = (f32[16,1024]{1,0:T(8,128)S(1)}, f32[16,1024]{1,0:T(8,128)S(1)}, u32[]{:S(2)}, u32[]{:S(2)}) collective-permute-start(f32[16,1024]{1,0:T(8,128)S(1)} %slice.28), channel_id=1, source_target_pairs={{0,4},{4,0},{8,12},{12,8},{1,5},{5,1},{9,13},{13,9},{2,6},{6,2},{1... | collective-permute-start | bytes 196616 | tf_op jit(solution)/shard_map/ppermute | solution.py:289
  45.0 8.4 %collective-permute-start.15 = (f32[16,1024]{1,0:T(8,128)S(1)}, f32[16,1024]{1,0:T(8,128)S(1)}, u32[]{:S(2)}, u32[]{:S(2)}) collective-permute-start(f32[16,1024]{1,0:T(8,128)S(1)} %slice.28), channel_id=1, source_target_pairs={{0,8},{4,12},{8,0},{12,4},{1,9},{5,13},{9,1},{13,5},{2,10},{6,14},... | collective-permute-start | bytes 196616 | tf_op jit(solution)/shard_map/ppermute | solution.py:289
  46.7 6.7 %collective-permute-start.14 = (f32[16,1024]{1,0:T(8,128)S(1)}, f32[16,1024]{1,0:T(8,128)S(1)}, u32[]{:S(2)}, u32[]{:S(2)}) collective-permute-start(f32[16,1024]{1,0:T(8,128)S(1)} %slice.28), channel_id=1, source_target_pairs={{0,12},{4,8},{8,4},{12,0},{1,13},{5,9},{9,5},{13,1},{2,14},{6,10},... | collective-permute-start | bytes 196616 | tf_op jit(solution)/shard_map/ppermute | solution.py:289
  53.4 6.1 %slice-start.1 = ((s8[8388608]{0:T(1024)(128)(4,1)}), s8[4194304]{0:T(1024)(128)(4,1)S(1)}, s32[]{:S(2)}) async-start(s8[8388608]{0:T(1024)(128)(4,1)} %bitcast.15), calls=%async_computation.1 | async-start | bytes 8388608
  53.9 1.3 %collective-permute-start.17 = (f32[1,16,1024]{2,1,0:T(8,128)S(1)}, f32[1,16,1024]{2,1,0:T(8,128)S(1)}, u32[]{:S(2)}, u32[]{:S(2)}) collective-permute-start(f32[1,16,1024]{2,1,0:T(8,128)S(1)} %shard_map.87), channel_id=1, source_target_pairs={{0,1},{1,0},{2,3},{3,2},{4,5},{5,4},{6,7},{7,6},{8,9},{9,8},{10,11... | collective-permute-start | bytes 196616 | tf_op jit(solution)/shard_map/ppermute | solution.py:289
  55.1 4.1 %collective-permute-start.18 = (f32[1,16,1024]{2,1,0:T(8,128)S(1)}, f32[1,16,1024]{2,1,0:T(8,128)S(1)}, u32[]{:S(2)}, u32[]{:S(2)}) collective-permute-start(f32[1,16,1024]{2,1,0:T(8,128)S(1)} %add.56), channel_id=1, source_target_pairs={{0,3},{1,2},{2,1},{3,0},{4,7},{5,6},{6,5},{7,4},{8,11},{9,10},{10,... | collective-permute-start | bytes 196616 | tf_op jit(solution)/shard_map/ppermute | solution.py:289
  59.3 1.3 %collective-permute-start.19 = (f32[1,16,1024]{2,1,0:T(8,128)S(1)}, f32[1,16,1024]{2,1,0:T(8,128)S(1)}, u32[]{:S(2)}, u32[]{:S(2)}) collective-permute-start(f32[1,16,1024]{2,1,0:T(8,128)S(1)} %add.57.pull), channel_id=1, source_target_pairs={{0,1},{1,0},{2,3},{3,2},{4,5},{5,4},{6,7},{7,6},{8,9},{9,8},{10,11... | collective-permute-start | bytes 196616 | tf_op jit(solution)/shard_map/ppermute | solution.py:289
  61.3 6.0 %collective-permute-start.22 = (f32[16,640]{1,0:T(8,128)S(1)}, f32[16,640]{1,0:T(8,128)S(1)}, u32[]{:S(2)}, u32[]{:S(2)}) collective-permute-start(f32[16,640]{1,0:T(8,128)S(1)} %pad_maximum_fusion.5), channel_id=1, source_target_pairs={{0,12},{4,8},{8,4},{12,0},{1,13},{5,9},{9,5},{13,1},{2,14},{6,10},... | collective-permute-start | bytes 122888 | tf_op jit(solution)/shard_map/ppermute | solution.py:289
  63.4 5.3 %collective-permute-start.21 = (f32[16,640]{1,0:T(8,128)S(1)}, f32[16,640]{1,0:T(8,128)S(1)}, u32[]{:S(2)}, u32[]{:S(2)}) collective-permute-start(f32[16,640]{1,0:T(8,128)S(1)} %pad_maximum_fusion.4), channel_id=1, source_target_pairs={{0,8},{4,12},{8,0},{12,4},{1,9},{5,13},{9,1},{13,5},{2,10},{6,14},... | collective-permute-start | bytes 122888 | tf_op jit(solution)/shard_map/ppermute | solution.py:289
  64.2 4.7 %collective-permute-start.20 = (f32[16,640]{1,0:T(8,128)S(1)}, f32[16,640]{1,0:T(8,128)S(1)}, u32[]{:S(2)}, u32[]{:S(2)}) collective-permute-start(f32[16,640]{1,0:T(8,128)S(1)} %pad_maximum_fusion.3), channel_id=1, source_target_pairs={{0,4},{4,0},{8,12},{12,8},{1,5},{5,1},{9,13},{13,9},{2,6},{6,2},{1... | collective-permute-start | bytes 122888 | tf_op jit(solution)/shard_map/ppermute | solution.py:289
